TPU v7x, 32 devices: a whole 2x2x4 slice. The times are simulated.
32 devices in a mesh: gx: 4 (over z), gy: 2 (over y), gz: 4 (over x, core).
Axes of the slice: x: 2, y: 2, z: 4, core: 2. Of those that a mesh axis runs over, the one named last changes fastest.
Arguments:
- stress_trial: float32 [6, 786432], P(None, ('gx', 'gy', 'gz')), may hold values from -6 to 6
- mean_stress: float32 [786432], P(('gx', 'gy', 'gz')), may hold values from 0.3 to 2
- consolidation: float32 [786432], P(('gx', 'gy', 'gz')), may hold values from 2.5 to 4
- point_velocity: float32 [3, 786432], P(None, ('gx', 'gy', 'gz')), may hold values from -6 to 6
- point_weight: float32 [786432], P(('gx', 'gy', 'gz')), may hold values from 0.5 to 1
- point_cell: int32 [786432], P(('gx', 'gy', 'gz')), may hold values from 0 to 16383
- yield_flag: int32 [786432], P(('gx', 'gy', 'gz')), may hold values 0 or 1
- point_count: int32 [4, 2, 4], P('gx', 'gy', 'gz'), may hold values from 12288 to 24576, as said below
- porosity: float32 [64, 32, 256], P('gz', 'gx', 'gy'), may hold values from 0.2 to 0.5
- permeability: float32 [64, 32, 256], P('gz', 'gx', 'gy'), may hold values from 1 to 10
Outputs:
- velocity: float32 [3, 64, 32, 256], P(None, 'gz', 'gx', 'gy')
- pressure: float32 [64, 32, 256], P('gz', 'gx', 'gy')
Inputs may be any that keep to these rules, and one draw needn't show every extreme that they name: `point_cell`: a cell index within the brick, levels slowest, then rows, then columns. `point_count`: slots below the count hold live points, the rest are empty; some brick is full.
All inputs are finite; a program needn't handle non-finite values. No bound on the sum of `yield_flag` on one device may be relied on, other than what follows from the above.
Results may differ from a plain program's by a relative error of at most 0.0003.
Values sent between devices are 32-bit elements; how exact they have to be, the bound alone decides.
No kernel may reach another device: no remote copies, remote signals or barrier semaphores. Data moves between devices by JAX's collectives and lax.ppermute only.
A program may use at most 128 MiB of HBM per device.

v0:
```python
import jax
import jax.numpy as jnp
from jax import lax
from jax.sharding import PartitionSpec as P

time_step = 0.25
storage_rate = 0.002
source_rate = 0.003
critical_slope = 1.2
mass_floor = 0.5
shear_floor = 1.0


def padded_2(cells, sides, width):
    for axis, dim in sides:
        count = lax.axis_size(axis)
        ends = count - 1
        head = lax.slice_in_dim(cells, 0, width, axis=dim)
        tail = lax.slice_in_dim(cells, cells.shape[dim] - width, cells.shape[dim], axis=dim)
        cells = jnp.concatenate(
            [
                lax.ppermute(tail, axis, [(i, (i + 1) % count) for i in range(ends)]),
                cells,
                lax.ppermute(head, axis, [((i + 1) % count, i) for i in range(ends)]),
            ],
            axis=dim,
        )
    return cells


def along_x(padded):
    return (padded[..., 1:-1, 2:, 1:-1] - padded[..., 1:-1, :-2, 1:-1]) * 0.5


def along_y(padded):
    return (padded[..., 1:-1, 1:-1, 2:] - padded[..., 1:-1, 1:-1, :-2]) * 0.5


def along_z(padded):
    return (padded[..., 2:, 1:-1, 1:-1] - padded[..., :-2, 1:-1, 1:-1]) * 0.5


def harmonic(former, latter):
    return 2.0 * former * latter / (former + latter)


def returned_stress(stress_trial, mean_stress, consolidation, yield_flag):
    sq_normal = (
        stress_trial[0] * stress_trial[0]
        + stress_trial[1] * stress_trial[1]
        + stress_trial[2] * stress_trial[2]
    )
    sq_shear = (
        stress_trial[3] * stress_trial[3]
        + stress_trial[4] * stress_trial[4]
        + stress_trial[5] * stress_trial[5]
    )
    shear_size = jnp.sqrt(1.5 * (sq_normal + 2.0 * sq_shear))
    yield_size = critical_slope * jnp.sqrt(mean_stress * (consolidation - mean_stress))
    factor = jnp.where(yield_flag == 1, yield_size / jnp.maximum(shear_size, shear_floor), 1.0)
    isotropic = jnp.array([1.0, 1.0, 1.0, 0.0, 0.0, 0.0], dtype=jnp.float32)[:, None]
    return stress_trial * factor - isotropic * mean_stress


def point_sums(stress, point_velocity, weight, cell_index, segments):
    stacked = jnp.concatenate([stress * weight, point_velocity * weight, weight[None]], axis=0)
    return jax.vmap(
        lambda component: jax.ops.segment_sum(component, cell_index, num_segments=segments)
    )(stacked)


def brick_velocity(cell_sums, padded):
    floored = jnp.maximum(cell_sums[9], mass_floor)
    force_x = along_x(padded[0]) + along_y(padded[3]) + along_z(padded[5])
    force_y = along_x(padded[3]) + along_y(padded[1]) + along_z(padded[4])
    force_z = along_x(padded[5]) + along_y(padded[4]) + along_z(padded[2])
    return jnp.stack(
        [
            (cell_sums[6] + time_step * force_x) / floored,
            (cell_sums[7] + time_step * force_y) / floored,
            (cell_sums[8] + time_step * force_z) / floored,
        ]
    )


def divergence(padded_velocity):
    return along_x(padded_velocity[0]) + along_y(padded_velocity[1]) + along_z(padded_velocity[2])


def band_terms(porosity, permeability, level_below, level_above, at_top, dilation):
    up_face = harmonic(permeability, level_above)
    down_face = harmonic(level_below, permeability)
    top_face = jnp.where(at_top, permeability, up_face)
    lower_band = -time_step * down_face
    upper_band = -time_step * up_face
    main_band = storage_rate * porosity + time_step * (down_face + top_face)
    right_side = -source_rate * (1.0 - porosity) * dilation
    return (lower_band, main_band, upper_band, right_side)


def earlier(values, stride, filler):
    head = jnp.full((stride,) + values.shape[1:], filler, values.dtype)
    return jnp.concatenate([head, values[:-stride]], axis=0)


def later(values, stride, filler):
    tail = jnp.full((stride,) + values.shape[1:], filler, values.dtype)
    return jnp.concatenate([values[stride:], tail], axis=0)


def cyclic_solve(lower_band, main_band, upper_band, right_side):
    length = main_band.shape[0]
    for bit in range((length - 1).bit_length()):
        stride = 1 << bit
        back_weight = -lower_band / earlier(main_band, stride, 1.0)
        ahead_weight = -upper_band / later(main_band, stride, 1.0)
        new_lower = back_weight * earlier(lower_band, stride, 0.0)
        new_upper = ahead_weight * later(upper_band, stride, 0.0)
        new_main = (
            main_band
            + back_weight * earlier(upper_band, stride, 0.0)
            + ahead_weight * later(lower_band, stride, 0.0)
        )
        new_right = (
            right_side
            + back_weight * earlier(right_side, stride, 0.0)
            + ahead_weight * later(right_side, stride, 0.0)
        )
        lower_band, main_band, upper_band, right_side = (new_lower, new_main, new_upper, new_right)
    return right_side / main_band


def brick_bands(porosity, permeability, padded, dilation, levels, layer_count):
    level_index = lax.axis_index("gz") * levels + jnp.arange(levels, dtype=jnp.int32)
    at_top = (level_index == levels * layer_count - 1)[:, None, None]
    return band_terms(
        porosity,
        permeability,
        padded[6, :-2, 1:-1, 1:-1],
        padded[6, 2:, 1:-1, 1:-1],
        at_top,
        dilation,
    )


def partitioned_solve(band_set, levels, extent, breadth):
    lower, main, upper, right = [band.reshape(levels, -1) for band in band_set]
    columns = main.shape[1]
    zero_row = jnp.zeros((1, columns), jnp.float32)
    inner_lower = jnp.concatenate([zero_row, lower[2:-1]], axis=0)
    inner_upper = jnp.concatenate([upper[1:-2], zero_row], axis=0)
    inner_zeros = jnp.zeros((levels - 3, columns), jnp.float32)
    side_first = jnp.concatenate([-lower[1:2], inner_zeros], axis=0)
    side_last = jnp.concatenate([inner_zeros, -upper[levels - 2 : levels - 1]], axis=0)

    def tripled(values):
        return jnp.concatenate([values, values, values], axis=1)

    inner = cyclic_solve(
        tripled(inner_lower),
        tripled(main[1:-1]),
        tripled(inner_upper),
        jnp.concatenate([right[1:-1], side_first, side_last], axis=1),
    )
    base = inner[:, :columns]
    from_first = inner[:, columns : 2 * columns]
    from_last = inner[:, 2 * columns :]
    first_row = jnp.stack(
        [
            lower[0],
            main[0] + upper[0] * from_first[0],
            upper[0] * from_last[0],
            right[0] - upper[0] * base[0],
        ]
    )
    last_row = jnp.stack(
        [
            lower[-1] * from_first[-1],
            main[-1] + lower[-1] * from_last[-1],
            upper[-1],
            right[-1] - lower[-1] * base[-1],
        ]
    )
    reduced = jnp.stack([first_row, last_row])
    gathered = lax.all_gather(reduced, "gz", axis=0, tiled=True)
    coupled = cyclic_solve(gathered[:, 0], gathered[:, 1], gathered[:, 2], gathered[:, 3])
    own_pair = lax.dynamic_slice_in_dim(coupled, 2 * lax.axis_index("gz"), 2, 0)
    interior = base + from_first * own_pair[0][None] + from_last * own_pair[1][None]
    whole = jnp.concatenate([own_pair[0:1], interior, own_pair[1:2]], axis=0)
    return whole.reshape(levels, extent, breadth)


def shards(
    stress_trial,
    mean_stress,
    consolidation,
    point_velocity,
    point_weight,
    point_cell,
    yield_flag,
    point_count,
    porosity,
    permeability,
):
    levels, extent, breadth = porosity.shape
    slot_index = jnp.arange(mean_stress.shape[0], dtype=jnp.int32)
    weight = jnp.where(slot_index < point_count[0, 0, 0], point_weight, 0.0)
    stress = returned_stress(stress_trial, mean_stress, consolidation, yield_flag)
    cell_sums = point_sums(
        stress, point_velocity, weight, point_cell, levels * extent * breadth
    ).reshape(10, levels, extent, breadth)
    outgoing = jnp.concatenate([cell_sums[:6], permeability[None]], axis=0)
    padded = padded_2(outgoing, (("gx", 2), ("gy", 3), ("gz", 1)), 1)
    velocity = brick_velocity(cell_sums, padded)
    padded_velocity = padded_2(velocity, (("gx", 2), ("gy", 3), ("gz", 1)), 1)
    dilation = divergence(padded_velocity)
    layer_count = lax.axis_size("gz")
    band_set = brick_bands(porosity, permeability, padded, dilation, levels, layer_count)
    pressure = partitioned_solve(band_set, levels, extent, breadth)
    padded_pressure = padded_2(pressure, (("gx", 1), ("gy", 2), ("gz", 0)), 1)
    gradient = jnp.stack(
        [along_x(padded_pressure), along_y(padded_pressure), along_z(padded_pressure)]
    )
    return (velocity - time_step * gradient, pressure)


def solution(mesh):
    placed = (
        P(None, ("gx", "gy", "gz")),
        P(("gx", "gy", "gz")),
        P(("gx", "gy", "gz")),
        P(None, ("gx", "gy", "gz")),
        P(("gx", "gy", "gz")),
        P(("gx", "gy", "gz")),
        P(("gx", "gy", "gz")),
        P("gx", "gy", "gz"),
        P("gz", "gx", "gy"),
        P("gz", "gx", "gy"),
    )
    return jax.shard_map(
        shards,
        mesh=mesh,
        in_specs=placed,
        out_specs=(P(None, "gz", "gx", "gy"), P("gz", "gx", "gy")),
        check_vma=False,
    )
```

profile of v0, /device:TPU:0, one launch (start us, length us, event | category | flops | bytes accessed | tf_op | source)
XLA Modules:
  0.0 272.8 jit_solution(16613459947025742353)
XLA Ops:
  0.7 3.6 %sqrt_maximum_fusion = f32[1,24576]{1,0:T(1,128)S(1)} fusion(f32[6,24576]{1,0:T(8,128)} %param.11), kind=kLoop, calls=%fused_computation.66 | loop fusion | flops 344064 | bytes 688128 | tf_op jit(solution)/shard_map/max | solution.py:60
  7.7 7.0 %copy.19 = f32[24576,10]{1,0:T(8,128)} copy(f32[24576,10]{0,1:T(8,128)S(1)} %maximum_bitcast_fusion) | data formatting | bytes 1966080 | tf_op jit(solution)/shard_map/concatenate | solution.py:66
  14.7 134.6 %scatter_custom_fusion = f32[10,16384]{0,1:T(8,128)} fusion(s32[24576]{0:T(1024)} %param.16, f32[24576,10]{1,0:T(8,128)} %copy.19, f32[]{:T(128)} %constant.19.clone.1), kind=kCustom, calls=%fused_computation.6 | custom fusion | flops 245760 | bytes 655872 | tf_op jit(solution)/shard_map/vmap()/scatter-add | solution.py:68
  149.3 5.3 %copy.20 = f32[6,16,8,128]{3,2,1,0:T(8,128)S(1)} copy(f32[6,16,8,128]{0,3,2,1:T(8,128)} %bitcast.148) | data formatting | bytes 786432 | tf_op jit(solution)/shard_map/slice | solution.py:212
  154.7 4.9 %collective-permute-start = (f32[7,16,1,128]{3,2,1,0:T(1,128)S(1)}, f32[7,16,1,128]{3,2,1,0:T(1,128)S(1)}, u32[]{:S(2)}, u32[]{:S(2)}) collective-permute-start(f32[7,16,1,128]{3,2,1,0:T(1,128)S(1)} %get-tuple-element.34), channel_id=1, source_target_pairs={{0,8},{8,16},{16,24},{1,9},{9,17},{17,25},{2,10},{10,18},{18,26},{... | collective-permute-start | bytes 172040 | tf_op jit(solution)/shard_map/ppermute | solution.py:22
  161.4 4.3 %collective-permute-done.1 = f32[7,16,1,128]{3,2,1,0:T(1,128)S(1)} collective-permute-done((f32[7,16,1,128]{3,2,1,0:T(1,128)S(1)}, f32[7,16,1,128]{3,2,1,0:T(1,128)S(1)}, u32[]{:S(2)}, u32[]{:S(2)}) %collective-permute-start.1) | collective-permute-done | bytes 57376 | tf_op jit(solution)/shard_map/ppermute | solution.py:24
  166.7 3.4 %collective-permute-start.2 = (f32[7,16,10,1]{1,3,2,0:T(1,128)S(1)}, f32[7,16,10,1]{1,3,2,0:T(1,128)S(1)}, u32[]{:S(2)}, u32[]{:S(2)}) collective-permute-start(f32[7,16,10,1]{1,3,2,0:T(1,128)S(1)} %copy.21), channel_id=1, source_target_pairs={{0,4},{1,5},{2,6},{3,7},{8,12},{9,13},{10,14},{11,15},{16,20},{17,... | collective-permute-start | bytes 13448 | tf_op jit(solution)/shard_map/ppermute | solution.py:22
  172.5 4.0 %collective-permute-done.3 = f32[7,16,10,1]{1,3,2,0:T(1,128)S(1)} collective-permute-done((f32[7,16,10,1]{1,3,2,0:T(1,128)S(1)}, f32[7,16,10,1]{1,3,2,0:T(1,128)S(1)}, u32[]{:S(2)}, u32[]{:S(2)}) %collective-permute-start.3) | collective-permute-done | bytes 4512 | tf_op jit(solution)/shard_map/ppermute | solution.py:24
  178.5 1.5 collective-permute-start.5
  180.0 28.1 %slice_reduce_fusion.2 = (f32[16384]{0:T(1024)S(1)}, f32[16384]{0:T(1024)S(1)}, f32[16384]{0:T(1024)S(1)}, f32[16384]{0:T(1024)S(1)}) fusion(f32[10,16384]{0,1:T(8,128)} %scatter_custom_fusion), kind=kLoop, calls=%fused_computation.5 | loop fusion | flops 16384 | bytes 524288 | tf_op jit(solution)/shard_map/slice | solution.py:79
  210.1 3.5 %collective-permute-start.6 = (f32[3,16,1,128]{3,2,1,0:T(1,128)S(1)}, f32[3,16,1,128]{3,2,1,0:T(1,128)S(1)}, u32[]{:S(2)}, u32[]{:S(2)}) collective-permute-start(f32[3,16,1,128]{3,2,1,0:T(1,128)S(1)} %get-tuple-element.82), channel_id=1, source_target_pairs={{0,8},{8,16},{16,24},{1,9},{9,17},{17,25},{2,10},{10,18},{18,26},{... | collective-permute-start | bytes 73736 | tf_op jit(solution)/shard_map/ppermute | solution.py:22
  215.1 4.2 %collective-permute-done.7 = f32[3,16,1,128]{3,2,1,0:T(1,128)S(1)} collective-permute-done((f32[3,16,1,128]{3,2,1,0:T(1,128)S(1)}, f32[3,16,1,128]{3,2,1,0:T(1,128)S(1)}, u32[]{:S(2)}, u32[]{:S(2)}) %collective-permute-start.7) | collective-permute-done | bytes 24608 | tf_op jit(solution)/shard_map/ppermute | solution.py:24
  219.5 1.6 collective-permute-start.8
  222.6 7.7 %collective-permute-done.8 = f32[3,16,10,1]{3,2,1,0:T(8,128)S(1)} collective-permute-done((f32[3,16,10,1]{3,2,1,0:T(8,128)S(1)}, f32[3,16,10,1]{3,2,1,0:T(8,128)S(1)}, u32[]{:S(2)}, u32[]{:S(2)}) %collective-permute-start.8) | collective-permute-done | bytes 1952 | tf_op jit(solution)/shard_map/ppermute | solution.py:22
  230.3 4.6 %collective-permute-done.9 = f32[3,16,10,1]{3,2,1,0:T(8,128)S(1)} collective-permute-done((f32[3,16,10,1]{3,2,1,0:T(8,128)S(1)}, f32[3,16,10,1]{3,2,1,0:T(8,128)S(1)}, u32[]{:S(2)}, u32[]{:S(2)}) %collective-permute-start.9) | collective-permute-done | bytes 1952 | tf_op jit(solution)/shard_map/ppermute | solution.py:24
  235.0 2.0 collective-permute-start.10
  237.1 1.5 collective-permute-start.11
  238.7 1.7 collective-permute-done.11
  243.3 6.9 %all_gather.3 = f32[8,4,1024]{2,1,0:T(4,128)S(1)} all-gather(f32[2,4,1024]{2,1,0:T(4,128)S(1)} %pad_maximum_fusion.53), channel_id=1, replica_groups=mesh['gx'=4,'gy'=2,'gz'=4] {'gz'}, dimensions={0}, use_global_device_ids=true | all-gather | bytes 163840 | tf_op jit(solution)/shard_map/all_gather | solution.py:185
  252.4 4.5 %collective-permute-start.13 = (f32[16,1,128]{2,1,0:T(1,128)S(1)}, f32[16,1,128]{2,1,0:T(1,128)S(1)}, u32[]{:S(2)}, u32[]{:S(2)}) collective-permute-start(f32[16,1,128]{2,1,0:T(1,128)S(1)} %get-tuple-element.102), channel_id=1, source_target_pairs={{0,8},{8,16},{16,24},{1,9},{9,17},{17,25},{2,10},{10,18},{18,26},{... | collective-permute-start | bytes 24584 | tf_op jit(solution)/shard_map/ppermute | solution.py:22
  256.9 1.3 collective-permute-done.13
  259.7 4.6 %collective-permute-start.15 = (f32[16,10,1]{2,1,0:T(8,128)S(1)}, f32[16,10,1]{2,1,0:T(8,128)S(1)}, u32[]{:S(2)}, u32[]{:S(2)}) collective-permute-start(f32[16,10,1]{2,1,0:T(8,128)S(1)} %get-tuple-element.84), channel_id=1, source_target_pairs={{0,4},{1,5},{2,6},{3,7},{8,12},{9,13},{10,14},{11,15},{16,20},{17,... | collective-permute-start | bytes 1928 | tf_op jit(solution)/shard_map/ppermute | solution.py:22
  265.3 1.5 collective-permute-done.15
  268.1 3.0 %collective-permute-start.17 = (f32[1,10,130]{2,1,0:T(8,128)S(1)}, f32[1,10,130]{2,1,0:T(8,128)S(1)}, u32[]{:S(2)}, u32[]{:S(2)}) collective-permute-start(f32[1,10,130]{2,1,0:T(8,128)S(1)} %get-tuple-element.44), channel_id=1, source_target_pairs={{0,1},{1,2},{2,3},{4,5},{5,6},{6,7},{8,9},{9,10},{10,11},{12,13},{... | collective-permute-start | bytes 15608 | tf_op jit(solution)/shard_map/ppermute | solution.py:22
  (139 shorter events, 25.1 us)
Async XLA Ops:
  0.6 6.5 %copy-start.5 = (f32[6]{0:T(128)S(1)}, f32[6]{0:T(128)}, u32[]{:S(2)}) copy-start(f32[6]{0:T(128)} %constant.37.clone) | copy-start | bytes 76
  0.6 6.5 %copy-start.1 = (f32[6,24576]{1,0:T(8,128)S(1)}, f32[6,24576]{1,0:T(8,128)}, u32[]{:S(2)}) copy-start(f32[6,24576]{1,0:T(8,128)} %param.11) | copy-start | bytes 1769476
  0.7 6.5 %copy-start.3 = (f32[24576]{0:T(1024)S(1)}, f32[24576]{0:T(1024)}, u32[]{:S(2)}) copy-start(f32[24576]{0:T(1024)} %param.12) | copy-start | bytes 294916
  149.3 5.3 %copy-start = (f32[16,8,128]{2,1,0:T(8,128)S(1)}, f32[16,8,128]{2,1,0:T(8,128)}, u32[]{:S(2)}) copy-start(f32[16,8,128]{2,1,0:T(8,128)} %param.20) | copy-start | bytes 196612
  154.7 6.7 %collective-permute-start = (f32[7,16,1,128]{3,2,1,0:T(1,128)S(1)}, f32[7,16,1,128]{3,2,1,0:T(1,128)S(1)}, u32[]{:S(2)}, u32[]{:S(2)}) collective-permute-start(f32[7,16,1,128]{3,2,1,0:T(1,128)S(1)} %get-tuple-element.34), channel_id=1, source_target_pairs={{0,8},{8,16},{16,24},{1,9},{9,17},{17,25},{2,10},{10,18},{18,26},{... | collective-permute-start | bytes 172040 | tf_op jit(solution)/shard_map/ppermute | solution.py:22
  159.6 6.1 %collective-permute-start.1 = (f32[7,16,1,128]{3,2,1,0:T(1,128)S(1)}, f32[7,16,1,128]{3,2,1,0:T(1,128)S(1)}, u32[]{:S(2)}, u32[]{:S(2)}) collective-permute-start(f32[7,16,1,128]{3,2,1,0:T(1,128)S(1)} %get-tuple-element.35), channel_id=1, source_target_pairs={{8,0},{16,8},{24,16},{9,1},{17,9},{25,17},{10,2},{18,10},{26,18},{... | collective-permute-start | bytes 172040 | tf_op jit(solution)/shard_map/ppermute | solution.py:24
  166.7 5.2 %collective-permute-start.2 = (f32[7,16,10,1]{1,3,2,0:T(1,128)S(1)}, f32[7,16,10,1]{1,3,2,0:T(1,128)S(1)}, u32[]{:S(2)}, u32[]{:S(2)}) collective-permute-start(f32[7,16,10,1]{1,3,2,0:T(1,128)S(1)} %copy.21), channel_id=1, source_target_pairs={{0,4},{1,5},{2,6},{3,7},{8,12},{9,13},{10,14},{11,15},{16,20},{17,... | collective-permute-start | bytes 13448 | tf_op jit(solution)/shard_map/ppermute | solution.py:22
  170.6 5.8 %collective-permute-start.3 = (f32[7,16,10,1]{1,3,2,0:T(1,128)S(1)}, f32[7,16,10,1]{1,3,2,0:T(1,128)S(1)}, u32[]{:S(2)}, u32[]{:S(2)}) collective-permute-start(f32[7,16,10,1]{1,3,2,0:T(1,128)S(1)} %copy.22), channel_id=1, source_target_pairs={{4,0},{5,1},{6,2},{7,3},{12,8},{13,9},{14,10},{15,11},{20,16},{21,... | collective-permute-start | bytes 13448 | tf_op jit(solution)/shard_map/ppermute | solution.py:24
  177.2 30.9 %collective-permute-start.4 = (f32[7,1,10,130]{3,2,1,0:T(8,128)S(1)}, f32[7,1,10,130]{3,2,1,0:T(8,128)S(1)}, u32[]{:S(2)}, u32[]{:S(2)}) collective-permute-start(f32[7,1,10,130]{3,2,1,0:T(8,128)S(1)} %get-tuple-element.19), channel_id=1, source_target_pairs={{0,1},{1,2},{2,3},{4,5},{5,6},{6,7},{8,9},{9,10},{10,11},{12,13},{... | collective-permute-start | bytes 109208 | tf_op jit(solution)/shard_map/ppermute | solution.py:22
  178.5 29.6 %collective-permute-start.5 = (f32[7,1,10,130]{3,2,1,0:T(8,128)S(1)}, f32[7,1,10,130]{3,2,1,0:T(8,128)S(1)}, u32[]{:S(2)}, u32[]{:S(2)}) collective-permute-start(f32[7,1,10,130]{3,2,1,0:T(8,128)S(1)} %get-tuple-element.20), channel_id=1, source_target_pairs={{1,0},{2,1},{3,2},{5,4},{6,5},{7,6},{9,8},{10,9},{11,10},{13,12},{... | collective-permute-start | bytes 109208 | tf_op jit(solution)/shard_map/ppermute | solution.py:24
  210.1 5.0 %collective-permute-start.6 = (f32[3,16,1,128]{3,2,1,0:T(1,128)S(1)}, f32[3,16,1,128]{3,2,1,0:T(1,128)S(1)}, u32[]{:S(2)}, u32[]{:S(2)}) collective-permute-start(f32[3,16,1,128]{3,2,1,0:T(1,128)S(1)} %get-tuple-element.82), channel_id=1, source_target_pairs={{0,8},{8,16},{16,24},{1,9},{9,17},{17,25},{2,10},{10,18},{18,26},{... | collective-permute-start | bytes 73736 | tf_op jit(solution)/shard_map/ppermute | solution.py:22
  213.6 5.7 %collective-permute-start.7 = (f32[3,16,1,128]{3,2,1,0:T(1,128)S(1)}, f32[3,16,1,128]{3,2,1,0:T(1,128)S(1)}, u32[]{:S(2)}, u32[]{:S(2)}) collective-permute-start(f32[3,16,1,128]{3,2,1,0:T(1,128)S(1)} %get-tuple-element.83), channel_id=1, source_target_pairs={{8,0},{16,8},{24,16},{9,1},{17,9},{25,17},{10,2},{18,10},{26,18},{... | collective-permute-start | bytes 73736 | tf_op jit(solution)/shard_map/ppermute | solution.py:24
  219.5 10.7 %collective-permute-start.8 = (f32[3,16,10,1]{3,2,1,0:T(8,128)S(1)}, f32[3,16,10,1]{3,2,1,0:T(8,128)S(1)}, u32[]{:S(2)}, u32[]{:S(2)}) collective-permute-start(f32[3,16,10,1]{3,2,1,0:T(8,128)S(1)} %get-tuple-element.39), channel_id=1, source_target_pairs={{0,4},{1,5},{2,6},{3,7},{8,12},{9,13},{10,14},{11,15},{16,20},{17,... | collective-permute-start | bytes 5768 | tf_op jit(solution)/shard_map/ppermute | solution.py:22
  221.2 13.7 %collective-permute-start.9 = (f32[3,16,10,1]{3,2,1,0:T(8,128)S(1)}, f32[3,16,10,1]{3,2,1,0:T(8,128)S(1)}, u32[]{:S(2)}, u32[]{:S(2)}) collective-permute-start(f32[3,16,10,1]{3,2,1,0:T(8,128)S(1)} %get-tuple-element.40), channel_id=1, source_target_pairs={{4,0},{5,1},{6,2},{7,3},{12,8},{13,9},{14,10},{15,11},{20,16},{21,... | collective-permute-start | bytes 5768 | tf_op jit(solution)/shard_map/ppermute | solution.py:24
  235.0 3.6 %collective-permute-start.10 = (f32[3,1,10,130]{3,2,1,0:T(8,128)S(1)}, f32[3,1,10,130]{3,2,1,0:T(8,128)S(1)}, u32[]{:S(2)}, u32[]{:S(2)}) collective-permute-start(f32[3,1,10,130]{3,2,1,0:T(8,128)S(1)} %get-tuple-element.27), channel_id=1, source_target_pairs={{0,1},{1,2},{2,3},{4,5},{5,6},{6,7},{8,9},{9,10},{10,11},{12,13},{... | collective-permute-start | bytes 46808 | tf_op jit(solution)/shard_map/ppermute | solution.py:22
  237.1 3.4 %collective-permute-start.11 = (f32[3,1,10,130]{3,2,1,0:T(8,128)S(1)}, f32[3,1,10,130]{3,2,1,0:T(8,128)S(1)}, u32[]{:S(2)}, u32[]{:S(2)}) collective-permute-start(f32[3,1,10,130]{3,2,1,0:T(8,128)S(1)} %get-tuple-element.28), channel_id=1, source_target_pairs={{1,0},{2,1},{3,2},{5,4},{6,5},{7,6},{9,8},{10,9},{11,10},{13,12},{... | collective-permute-start | bytes 46808 | tf_op jit(solution)/shard_map/ppermute | solution.py:24
  238.6 2.5 copy-start.4
  251.0 21.8 %copy-start.2 = (f32[2,8,8,128]{3,2,1,0:T(8,128)}, f32[2,8,8,128]{3,2,1,0:T(8,128)S(1)}, u32[]{:S(2)}) copy-start(f32[2,8,8,128]{3,2,1,0:T(8,128)S(1)} %copy.53) | copy-start | bytes 196612
  251.1 5.9 %collective-permute-start.12 = (f32[16,1,128]{2,1,0:T(1,128)S(1)}, f32[16,1,128]{2,1,0:T(1,128)S(1)}, u32[]{:S(2)}, u32[]{:S(2)}) collective-permute-start(f32[16,1,128]{2,1,0:T(1,128)S(1)} %get-tuple-element.103), channel_id=1, source_target_pairs={{8,0},{16,8},{24,16},{9,1},{17,9},{25,17},{10,2},{18,10},{26,18},{... | collective-permute-start | bytes 24584 | tf_op jit(solution)/shard_map/ppermute | solution.py:24
  252.4 5.9 %collective-permute-start.13 = (f32[16,1,128]{2,1,0:T(1,128)S(1)}, f32[16,1,128]{2,1,0:T(1,128)S(1)}, u32[]{:S(2)}, u32[]{:S(2)}) collective-permute-start(f32[16,1,128]{2,1,0:T(1,128)S(1)} %get-tuple-element.102), channel_id=1, source_target_pairs={{0,8},{8,16},{16,24},{1,9},{9,17},{17,25},{2,10},{10,18},{18,26},{... | collective-permute-start | bytes 24584 | tf_op jit(solution)/shard_map/ppermute | solution.py:22
  258.4 6.9 %collective-permute-start.14 = (f32[16,10,1]{2,1,0:T(8,128)S(1)}, f32[16,10,1]{2,1,0:T(8,128)S(1)}, u32[]{:S(2)}, u32[]{:S(2)}) collective-permute-start(f32[16,10,1]{2,1,0:T(8,128)S(1)} %get-tuple-element.85), channel_id=1, source_target_pairs={{4,0},{5,1},{6,2},{7,3},{12,8},{13,9},{14,10},{15,11},{20,16},{21,... | collective-permute-start | bytes 1928 | tf_op jit(solution)/shard_map/ppermute | solution.py:24
  259.7 7.1 %collective-permute-start.15 = (f32[16,10,1]{2,1,0:T(8,128)S(1)}, f32[16,10,1]{2,1,0:T(8,128)S(1)}, u32[]{:S(2)}, u32[]{:S(2)}) collective-permute-start(f32[16,10,1]{2,1,0:T(8,128)S(1)} %get-tuple-element.84), channel_id=1, source_target_pairs={{0,4},{1,5},{2,6},{3,7},{8,12},{9,13},{10,14},{11,15},{16,20},{17,... | collective-permute-start | bytes 1928 | tf_op jit(solution)/shard_map/ppermute | solution.py:22
  266.8 4.5 %collective-permute-start.16 = (f32[1,10,130]{2,1,0:T(8,128)S(1)}, f32[1,10,130]{2,1,0:T(8,128)S(1)}, u32[]{:S(2)}, u32[]{:S(2)}) collective-permute-start(f32[1,10,130]{2,1,0:T(8,128)S(1)} %get-tuple-element.43), channel_id=1, source_target_pairs={{1,0},{2,1},{3,2},{5,4},{6,5},{7,6},{9,8},{10,9},{11,10},{13,12},{... | collective-permute-start | bytes 15608 | tf_op jit(solution)/shard_map/ppermute | solution.py:24
  268.1 3.9 %collective-permute-start.17 = (f32[1,10,130]{2,1,0:T(8,128)S(1)}, f32[1,10,130]{2,1,0:T(8,128)S(1)}, u32[]{:S(2)}, u32[]{:S(2)}) collective-permute-start(f32[1,10,130]{2,1,0:T(8,128)S(1)} %get-tuple-element.44), channel_id=1, source_target_pairs={{0,1},{1,2},{2,3},{4,5},{5,6},{6,7},{8,9},{9,10},{10,11},{12,13},{... | collective-permute-start | bytes 15608 | tf_op jit(solution)/shard_map/ppermute | solution.py:22
where the time goes:
time: 275 us; the launch traced here: 273 us
  other arithmetic  175 us (64%)
  starting transfers between devices  40.9 us (15%)
  waiting for transfers between devices  31.7 us (12%)
  local copies, waits for them, and re-layouts  16.1 us (6%)
  blocking collectives  6.89 us (3%)
    scatter-add x1, other arithmetic, point_sums(): jax.ops.segment_sum(component, cell_index, num_segments=segments)  135 us
    ppermute x9, starting transfers between devices, padded_2(): lax.ppermute(tail, axis, [(i, (i + 1) % count) for i in range(ends)])  28.9 us
    slice x1, other arithmetic, brick_velocity(): cell_sums[6] + time_step * force_x  28.1 us
    ppermute x9, waiting for transfers between devices, padded_2(): lax.ppermute(head, axis, [((i + 1) % count, i) for i in range(ends)])  19.8 us
    ppermute x9, starting transfers between devices, padded_2(): lax.ppermute(head, axis, [((i + 1) % count, i) for i in range(ends)])  12 us
    ppermute x9, waiting for transfers between devices, padded_2(): lax.ppermute(tail, axis, [(i, (i + 1) % count) for i in range(ends)])  11.9 us
    concatenate x1, local copies, waits for them, and re-layouts, point_sums(): jnp.concatenate([stress * weight, point_velocity * weight, weight[None]],...  6.96 us
    all_gather x1, blocking collectives, partitioned_solve(): gathered = lax.all_gather(reduced, 'gz', axis=0, tiled=True)  6.89 us
  transfers between devices with their start and end apart: 18, of which 12 were waited for; matrix products, arithmetic and copies ran while one was open for 11% of the time, Pallas kernels for 0%

commit v1 on v0

--- a/solution.py
+++ b/solution.py
@@ -1,7 +1,14 @@
+import functools
+
 import jax
 import jax.numpy as jnp
 from jax import lax
+from jax.experimental import pallas as pl
+from jax.experimental.pallas import tpu as pltpu
 from jax.sharding import PartitionSpec as P
+
+bf = jnp.bfloat16
+f32 = jnp.float32
 
 time_step = 0.25
 storage_rate = 0.002
@@ -44,29 +51,76 @@
     return 2.0 * former * latter / (former + latter)
 
 
-def returned_stress(stress_trial, mean_stress, consolidation, yield_flag):
-    sq_normal = (
-        stress_trial[0] * stress_trial[0]
-        + stress_trial[1] * stress_trial[1]
-        + stress_trial[2] * stress_trial[2]
-    )
-    sq_shear = (
-        stress_trial[3] * stress_trial[3]
-        + stress_trial[4] * stress_trial[4]
-        + stress_trial[5] * stress_trial[5]
-    )
-    shear_size = jnp.sqrt(1.5 * (sq_normal + 2.0 * sq_shear))
-    yield_size = critical_slope * jnp.sqrt(mean_stress * (consolidation - mean_stress))
-    factor = jnp.where(yield_flag == 1, yield_size / jnp.maximum(shear_size, shear_floor), 1.0)
-    isotropic = jnp.array([1.0, 1.0, 1.0, 0.0, 0.0, 0.0], dtype=jnp.float32)[:, None]
-    return stress_trial * factor - isotropic * mean_stress
-
-
-def point_sums(stress, point_velocity, weight, cell_index, segments):
-    stacked = jnp.concatenate([stress * weight, point_velocity * weight, weight[None]], axis=0)
-    return jax.vmap(
-        lambda component: jax.ops.segment_sum(component, cell_index, num_segments=segments)
-    )(stacked)
+def row_stress(st, mean, cons, flag):
+    r = lax.broadcasted_iota(jnp.int32, st.shape, 0)
+    w = jnp.where(r < 3, 1.5, 3.0)
+    size = jnp.sqrt(jnp.sum(st*st*w, axis=0, keepdims=True))
+    ysz = 1.2*jnp.sqrt(mean*(cons-mean))
+    factor = jnp.where(flag == 1, ysz/jnp.maximum(size,1.0), 1.0)
+    return st*factor - jnp.where(r<3, mean, 0.0)
+
+def scatter_kernel(kc, count, st, mean, cons, vel, wt, cell, flag, out, acc):
+    step = pl.program_id(0)
+    slot = step*kc + lax.broadcasted_iota(jnp.int32,(1,kc),1)
+    w = jnp.where(slot < count[0], wt[...], 0.0)
+    stress = row_stress(st[...], mean[...], cons[...], flag[...]) * w
+    mom = vel[...]*w
+    c = cell[...]
+    hi = (c >> 7) & 63
+    lo = ((c >> 13) << 7) | (c & 127)
+
+    f8 = jnp.float8_e4m3fn
+    def tile(row, n, t):
+        return jnp.broadcast_to(row, (n,kc)).astype(t)
+    hi16 = tile(hi.astype(f32),16,bf); lo16 = tile(lo.astype(f32),16,bf)
+    one, zero = jnp.array(1,bf), jnp.array(0,bf)
+    base = lax.broadcasted_iota(jnp.int32,(16,kc),0)
+    def eqs(idx16, n):
+        return [(base + b*16).astype(f32).astype(bf) == idx16 for b in range(n//16)]
+    hm = eqs(hi16, 64)
+    lt = jnp.concatenate([jnp.where(m,one,zero) for m in eqs(lo16, 256)], axis=0)
+    lt8 = lt.astype(f8)
+    rows=[stress[i:i+1] for i in range(6)]+[mom[i:i+1] for i in range(3)]+[w]
+    b32 = lax.broadcasted_iota(jnp.int32,(32,kc),0)
+    hmask = [b32 + 32*b == jnp.broadcast_to(hi,(32,kc)) for b in range(2)]
+    pieces=[]; p8=[]
+    for r in rows:
+        top = r.astype(bf).astype(f32)
+        t = tile(top,16,bf)
+        pieces += [jnp.where(m,t,zero) for m in hm]
+        t = tile((r-top)*256.0,32,f8)
+        z = jnp.zeros((32,kc), f8)
+        p8 += [jnp.where(m, t, z) for m in hmask]
+    a = jnp.concatenate(pieces, axis=0)
+    a8 = jnp.concatenate(p8, axis=0)
+    prod = lax.dot_general(a, lt, (((1,),(1,)),((),())), preferred_element_type=f32)
+    prod8 = lax.dot_general(a8, lt8, (((1,),(1,)),((),())), preferred_element_type=f32)
+    prod = prod + prod8*(1/256.)
+    @pl.when(step == 0)
+    def _(): acc[...] = prod
+    @pl.when(step > 0)
+    def _(): acc[...] += prod
+    @pl.when(step == pl.num_programs(0)-1)
+    def _():
+        for i in range(10):
+            s = acc[i*64:i*64+64,:]
+            out[i,0:64,:] = s[:,:128]
+            out[i,64:128,:] = s[:,128:]
+
+def scatter(st, mean, cons, vel, wt, cell, flag, count):
+    kc = 8192 if mean.shape[0] % 8192 == 0 else mean.shape[0]
+    n = mean.shape[0]
+    row = lambda v: v.reshape(1,n)
+    spec = lambda r: pl.BlockSpec((r,kc), lambda i: (0,i))
+    return pl.pallas_call(functools.partial(scatter_kernel, kc),
+        grid=(n//kc,),
+        in_specs=[pl.BlockSpec(memory_space=pltpu.SMEM), spec(6), spec(1), spec(1), spec(3), spec(1), spec(1), spec(1)],
+        out_specs=pl.BlockSpec((10,128,128), lambda i: (0,0,0)),
+        out_shape=jax.ShapeDtypeStruct((10,128,128), f32),
+        scratch_shapes=[pltpu.VMEM((640,256), f32)],
+        compiler_params=pltpu.CompilerParams(vmem_limit_bytes=60<<20),
+        cost_estimate=pl.CostEstimate(flops=2*1280*256*n, bytes_accessed=64*n, transcendentals=0),
+    )(count.reshape(1), st, row(mean), row(cons), vel, row(wt), row(cell), row(flag))
 
 
 def brick_velocity(cell_sums, padded):
@@ -203,11 +257,15 @@
     permeability,
 ):
     levels, extent, breadth = porosity.shape
-    slot_index = jnp.arange(mean_stress.shape[0], dtype=jnp.int32)
-    weight = jnp.where(slot_index < point_count[0, 0, 0], point_weight, 0.0)
-    stress = returned_stress(stress_trial, mean_stress, consolidation, yield_flag)
-    cell_sums = point_sums(
-        stress, point_velocity, weight, point_cell, levels * extent * breadth
+    cell_sums = scatter(
+        stress_trial,
+        mean_stress,
+        consolidation,
+        point_velocity,
+        point_weight,
+        point_cell,
+        yield_flag,
+        point_count,
     ).reshape(10, levels, extent, breadth)
     outgoing = jnp.concatenate([cell_sums[:6], permeability[None]], axis=0)
     padded = padded_2(outgoing, (("gx", 2), ("gy", 3), ("gz", 1)), 1)

time: 275 us -> 113 us (0.41)
  the two profiles are of different devices: /device:TPU:0 before, /device:TPU:22 now
where the time goes in v1:
time: 113 us
  starting transfers between devices  51.3 us (45%)
  waiting for transfers between devices  27.1 us (24%)
  Pallas kernels  15 us (13%)
  local copies, waits for them, and re-layouts  5.78 us (5%)
  other arithmetic  5.74 us (5%)
  blocking collectives  5.53 us (5%)
  between operations  2.2 us (2%)
    ppermute x9, starting transfers between devices, padded_2(): lax.ppermute(head, axis, [((i + 1) % count, i) for i in range(ends)])  33.9 us
    ppermute x9, starting transfers between devices, padded_2(): lax.ppermute(tail, axis, [(i, (i + 1) % count) for i in range(ends)])  17.4 us
    pallas_call x1, Pallas kernels, scatter(): pl.pallas_call(functools.partial(scatter_kernel, kc), grid=(n // kc,), in...  15 us
    ppermute x9, waiting for transfers between devices, padded_2(): lax.ppermute(tail, axis, [(i, (i + 1) % count) for i in range(ends)])  14.9 us
    ppermute x9, waiting for transfers between devices, padded_2(): lax.ppermute(head, axis, [((i + 1) % count, i) for i in range(ends)])  12.3 us
    all_gather x1, blocking collectives, partitioned_solve(): gathered = lax.all_gather(reduced, 'gz', axis=0, tiled=True)  5.53 us
  transfers between devices with their start and end apart: 18, of which 13 were waited for; matrix products, arithmetic and copies ran while one was open for 1% of the time, Pallas kernels for 0%

profile of v1, /device:TPU:22, one launch (start us, length us, event | category | flops | bytes accessed | tf_op | source)
XLA Modules:
  0.0 112.7 jit_solution(8232455670617578964)
XLA Ops:
  1.3 15.0 %shard_map.113 = f32[10,128,128]{2,1,0:T(8,128)} custom-call(s32[1]{0:T(128)} %bitcast.158.count, f32[6,24576]{1,0:T(8,128)} %st.1, f32[1,24576]{1,0:T(1,128)} %bitcast.206, f32[1,24576]{1,0:T(1,128)} %bitcast.207, f32[3,24576]{1,0:T(4,128)} %vel.1, f32[1,24576]{1,0:T(1,128)} %bitcast.208, s32[1,24576]{1,0:T(1,128)} %bitcast.209, s32[1,24576]{1,0:T(1,128)} %bitcast.210), custom_call_target="tpu_custom_call" | custom-call | flops 16106127360 | bytes 1572864 | tf_op jit(solution)/shard_map/pallas_call | solution.py:115
  17.5 3.5 %collective-permute-start = (f32[7,16,1,128]{3,2,1,0:T(1,128)S(1)}, f32[7,16,1,128]{3,2,1,0:T(1,128)S(1)}, u32[]{:S(2)}, u32[]{:S(2)}) collective-permute-start(f32[7,16,1,128]{3,2,1,0:T(1,128)S(1)} %get-tuple-element.34), channel_id=1, source_target_pairs={{0,8},{8,16},{16,24},{1,9},{9,17},{17,25},{2,10},{10,18},{18,26},{... | collective-permute-start | bytes 172040 | tf_op jit(solution)/shard_map/ppermute | solution.py:29
  20.9 2.4 %collective-permute-start.1 = (f32[7,16,1,128]{3,2,1,0:T(1,128)S(1)}, f32[7,16,1,128]{3,2,1,0:T(1,128)S(1)}, u32[]{:S(2)}, u32[]{:S(2)}) collective-permute-start(f32[7,16,1,128]{3,2,1,0:T(1,128)S(1)} %get-tuple-element.35), channel_id=1, source_target_pairs={{8,0},{16,8},{24,16},{9,1},{17,9},{25,17},{10,2},{18,10},{26,18},{... | collective-permute-start | bytes 172040 | tf_op jit(solution)/shard_map/ppermute | solution.py:31
  23.5 3.5 %collective-permute-done.1 = f32[7,16,1,128]{3,2,1,0:T(1,128)S(1)} collective-permute-done((f32[7,16,1,128]{3,2,1,0:T(1,128)S(1)}, f32[7,16,1,128]{3,2,1,0:T(1,128)S(1)}, u32[]{:S(2)}, u32[]{:S(2)}) %collective-permute-start.1) | collective-permute-done | bytes 57376 | tf_op jit(solution)/shard_map/ppermute | solution.py:31
  29.8 4.5 %collective-permute-start.3 = (f32[7,16,10,1]{1,3,2,0:T(1,128)S(1)}, f32[7,16,10,1]{1,3,2,0:T(1,128)S(1)}, u32[]{:S(2)}, u32[]{:S(2)}) collective-permute-start(f32[7,16,10,1]{1,3,2,0:T(1,128)S(1)} %copy.54), channel_id=1, source_target_pairs={{4,0},{5,1},{6,2},{7,3},{12,8},{13,9},{14,10},{15,11},{20,16},{21,... | collective-permute-start | bytes 13448 | tf_op jit(solution)/shard_map/ppermute | solution.py:31
  36.7 1.9 %collective-permute-start.4 = (f32[7,1,10,130]{3,2,1,0:T(8,128)S(1)}, f32[7,1,10,130]{3,2,1,0:T(8,128)S(1)}, u32[]{:S(2)}, u32[]{:S(2)}) collective-permute-start(f32[7,1,10,130]{3,2,1,0:T(8,128)S(1)} %get-tuple-element.17), channel_id=1, source_target_pairs={{0,1},{1,2},{2,3},{4,5},{5,6},{6,7},{8,9},{9,10},{10,11},{12,13},{... | collective-permute-start | bytes 109208 | tf_op jit(solution)/shard_map/ppermute | solution.py:29
  38.6 3.6 %collective-permute-start.5 = (f32[7,1,10,130]{3,2,1,0:T(8,128)S(1)}, f32[7,1,10,130]{3,2,1,0:T(8,128)S(1)}, u32[]{:S(2)}, u32[]{:S(2)}) collective-permute-start(f32[7,1,10,130]{3,2,1,0:T(8,128)S(1)} %get-tuple-element.18), channel_id=1, source_target_pairs={{1,0},{2,1},{3,2},{5,4},{6,5},{7,6},{9,8},{10,9},{11,10},{13,12},{... | collective-permute-start | bytes 109208 | tf_op jit(solution)/shard_map/ppermute | solution.py:31
  42.8 1.8 %collective-permute-done.5 = f32[7,1,10,130]{3,2,1,0:T(8,128)S(1)} collective-permute-done((f32[7,1,10,130]{3,2,1,0:T(8,128)S(1)}, f32[7,1,10,130]{3,2,1,0:T(8,128)S(1)}, u32[]{:S(2)}, u32[]{:S(2)}) %collective-permute-start.5) | collective-permute-done | bytes 36432 | tf_op jit(solution)/shard_map/ppermute | solution.py:31
  47.5 1.9 %collective-permute-start.6 = (f32[3,16,1,128]{3,2,1,0:T(1,128)S(1)}, f32[3,16,1,128]{3,2,1,0:T(1,128)S(1)}, u32[]{:S(2)}, u32[]{:S(2)}) collective-permute-start(f32[3,16,1,128]{3,2,1,0:T(1,128)S(1)} %get-tuple-element.80), channel_id=1, source_target_pairs={{0,8},{8,16},{16,24},{1,9},{9,17},{17,25},{2,10},{10,18},{18,26},{... | collective-permute-start | bytes 73736 | tf_op jit(solution)/shard_map/ppermute | solution.py:29
  49.4 3.9 %collective-permute-start.7 = (f32[3,16,1,128]{3,2,1,0:T(1,128)S(1)}, f32[3,16,1,128]{3,2,1,0:T(1,128)S(1)}, u32[]{:S(2)}, u32[]{:S(2)}) collective-permute-start(f32[3,16,1,128]{3,2,1,0:T(1,128)S(1)} %get-tuple-element.81), channel_id=1, source_target_pairs={{8,0},{16,8},{24,16},{9,1},{17,9},{25,17},{10,2},{18,10},{26,18},{... | collective-permute-start | bytes 73736 | tf_op jit(solution)/shard_map/ppermute | solution.py:31
  53.3 1.8 %collective-permute-done.7 = f32[3,16,1,128]{3,2,1,0:T(1,128)S(1)} collective-permute-done((f32[3,16,1,128]{3,2,1,0:T(1,128)S(1)}, f32[3,16,1,128]{3,2,1,0:T(1,128)S(1)}, u32[]{:S(2)}, u32[]{:S(2)}) %collective-permute-start.7) | collective-permute-done | bytes 24608 | tf_op jit(solution)/shard_map/ppermute | solution.py:31
  56.7 4.6 %collective-permute-start.9 = (f32[3,16,10,1]{3,2,1,0:T(8,128)S(1)}, f32[3,16,10,1]{3,2,1,0:T(8,128)S(1)}, u32[]{:S(2)}, u32[]{:S(2)}) collective-permute-start(f32[3,16,10,1]{3,2,1,0:T(8,128)S(1)} %get-tuple-element.40), channel_id=1, source_target_pairs={{4,0},{5,1},{6,2},{7,3},{12,8},{13,9},{14,10},{15,11},{20,16},{21,... | collective-permute-start | bytes 5768 | tf_op jit(solution)/shard_map/ppermute | solution.py:31
  61.4 3.7 %collective-permute-done.8 = f32[3,16,10,1]{3,2,1,0:T(8,128)S(1)} collective-permute-done((f32[3,16,10,1]{3,2,1,0:T(8,128)S(1)}, f32[3,16,10,1]{3,2,1,0:T(8,128)S(1)}, u32[]{:S(2)}, u32[]{:S(2)}) %collective-permute-start.8) | collective-permute-done | bytes 1952 | tf_op jit(solution)/shard_map/ppermute | solution.py:29
  66.6 1.9 %collective-permute-start.10 = (f32[3,1,10,130]{3,2,1,0:T(8,128)S(1)}, f32[3,1,10,130]{3,2,1,0:T(8,128)S(1)}, u32[]{:S(2)}, u32[]{:S(2)}) collective-permute-start(f32[3,1,10,130]{3,2,1,0:T(8,128)S(1)} %get-tuple-element.25), channel_id=1, source_target_pairs={{0,1},{1,2},{2,3},{4,5},{5,6},{6,7},{8,9},{9,10},{10,11},{12,13},{... | collective-permute-start | bytes 46808 | tf_op jit(solution)/shard_map/ppermute | solution.py:29
  68.6 4.9 %collective-permute-start.11 = (f32[3,1,10,130]{3,2,1,0:T(8,128)S(1)}, f32[3,1,10,130]{3,2,1,0:T(8,128)S(1)}, u32[]{:S(2)}, u32[]{:S(2)}) collective-permute-start(f32[3,1,10,130]{3,2,1,0:T(8,128)S(1)} %get-tuple-element.26), channel_id=1, source_target_pairs={{1,0},{2,1},{3,2},{5,4},{6,5},{7,6},{9,8},{10,9},{11,10},{13,12},{... | collective-permute-start | bytes 46808 | tf_op jit(solution)/shard_map/ppermute | solution.py:31
  77.9 5.5 %all_gather.3 = f32[8,4,1024]{2,1,0:T(4,128)S(1)} all-gather(f32[2,4,1024]{2,1,0:T(4,128)S(1)} %pad_maximum_fusion.53), channel_id=1, replica_groups=mesh['gx'=4,'gy'=2,'gz'=4] {'gz'}, dimensions={0}, use_global_device_ids=true | all-gather | bytes 163840 | tf_op jit(solution)/shard_map/all_gather | solution.py:239
  84.2 3.9 %collective-permute-start.12 = (f32[16,1,128]{2,1,0:T(1,128)S(1)}, f32[16,1,128]{2,1,0:T(1,128)S(1)}, u32[]{:S(2)}, u32[]{:S(2)}) collective-permute-start(f32[16,1,128]{2,1,0:T(1,128)S(1)} %get-tuple-element.101), channel_id=1, source_target_pairs={{8,0},{16,8},{24,16},{9,1},{17,9},{25,17},{10,2},{18,10},{26,18},{... | collective-permute-start | bytes 24584 | tf_op jit(solution)/shard_map/ppermute | solution.py:31
  88.2 1.9 %collective-permute-start.13 = (f32[16,1,128]{2,1,0:T(1,128)S(1)}, f32[16,1,128]{2,1,0:T(1,128)S(1)}, u32[]{:S(2)}, u32[]{:S(2)}) collective-permute-start(f32[16,1,128]{2,1,0:T(1,128)S(1)} %get-tuple-element.100), channel_id=1, source_target_pairs={{0,8},{8,16},{16,24},{1,9},{9,17},{17,25},{2,10},{10,18},{18,26},{... | collective-permute-start | bytes 24584 | tf_op jit(solution)/shard_map/ppermute | solution.py:29
  90.1 3.6 %collective-permute-done.13 = f32[16,1,128]{2,1,0:T(1,128)S(1)} collective-permute-done((f32[16,1,128]{2,1,0:T(1,128)S(1)}, f32[16,1,128]{2,1,0:T(1,128)S(1)}, u32[]{:S(2)}, u32[]{:S(2)}) %collective-permute-start.13) | collective-permute-done | bytes 8224 | tf_op jit(solution)/shard_map/ppermute | solution.py:29
  93.8 4.1 %collective-permute-start.14 = (f32[16,10,1]{2,1,0:T(8,128)S(1)}, f32[16,10,1]{2,1,0:T(8,128)S(1)}, u32[]{:S(2)}, u32[]{:S(2)}) collective-permute-start(f32[16,10,1]{2,1,0:T(8,128)S(1)} %get-tuple-element.83), channel_id=1, source_target_pairs={{4,0},{5,1},{6,2},{7,3},{12,8},{13,9},{14,10},{15,11},{20,16},{21,... | collective-permute-start | bytes 1928 | tf_op jit(solution)/shard_map/ppermute | solution.py:31
  100.5 4.4 %collective-permute-done.15 = f32[16,10,1]{2,1,0:T(8,128)S(1)} collective-permute-done((f32[16,10,1]{2,1,0:T(8,128)S(1)}, f32[16,10,1]{2,1,0:T(8,128)S(1)}, u32[]{:S(2)}, u32[]{:S(2)}) %collective-permute-start.15) | collective-permute-done | bytes 672 | tf_op jit(solution)/shard_map/ppermute | solution.py:29
  104.9 1.9 %collective-permute-start.16 = (f32[1,10,130]{2,1,0:T(8,128)S(1)}, f32[1,10,130]{2,1,0:T(8,128)S(1)}, u32[]{:S(2)}, u32[]{:S(2)}) collective-permute-start(f32[1,10,130]{2,1,0:T(8,128)S(1)} %get-tuple-element.41), channel_id=1, source_target_pairs={{1,0},{2,1},{3,2},{5,4},{6,5},{7,6},{9,8},{10,9},{11,10},{13,12},{... | collective-permute-start | bytes 15608 | tf_op jit(solution)/shard_map/ppermute | solution.py:31
  106.8 2.4 %collective-permute-start.17 = (f32[1,10,130]{2,1,0:T(8,128)S(1)}, f32[1,10,130]{2,1,0:T(8,128)S(1)}, u32[]{:S(2)}, u32[]{:S(2)}) collective-permute-start(f32[1,10,130]{2,1,0:T(8,128)S(1)} %get-tuple-element.42), channel_id=1, source_target_pairs={{0,1},{1,2},{2,3},{4,5},{5,6},{6,7},{8,9},{9,10},{10,11},{12,13},{... | collective-permute-start | bytes 15608 | tf_op jit(solution)/shard_map/ppermute | solution.py:29
  109.4 2.5 %collective-permute-done.17 = f32[1,10,130]{2,1,0:T(8,128)S(1)} collective-permute-done((f32[1,10,130]{2,1,0:T(8,128)S(1)}, f32[1,10,130]{2,1,0:T(8,128)S(1)}, u32[]{:S(2)}, u32[]{:S(2)}) %collective-permute-start.17) | collective-permute-done | bytes 5232 | tf_op jit(solution)/shard_map/ppermute | solution.py:29
  (126 shorter events, 21.3 us)
Async XLA Ops:
  1.3 16.1 %copy-start = (f32[16,8,128]{2,1,0:T(8,128)S(1)}, f32[16,8,128]{2,1,0:T(8,128)}, u32[]{:S(2)}) copy-start(f32[16,8,128]{2,1,0:T(8,128)} %param.19) | copy-start | bytes 196612
  17.5 6.1 %collective-permute-start = (f32[7,16,1,128]{3,2,1,0:T(1,128)S(1)}, f32[7,16,1,128]{3,2,1,0:T(1,128)S(1)}, u32[]{:S(2)}, u32[]{:S(2)}) collective-permute-start(f32[7,16,1,128]{3,2,1,0:T(1,128)S(1)} %get-tuple-element.34), channel_id=1, source_target_pairs={{0,8},{8,16},{16,24},{1,9},{9,17},{17,25},{2,10},{10,18},{18,26},{... | collective-permute-start | bytes 172040 | tf_op jit(solution)/shard_map/ppermute | solution.py:29
  20.9 6.1 %collective-permute-start.1 = (f32[7,16,1,128]{3,2,1,0:T(1,128)S(1)}, f32[7,16,1,128]{3,2,1,0:T(1,128)S(1)}, u32[]{:S(2)}, u32[]{:S(2)}) collective-permute-start(f32[7,16,1,128]{3,2,1,0:T(1,128)S(1)} %get-tuple-element.35), channel_id=1, source_target_pairs={{8,0},{16,8},{24,16},{9,1},{17,9},{25,17},{10,2},{18,10},{26,18},{... | collective-permute-start | bytes 172040 | tf_op jit(solution)/shard_map/ppermute | solution.py:31
  28.0 6.3 %collective-permute-start.2 = (f32[7,16,10,1]{1,3,2,0:T(1,128)S(1)}, f32[7,16,10,1]{1,3,2,0:T(1,128)S(1)}, u32[]{:S(2)}, u32[]{:S(2)}) collective-permute-start(f32[7,16,10,1]{1,3,2,0:T(1,128)S(1)} %copy.53), channel_id=1, source_target_pairs={{0,4},{1,5},{2,6},{3,7},{8,12},{9,13},{10,14},{11,15},{16,20},{17,... | collective-permute-start | bytes 13448 | tf_op jit(solution)/shard_map/ppermute | solution.py:29
  29.8 6.2 %collective-permute-start.3 = (f32[7,16,10,1]{1,3,2,0:T(1,128)S(1)}, f32[7,16,10,1]{1,3,2,0:T(1,128)S(1)}, u32[]{:S(2)}, u32[]{:S(2)}) collective-permute-start(f32[7,16,10,1]{1,3,2,0:T(1,128)S(1)} %copy.54), channel_id=1, source_target_pairs={{4,0},{5,1},{6,2},{7,3},{12,8},{13,9},{14,10},{15,11},{20,16},{21,... | collective-permute-start | bytes 13448 | tf_op jit(solution)/shard_map/ppermute | solution.py:31
  36.7 6.1 %collective-permute-start.4 = (f32[7,1,10,130]{3,2,1,0:T(8,128)S(1)}, f32[7,1,10,130]{3,2,1,0:T(8,128)S(1)}, u32[]{:S(2)}, u32[]{:S(2)}) collective-permute-start(f32[7,1,10,130]{3,2,1,0:T(8,128)S(1)} %get-tuple-element.17), channel_id=1, source_target_pairs={{0,1},{1,2},{2,3},{4,5},{5,6},{6,7},{8,9},{9,10},{10,11},{12,13},{... | collective-permute-start | bytes 109208 | tf_op jit(solution)/shard_map/ppermute | solution.py:29
  38.6 6.0 %collective-permute-start.5 = (f32[7,1,10,130]{3,2,1,0:T(8,128)S(1)}, f32[7,1,10,130]{3,2,1,0:T(8,128)S(1)}, u32[]{:S(2)}, u32[]{:S(2)}) collective-permute-start(f32[7,1,10,130]{3,2,1,0:T(8,128)S(1)} %get-tuple-element.18), channel_id=1, source_target_pairs={{1,0},{2,1},{3,2},{5,4},{6,5},{7,6},{9,8},{10,9},{11,10},{13,12},{... | collective-permute-start | bytes 109208 | tf_op jit(solution)/shard_map/ppermute | solution.py:31
  45.9 1.1 copy-start.2
  47.5 5.9 %collective-permute-start.6 = (f32[3,16,1,128]{3,2,1,0:T(1,128)S(1)}, f32[3,16,1,128]{3,2,1,0:T(1,128)S(1)}, u32[]{:S(2)}, u32[]{:S(2)}) collective-permute-start(f32[3,16,1,128]{3,2,1,0:T(1,128)S(1)} %get-tuple-element.80), channel_id=1, source_target_pairs={{0,8},{8,16},{16,24},{1,9},{9,17},{17,25},{2,10},{10,18},{18,26},{... | collective-permute-start | bytes 73736 | tf_op jit(solution)/shard_map/ppermute | solution.py:29
  49.4 5.7 %collective-permute-start.7 = (f32[3,16,1,128]{3,2,1,0:T(1,128)S(1)}, f32[3,16,1,128]{3,2,1,0:T(1,128)S(1)}, u32[]{:S(2)}, u32[]{:S(2)}) collective-permute-start(f32[3,16,1,128]{3,2,1,0:T(1,128)S(1)} %get-tuple-element.81), channel_id=1, source_target_pairs={{8,0},{16,8},{24,16},{9,1},{17,9},{25,17},{10,2},{18,10},{26,18},{... | collective-permute-start | bytes 73736 | tf_op jit(solution)/shard_map/ppermute | solution.py:31
  55.4 9.7 %collective-permute-start.8 = (f32[3,16,10,1]{3,2,1,0:T(8,128)S(1)}, f32[3,16,10,1]{3,2,1,0:T(8,128)S(1)}, u32[]{:S(2)}, u32[]{:S(2)}) collective-permute-start(f32[3,16,10,1]{3,2,1,0:T(8,128)S(1)} %get-tuple-element.39), channel_id=1, source_target_pairs={{0,4},{1,5},{2,6},{3,7},{8,12},{9,13},{10,14},{11,15},{16,20},{17,... | collective-permute-start | bytes 5768 | tf_op jit(solution)/shard_map/ppermute | solution.py:29
  56.7 9.9 %collective-permute-start.9 = (f32[3,16,10,1]{3,2,1,0:T(8,128)S(1)}, f32[3,16,10,1]{3,2,1,0:T(8,128)S(1)}, u32[]{:S(2)}, u32[]{:S(2)}) collective-permute-start(f32[3,16,10,1]{3,2,1,0:T(8,128)S(1)} %get-tuple-element.40), channel_id=1, source_target_pairs={{4,0},{5,1},{6,2},{7,3},{12,8},{13,9},{14,10},{15,11},{20,16},{21,... | collective-permute-start | bytes 5768 | tf_op jit(solution)/shard_map/ppermute | solution.py:31
  66.6 6.9 %collective-permute-start.10 = (f32[3,1,10,130]{3,2,1,0:T(8,128)S(1)}, f32[3,1,10,130]{3,2,1,0:T(8,128)S(1)}, u32[]{:S(2)}, u32[]{:S(2)}) collective-permute-start(f32[3,1,10,130]{3,2,1,0:T(8,128)S(1)} %get-tuple-element.25), channel_id=1, source_target_pairs={{0,1},{1,2},{2,3},{4,5},{5,6},{6,7},{8,9},{9,10},{10,11},{12,13},{... | collective-permute-start | bytes 46808 | tf_op jit(solution)/shard_map/ppermute | solution.py:29
  68.6 6.4 %collective-permute-start.11 = (f32[3,1,10,130]{3,2,1,0:T(8,128)S(1)}, f32[3,1,10,130]{3,2,1,0:T(8,128)S(1)}, u32[]{:S(2)}, u32[]{:S(2)}) collective-permute-start(f32[3,1,10,130]{3,2,1,0:T(8,128)S(1)} %get-tuple-element.26), channel_id=1, source_target_pairs={{1,0},{2,1},{3,2},{5,4},{6,5},{7,6},{9,8},{10,9},{11,10},{13,12},{... | collective-permute-start | bytes 46808 | tf_op jit(solution)/shard_map/ppermute | solution.py:31
  73.5 2.2 %copy-start.3 = (f32[16,8,128]{2,1,0:T(8,128)S(1)}, f32[16,8,128]{2,1,0:T(8,128)}, u32[]{:S(2)}) copy-start(f32[16,8,128]{2,1,0:T(8,128)} %param.18) | copy-start | bytes 196612
  84.2 28.5 %copy-start.1 = (f32[2,8,8,128]{3,2,1,0:T(8,128)}, f32[2,8,8,128]{3,2,1,0:T(8,128)S(1)}, u32[]{:S(2)}) copy-start(f32[2,8,8,128]{3,2,1,0:T(8,128)S(1)} %copy.85) | copy-start | bytes 196612
  84.2 5.9 %collective-permute-start.12 = (f32[16,1,128]{2,1,0:T(1,128)S(1)}, f32[16,1,128]{2,1,0:T(1,128)S(1)}, u32[]{:S(2)}, u32[]{:S(2)}) collective-permute-start(f32[16,1,128]{2,1,0:T(1,128)S(1)} %get-tuple-element.101), channel_id=1, source_target_pairs={{8,0},{16,8},{24,16},{9,1},{17,9},{25,17},{10,2},{18,10},{26,18},{... | collective-permute-start | bytes 24584 | tf_op jit(solution)/shard_map/ppermute | solution.py:31
  88.2 5.5 %collective-permute-start.13 = (f32[16,1,128]{2,1,0:T(1,128)S(1)}, f32[16,1,128]{2,1,0:T(1,128)S(1)}, u32[]{:S(2)}, u32[]{:S(2)}) collective-permute-start(f32[16,1,128]{2,1,0:T(1,128)S(1)} %get-tuple-element.100), channel_id=1, source_target_pairs={{0,8},{8,16},{16,24},{1,9},{9,17},{17,25},{2,10},{10,18},{18,26},{... | collective-permute-start | bytes 24584 | tf_op jit(solution)/shard_map/ppermute | solution.py:29
  93.8 6.6 %collective-permute-start.14 = (f32[16,10,1]{2,1,0:T(8,128)S(1)}, f32[16,10,1]{2,1,0:T(8,128)S(1)}, u32[]{:S(2)}, u32[]{:S(2)}) collective-permute-start(f32[16,10,1]{2,1,0:T(8,128)S(1)} %get-tuple-element.83), channel_id=1, source_target_pairs={{4,0},{5,1},{6,2},{7,3},{12,8},{13,9},{14,10},{15,11},{20,16},{21,... | collective-permute-start | bytes 1928 | tf_op jit(solution)/shard_map/ppermute | solution.py:31
  98.0 6.9 %collective-permute-start.15 = (f32[16,10,1]{2,1,0:T(8,128)S(1)}, f32[16,10,1]{2,1,0:T(8,128)S(1)}, u32[]{:S(2)}, u32[]{:S(2)}) collective-permute-start(f32[16,10,1]{2,1,0:T(8,128)S(1)} %get-tuple-element.82), channel_id=1, source_target_pairs={{0,4},{1,5},{2,6},{3,7},{8,12},{9,13},{10,14},{11,15},{16,20},{17,... | collective-permute-start | bytes 1928 | tf_op jit(solution)/shard_map/ppermute | solution.py:29
  104.9 4.5 %collective-permute-start.16 = (f32[1,10,130]{2,1,0:T(8,128)S(1)}, f32[1,10,130]{2,1,0:T(8,128)S(1)}, u32[]{:S(2)}, u32[]{:S(2)}) collective-permute-start(f32[1,10,130]{2,1,0:T(8,128)S(1)} %get-tuple-element.41), channel_id=1, source_target_pairs={{1,0},{2,1},{3,2},{5,4},{6,5},{7,6},{9,8},{10,9},{11,10},{13,12},{... | collective-permute-start | bytes 15608 | tf_op jit(solution)/shard_map/ppermute | solution.py:31
  106.8 5.1 %collective-permute-start.17 = (f32[1,10,130]{2,1,0:T(8,128)S(1)}, f32[1,10,130]{2,1,0:T(8,128)S(1)}, u32[]{:S(2)}, u32[]{:S(2)}) collective-permute-start(f32[1,10,130]{2,1,0:T(8,128)S(1)} %get-tuple-element.42), channel_id=1, source_target_pairs={{0,1},{1,2},{2,3},{4,5},{5,6},{6,7},{8,9},{9,10},{10,11},{12,13},{... | collective-permute-start | bytes 15608 | tf_op jit(solution)/shard_map/ppermute | solution.py:29

commit v2 on v0

v2 whole, which is shorter than its diff:
```python
import functools

import jax
import jax.numpy as jnp
from jax import lax
from jax.experimental import pallas as pl
from jax.experimental.pallas import tpu as pltpu
from jax.sharding import PartitionSpec as P

bf = jnp.bfloat16
f8 = jnp.float8_e4m3fn
f32 = jnp.float32
i32 = jnp.int32

LEVELS, ROWS, COLS = 16, 8, 128
CELLS = LEVELS * ROWS

ZX, YZ, ZZ, XX, YY, XY, MX, MY, MZ, MASS, POR, PERM = range(12)
FIELDS = 12
STRESS_ORDER = (5, 4, 2, 0, 1, 3)

X_ROWS = (
    (ZX, 0), (ZX, 1), (YZ, 0), (ZZ, 0), (PERM, 0),
    (XX, 0), (XX, 1), (XX, 2), (XY, 0), (XY, 1), (YY, 0),
    (MX, 0), (MX, 1), (MY, 0), (MZ, 0), (MASS, 0), (MASS, 1), (POR, 0),
)
X_LEVEL = 5
Y_DEPTH = {ZX: 1, YZ: 2, ZZ: 1, XX: 1, YY: 3, XY: 2, MX: 1, MY: 2, MZ: 1, MASS: 2, POR: 1, PERM: 1}
Y_PLACE = {}
_at = 0
for _f in range(FIELDS):
    Y_PLACE[_f] = _at + Y_DEPTH[_f]
    _at += 2 * Y_DEPTH[_f]
HALF = 64
Z_FIELDS = (ZX, YZ, ZZ, PERM)
Z_X = 8 * len(Z_FIELDS)
Z_Y = Z_X + 16
Z_ROWS = Z_Y + 8
REDUCED = 10
RED_X = 8 * REDUCED
RED_Y = RED_X + 24
RED_ROWS = RED_Y + 8


def tile_iota(dim):
    return lax.broadcasted_iota(i32, (ROWS, COLS), dim)


def turn(tile, shift, axis):
    shift %= tile.shape[axis]
    return tile if shift == 0 else pltpu.roll(tile, shift, axis)


def row_stress(trial, mean, cons, flag):
    part = lax.broadcasted_iota(i32, trial.shape, 0)
    size = jnp.sqrt(
        jnp.sum(trial * trial * jnp.where(part < 3, 1.5, 3.0), axis=0, keepdims=True)
    )
    yield_size = 1.2 * jnp.sqrt(mean * (cons - mean))
    factor = jnp.where(flag == 1, yield_size / jnp.maximum(size, 1.0), 1.0)
    return trial * factor - jnp.where(part < 3, mean, 0.0)


def scatter_kernel(
    chunk, count, trial, mean, cons, vel, wt, cell, flag, por, perm, out, low, high, acc
):
    step = pl.program_id(0)
    slot = step * chunk + lax.broadcasted_iota(i32, (1, chunk), 1)
    weight = jnp.where(slot < count[0], wt[...], 0.0)
    stress = row_stress(trial[...], mean[...], cons[...], flag[...]) * weight
    momentum = vel[...] * weight
    place = cell[...]
    hi = (place >> 7) & 63
    lo = ((place >> 13) << 7) | (place & 127)

    def spread(row, count, kind):
        return jnp.broadcast_to(row, (count, chunk)).astype(kind)

    one, zero = jnp.array(1, bf), jnp.array(0, bf)
    base = lax.broadcasted_iota(i32, (16, chunk), 0)

    def equal(index, count):
        index = spread(index.astype(f32), 16, bf)
        return [(base + b * 16).astype(f32).astype(bf) == index for b in range(count // 16)]

    hi_mask = equal(hi, 64)
    right = jnp.concatenate([jnp.where(m, one, zero) for m in equal(lo, 256)], axis=0)
    base32 = lax.broadcasted_iota(i32, (32, chunk), 0)
    hi_mask8 = [base32 + 32 * b == jnp.broadcast_to(hi, (32, chunk)) for b in range(2)]
    zero8 = jnp.zeros((32, chunk), f8)
    rows = [stress[i : i + 1] for i in STRESS_ORDER]
    rows += [momentum[i : i + 1] for i in range(3)] + [weight]
    left, left8 = [], []
    for row in rows:
        top = row.astype(bf).astype(f32)
        part = spread(top, 16, bf)
        left += [jnp.where(m, part, zero) for m in hi_mask]
        part = spread((row - top) * 256.0, 32, f8)
        left8 += [jnp.where(m, part, zero8) for m in hi_mask8]
    left = jnp.concatenate(left, axis=0)
    left8 = jnp.concatenate(left8, axis=0)
    dims = (((1,), (1,)), ((), ()))
    prod = lax.dot_general(left, right, dims, preferred_element_type=f32)
    prod8 = lax.dot_general(left8, right.astype(f8), dims, preferred_element_type=f32)
    prod = prod + prod8 * (1 / 256.0)

    @pl.when(step == 0)
    def _():
        acc[...] = prod

    @pl.when(step > 0)
    def _():
        acc[...] += prod

    @pl.when(step == pl.num_programs(0) - 1)
    def _():
        for i in range(10):
            out[i, 0:64, :] = acc[i * 64 : i * 64 + 64, :COLS]
            out[i, 64:128, :] = acc[i * 64 : i * 64 + 64, COLS:]
        for q, (field, depth) in enumerate(X_ROWS):
            for face, row in ((low, depth), (high, ROWS - 1 - depth)):
                rows = pl.ds(row, LEVELS, stride=ROWS)
                if field < 10:
                    face[q] = out[field, rows, :]
                else:
                    face[q] = (por if field == POR else perm)[rows, :]


def scatter(trial, mean, cons, vel, wt, cell, flag, count, por, perm):
    points = mean.shape[0]
    chunk = 8192 if points % 8192 == 0 else points
    row = lambda v: v.reshape(1, points)
    spec = lambda r: pl.BlockSpec((r, chunk), lambda i: (0, i))
    fixed = lambda *shape: pl.BlockSpec(shape, lambda i: (0,) * len(shape))
    faces = (len(X_ROWS), LEVELS, COLS)
    return pl.pallas_call(
        functools.partial(scatter_kernel, chunk),
        grid=(points // chunk,),
        in_specs=[pl.BlockSpec(memory_space=pltpu.SMEM)]
        + [spec(r) for r in (6, 1, 1, 3, 1, 1, 1)]
        + [fixed(CELLS, COLS)] * 2,
        out_specs=[fixed(10, CELLS, COLS), fixed(*faces), fixed(*faces)],
        out_shape=[
            jax.ShapeDtypeStruct((10, CELLS, COLS), f32),
            jax.ShapeDtypeStruct(faces, f32),
            jax.ShapeDtypeStruct(faces, f32),
        ],
        scratch_shapes=[pltpu.VMEM((640, 256), f32)],
        compiler_params=pltpu.CompilerParams(vmem_limit_bytes=60 << 20),
        cost_estimate=pl.CostEstimate(
            flops=2 * 960 * 256 * points, bytes_accessed=64 * points, transcendentals=0
        ),
        name="point_sums",
    )(count.reshape(1), trial, row(mean), row(cons), vel, row(wt), row(cell), row(flag), por, perm)


def y_pack_kernel(sums, por, perm, below, above, out):
    lane = lax.broadcasted_iota(i32, (CELLS, COLS), 1)
    lane16 = lax.broadcasted_iota(i32, (LEVELS, COLS), 1)
    packed = jnp.zeros((CELLS, COLS), f32)
    for field in range(FIELDS):
        at, depth = Y_PLACE[field], Y_DEPTH[field]
        own = sums[field] if field < 10 else (por if field == POR else perm)[...]
        packed = jnp.where((lane >= at - depth) & (lane < at + depth), turn(own, at, 1), packed)
    slots = [jnp.zeros((LEVELS, COLS), f32)] * ROWS
    for q, (field, deep) in enumerate(X_ROWS):
        at, depth = Y_PLACE[field] + HALF, Y_DEPTH[field]
        mask = (lane16 >= at - depth) & (lane16 < at + depth)
        for source, slot in ((above, deep), (below, ROWS - 1 - deep)):
            slots[slot] = jnp.where(mask, turn(source[q], at, 1), slots[slot])
    out[...] = jnp.where(lane < HALF, packed, jnp.concatenate(slots, axis=0))


def y_pack(sums, por, perm, below, above):
    return pl.pallas_call(
        y_pack_kernel,
        out_shape=jax.ShapeDtypeStruct((CELLS, COLS), f32),
        name="y_pack",
    )(sums, por, perm, below, above)


def y_from_above(shape):
    lane = lax.broadcasted_iota(i32, shape, 1) & (HALF - 1)
    mask = lane < 0
    for field in range(FIELDS):
        at = Y_PLACE[field]
        mask |= (lane >= at) & (lane < at + Y_DEPTH[field])
    return mask


Y_LOW, Y_HIGH, Z_LOW, Z_HIGH, X_HAS_LOW, X_HAS_HIGH, Y_HAS_LOW, Y_HAS_HIGH, Z_HAS_LOW, Z_HAS_HIGH, LAYER = range(11)


def met(where, packs, from_above, rows):
    low = packs[where[Y_LOW], rows, :] * where[Y_HAS_LOW].astype(f32)
    high = packs[where[Y_HIGH], rows, :] * where[Y_HAS_HIGH].astype(f32)
    return jnp.where(from_above, high, low)


def z_pack_kernel(where, first, last, perm_first, perm_last, below, above, packs, out):
    from_above = y_from_above((ROWS, COLS))
    lane = tile_iota(1)
    for side, (tiles, perm, level) in enumerate(
        ((first, perm_first, 0), (last, perm_last, LEVELS - 1))
    ):
        at = side * Z_ROWS
        for n in range(3):
            out[at + 8 * n : at + 8 * n + 8, :] = tiles[n]
        out[at + 24 : at + 32, :] = perm[...]
        for n, source in enumerate((below, above)):
            rows = [source[q, level : level + 1, :] for q in range(X_LEVEL)]
            rows.append(jnp.zeros((8 - X_LEVEL, COLS), f32))
            out[at + Z_X + 8 * n : at + Z_X + 8 * n + 8, :] = jnp.concatenate(rows, axis=0)
        own = met(where, packs, from_above, pl.ds(level * ROWS, ROWS))
        rim = met(where, packs, from_above, pl.ds(level, ROWS, stride=LEVELS))
        out[at + Z_Y : at + Z_Y + 8, :] = jnp.where(lane < HALF, own, rim)


def z_pack(where, sums, perm, below, above, packs):
    whole = lambda v: pl.BlockSpec(v.shape, lambda i: (0,) * v.ndim)
    block = lambda n: pl.BlockSpec((ROWS, COLS), lambda i: (n, 0))
    tiles = lambda n: pl.BlockSpec((3, ROWS, COLS), lambda i: (0, n, 0))
    rim = pl.BlockSpec((8, LEVELS, COLS), lambda i: (0, 0, 0))
    return pl.pallas_call(
        z_pack_kernel,
        grid=(1,),
        in_specs=[
            pl.BlockSpec(memory_space=pltpu.SMEM),
            tiles(0), tiles(LEVELS - 1), block(0), block(LEVELS - 1), rim, rim, whole(packs),
        ],
        out_specs=pl.BlockSpec((2 * Z_ROWS, COLS), lambda i: (0, 0)),
        out_shape=jax.ShapeDtypeStruct((2 * Z_ROWS, COLS), f32),
        name="z_pack",
    )(where, sums, sums, perm, perm, below, above, packs)


def diff_x(own, rim):
    row = tile_iota(0)
    own_up, rim_up = turn(own, -1, 0), turn(rim, -1, 0)
    own_down, rim_down = turn(own, 1, 0), turn(rim, 1, 0)
    top, bottom = row == ROWS - 1, row == 0
    return (
        jnp.where(top, rim_up, own_up) - jnp.where(bottom, rim_down, own_down),
        jnp.where(top, own_up, rim_up) - jnp.where(bottom, own_down, rim_down),
    )


def diff_y(own, rim):
    lane = tile_iota(1)
    own_up, rim_up = turn(own, -1, 1), turn(rim, -1, 1)
    own_down, rim_down = turn(own, 1, 1), turn(rim, 1, 1)
    top, bottom = lane == COLS - 1, lane == 0
    return (
        jnp.where(top, rim_up, own_up) - jnp.where(bottom, rim_down, own_down),
        jnp.where(top, own_up, rim_up) - jnp.where(bottom, own_down, rim_down),
    )


def ext_x(t):
    a0, a1 = diff_x(t[0], t[1])
    b0, b1 = diff_x(t[2], t[3])
    return [a0, a1, b0, b1]


def ext_y(t):
    a0, a2 = diff_y(t[0], t[2])
    b1, b3 = diff_y(t[1], t[3])
    return [a0, b1, a2, b3]


def rim_masks(where):
    row, lane = tile_iota(0), tile_iota(1)
    has = lambda low, high, test: jnp.where(test, where[high], where[low]) == 1
    in_x = has(X_HAS_LOW, X_HAS_HIGH, row < 4)
    in_y = has(Y_HAS_LOW, Y_HAS_HIGH, lane < HALF)
    return in_x, in_y, in_x & in_y


def local_kernel(
    where, sums, por, perm, below, above, packs, levels, vel, inner, out, rim, corner
):
    rim[...] = jnp.zeros_like(rim)
    for q, (field, deep) in enumerate(X_ROWS):
        rim[field, pl.ds(deep, LEVELS, stride=ROWS), :] = above[q]
        rim[field, pl.ds(ROWS - 1 - deep, LEVELS, stride=ROWS), :] = below[q]
    from_above = y_from_above((LEVELS, COLS))
    for slot in range(ROWS):
        rows = pl.ds(slot * LEVELS, LEVELS)
        corner[pl.ds(slot, LEVELS, stride=ROWS), :] = met(where, packs, from_above, rows)
    from_above = y_from_above((ROWS, COLS))
    in_x, in_y, in_xy = rim_masks(where)

    y_tiles = [met(where, packs, from_above, pl.ds(l * ROWS, ROWS)) for l in range(LEVELS)]

    def field_at(field, level):
        rows = pl.ds(level * ROWS, ROWS)
        at = Y_PLACE[field]
        own = sums[field, rows, :] if field < 10 else (por if field == POR else perm)[rows, :]
        return [
            own,
            rim[field, rows, :],
            turn(y_tiles[level], -at, 1),
            turn(corner[rows, :], -at - HALF, 1),
        ]

    def far_level(place, has, side):
        at = side * Z_ROWS
        has = where[has].astype(f32)
        read = lambda first, count: levels[where[place], pl.ds(at + first, count), :] * has
        lanes = read(Z_Y, 8)
        low, high = read(Z_X, 8), read(Z_X + 8, 8)
        row = tile_iota(0)
        found = {}
        for n, field in enumerate(Z_FIELDS):
            tile = jnp.zeros((ROWS, COLS), f32)
            for q, (other, deep) in enumerate(X_ROWS[:X_LEVEL]):
                if other == field:
                    tile = jnp.where(row == deep, turn(high, deep - q, 0), tile)
                    tile = jnp.where(
                        row == ROWS - 1 - deep, turn(low, ROWS - 1 - deep - q, 0), tile
                    )
            found[field] = [
                read(8 * n, 8),
                tile,
                turn(lanes, -Y_PLACE[field], 1),
                turn(lanes, -Y_PLACE[field] - HALF, 1),
            ]
        return found

    far_low = far_level(Z_LOW, Z_HAS_LOW, 1)
    far_high = far_level(Z_HIGH, Z_HAS_HIGH, 0)
    memo = {}

    def get(field, level):
        if level < 0:
            return far_low[field]
        if level >= LEVELS:
            return far_high[field]
        if (field, level) not in memo:
            memo[field, level] = field_at(field, level)
        return memo[field, level]

    def star(level):
        mass = get(MASS, level)
        inverse = [1.0 / jnp.maximum(m, 0.5) for m in mass]
        dz = lambda f: [u - d for u, d in zip(get(f, level + 1), get(f, level - 1))]
        forces = (
            (ext_x(get(XX, level)), ext_y(get(XY, level)), dz(ZX)),
            (ext_x(get(XY, level)), ext_y(get(YY, level)), dz(YZ)),
            (ext_x(get(ZX, level)), ext_y(get(YZ, level)), dz(ZZ)),
        )
        found = []
        for field, (fx, fy, fz) in zip((MX, MY, MZ), forces):
            parts = []
            for n, m in enumerate(get(field, level)):
                value = (m + 0.125 * (fx[n] + fy[n] + fz[n])) * inverse[n]
                if n > 0:
                    value = jnp.where((in_x, in_y, in_xy)[n - 1], value, 0.0)
                parts.append(value)
            found.append(parts)
        return found

    def level_perm(level):
        tiles = get(PERM, level)[:3]
        if 0 <= level < LEVELS:
            tiles = [tiles[0]] + [jnp.where(t > 0.0, t, 1.0) for t in tiles[1:]]
        return tiles

    def faces(level):
        pairs = zip(level_perm(level), level_perm(level + 1))
        return [0.5 * a * b / (a + b) for a, b in pairs]

    zero3 = [jnp.zeros((ROWS, COLS), f32)] * 3
    stars = {0: star(0)}
    first_star = stars[0][2]
    down = faces(-1)
    state = None
    kept = []
    first_terms = last_terms = None
    for level in range(LEVELS):
        if level + 1 < LEVELS:
            stars[level + 1] = star(level + 1)
        vx, vy, vz = stars[level]
        for n, part in enumerate((vx, vy, vz)):
            vel[n, pl.ds(level * ROWS, ROWS), :] = part[0]
        z_up = stars[level + 1][2] if level + 1 < LEVELS else zero3
        z_down = stars[level - 1][2] if level > 0 else zero3
        stars.pop(level - 2, None)
        for key in [k for k in memo if k[1] < level - 1]:
            del memo[key]
        dx, dy = ext_x(vx), ext_y(vy)
        porosity = get(POR, level)[:3]
        up = faces(level)
        open_top = where[Z_HAS_HIGH] == 0
        k_own = level_perm(level)
        now = []
        for n in range(3):
            source = -0.0015 * (1.0 - porosity[n])
            right = source * (dx[n] + dy[n] + (z_up[n] - z_down[n]))
            top = up[n]
            if level == LEVELS - 1:
                top = jnp.where(open_top, 0.25 * k_own[n], top)
            main = 0.002 * porosity[n] + (down[n] + top)
            now.append((-down[n], main, -up[n], right, source))
        down = up
        if level == 0:
            first_terms = now
        elif level == LEVELS - 1:
            last_terms = now
        elif level == 1:
            kept.append([(lo, 1.0 / mid, hi, r) for lo, mid, hi, r, _ in now])
        else:
            rows = []
            for (lo, mid, hi, r, _), (f, inv, u, pr) in zip(now, kept[-1]):
                w = lo * inv
                rows.append((-w * f, 1.0 / (mid - w * u), hi, r - w * pr))
            kept.append(rows)
    after = None
    for n_row in range(len(kept) - 1, -1, -1):
        rows = []
        for t in range(3):
            f, inv, u, r = kept[n_row][t]
            if after is None:
                rows.append((r * inv, -f * inv, -u * inv))
            else:
                b2, f2, g2 = after[t]
                rows.append(((r - u * b2) * inv, -(f + u * f2) * inv, -u * g2 * inv))
            for m in range(3):
                inner[t, m, n_row] = rows[t][m]
        if after is None:
            last_inner = rows
        after = rows
    first_inner = after
    values = []
    for t in range(3):
        lo, mid, hi, r, source = first_terms[t]
        b, f, g = first_inner[t]
        inv = 1.0 / (mid + hi * f)
        mine = [lo * inv, hi * g * inv, (r - hi * b) * inv, -source * inv]
        lo, mid, hi, r, source = last_terms[t]
        b, f, g = last_inner[t]
        inv = 1.0 / (mid + lo * g)
        mine += [lo * f * inv, hi * inv, (r - lo * b) * inv, source * inv]
        mine += [first_star[t], stars[LEVELS - 1][2][t]]
        values.append(mine)
    row, lane = tile_iota(0), tile_iota(1)
    x_parts = [jnp.zeros((ROWS, COLS), f32)] * 3
    y_part = jnp.zeros((ROWS, COLS), f32)
    for q in range(REDUCED):
        out[8 * q : 8 * q + 8, :] = values[0][q]
        at = 2 * q % 8
        x_parts[q // 4] = jnp.where(
            (row == at) | (row == at + 1), turn(values[1][q], at + 1, 0), x_parts[q // 4]
        )
        y_part = jnp.where(
            (lane == 2 * q) | (lane == 2 * q + 1), turn(values[2][q], 2 * q + 1, 1), y_part
        )
    for n in range(3):
        out[RED_X + 8 * n : RED_X + 8 * n + 8, :] = x_parts[n]
    out[RED_Y : RED_Y + 8, :] = y_part


def local_solve(where, sums, por, perm, below, above, packs, levels):
    smem = pl.BlockSpec(memory_space=pltpu.SMEM)
    vmem = pl.BlockSpec(memory_space=pltpu.VMEM)
    return pl.pallas_call(
        local_kernel,
        in_specs=[smem] + [vmem] * 7,
        out_shape=[
            jax.ShapeDtypeStruct((3, CELLS, COLS), f32),
            jax.ShapeDtypeStruct((3, 3, LEVELS - 2, ROWS, COLS), f32),
            jax.ShapeDtypeStruct((RED_ROWS, COLS), f32),
        ],
        scratch_shapes=[pltpu.VMEM((FIELDS, CELLS, COLS), f32), pltpu.VMEM((CELLS, COLS), f32)],
        compiler_params=pltpu.CompilerParams(vmem_limit_bytes=32 << 20),
        name="local_solve",
    )(where, sums, por, perm, below, above, packs, levels)


def final_kernel(layers, where, vel, inner, reduced, out, pressure):
    me = where[LAYER]

    def value(k, q):
        own = reduced[k, 8 * q : 8 * q + 8, :]
        at = RED_X + 8 * (q // 4)
        x = turn(reduced[k, at : at + 8, :], -(2 * q % 8 + 1), 0)
        y = turn(reduced[k, RED_Y : RED_Y + 8, :], -(2 * q + 1), 1)
        return [own, x, y]

    rows = []
    for k in range(layers):
        a = [value(k, q) for q in range(REDUCED)]
        rf, rl = a[2], a[6]
        if k > 0:
            below = value(k - 1, 9)
            rf = [r + c * v for r, c, v in zip(rf, a[3], below)]
        if k + 1 < layers:
            above = value(k + 1, 8)
            rl = [r + c * v for r, c, v in zip(rl, a[7], above)]
        rows.append((a[0], a[1], rf))
        rows.append((a[4], a[5], rl))
    done = []
    for n, (lo, hi, r) in enumerate(rows):
        if n == 0:
            done.append((hi, r))
            continue
        hs, rs = done[-1]
        inv = [1.0 / (1.0 - l * h) for l, h in zip(lo, hs)]
        done.append(
            (
                [h * i for h, i in zip(hi, inv)],
                [(a - l * b) * i for a, l, b, i in zip(r, lo, rs, inv)],
            )
        )
    ends = [None] * len(rows)
    ends[-1] = done[-1][1]
    for n in range(len(rows) - 2, -1, -1):
        hs, rs = done[n]
        ends[n] = [r - h * e for r, h, e in zip(rs, hs, ends[n + 1])]

    def pick(offset):
        chosen = [jnp.zeros((ROWS, COLS), f32)] * 3
        for k in range(layers):
            n = 2 * k + offset
            if 0 <= n < len(rows):
                chosen = [jnp.where(me == k, e, c) for e, c in zip(ends[n], chosen)]
        return chosen

    first, last = pick(0), pick(1)
    under, over = pick(-1)[0], pick(2)[0]
    in_x, in_y, _ = rim_masks(where)

    def press(level):
        if level < 0:
            return [under]
        if level >= LEVELS:
            return [over]
        if level == 0:
            parts = first
        elif level == LEVELS - 1:
            parts = last
        else:
            parts = [
                inner[t, 0, level - 1]
                + inner[t, 1, level - 1] * first[t]
                + inner[t, 2, level - 1] * last[t]
                for t in range(3)
            ]
        return [parts[0], jnp.where(in_x, parts[1], 0.0), jnp.where(in_y, parts[2], 0.0)]

    before, now = press(-1), press(0)
    for level in range(LEVELS):
        after = press(level + 1)
        rows_at = pl.ds(level * ROWS, ROWS)
        pressure[rows_at, :] = now[0]
        grads = (
            diff_x(now[0], now[1])[0],
            diff_y(now[0], now[2])[0],
            after[0] - before[0],
        )
        for n in range(3):
            out[n, rows_at, :] = vel[n, rows_at, :] - 0.125 * grads[n]
        before, now = now, after


def final(where, vel, inner, reduced):
    smem = pl.BlockSpec(memory_space=pltpu.SMEM)
    vmem = pl.BlockSpec(memory_space=pltpu.VMEM)
    return pl.pallas_call(
        functools.partial(final_kernel, reduced.shape[0]),
        in_specs=[smem] + [vmem] * 3,
        out_shape=[
            jax.ShapeDtypeStruct((3, CELLS, COLS), f32),
            jax.ShapeDtypeStruct((CELLS, COLS), f32),
        ],
        compiler_params=pltpu.CompilerParams(vmem_limit_bytes=32 << 20),
        name="final",
    )(where, vel, inner, reduced)


def shift_up(block, axis):
    count = lax.axis_size(axis)
    return lax.ppermute(block, axis, [(i, i + 1) for i in range(count - 1)])


def shift_down(block, axis):
    count = lax.axis_size(axis)
    return lax.ppermute(block, axis, [(i + 1, i) for i in range(count - 1)])


def neighbours(block, axis):
    count, me = lax.axis_size(axis), lax.axis_index(axis)
    if count > 4:
        return jnp.stack([shift_up(block, axis), shift_down(block, axis)]), 0, 1
    stacked = lax.all_gather(block, axis, axis=0)
    return stacked, jnp.maximum(me - 1, 0), jnp.minimum(me + 1, count - 1)


def shards(trial, mean, cons, vel, wt, cell, flag, count, por, perm):
    por = por.reshape(CELLS, COLS)
    perm = perm.reshape(CELLS, COLS)
    sums, low, high = scatter(trial, mean, cons, vel, wt, cell, flag, count, por, perm)
    above = shift_down(low, "gx")
    below = shift_up(high, "gx")

    def ends(axis):
        me = lax.axis_index(axis)
        return [(me > 0).astype(i32), (me < lax.axis_size(axis) - 1).astype(i32)]

    has = ends("gx") + ends("gy") + ends("gz")
    packs, y_low, y_high = neighbours(y_pack(sums, por, perm, below, above), "gy")
    gz = lax.axis_index("gz")
    places = [y_low, y_high, jnp.maximum(gz - 1, 0), jnp.minimum(gz + 1, lax.axis_size("gz") - 1)]
    where = jnp.stack([jnp.asarray(v, i32) for v in places + has + [gz]])
    levels = lax.all_gather(z_pack(where, sums, perm, below, above, packs), "gz", axis=0)
    star, inner, reduced = local_solve(where, sums, por, perm, below, above, packs, levels)
    velocity, pressure = final(where, star, inner, lax.all_gather(reduced, "gz", axis=0))
    return (
        velocity.reshape(3, LEVELS, ROWS, COLS),
        pressure.reshape(LEVELS, ROWS, COLS),
    )


def solution(mesh):
    points = ("gx", "gy", "gz")
    cells = P("gz", "gx", "gy")
    placed = (
        P(None, points), P(points), P(points), P(None, points), P(points), P(points), P(points),
        P(*points), cells, cells,
    )
    return jax.shard_map(
        shards,
        mesh=mesh,
        in_specs=placed,
        out_specs=(P(None, *cells), cells),
        check_vma=False,
    )
```

time: 275 us -> 57.1 us (0.21)
  other arithmetic: 175 us -> 0 us
  starting transfers between devices: 40.9 us -> 6.21 us
  waiting for transfers between devices: 31.7 us -> 5.46 us
  Pallas kernels: 0 us -> 23.9 us
  local copies, waits for them, and re-layouts: 16.1 us -> 1.89 us
  blocking collectives: 6.89 us -> 17.9 us
    scatter-add x1 -> x0, other arithmetic: 135 us -> none  [point_sums(): jax.ops.segment_sum(component, cell_index, num_segments=segments)]
    ppermute x18 -> x2, starting transfers between devices: 40.9 us -> 6.21 us  [the longest x1 4.92 us: shift_up(): return lax.ppermute(block, axis, [(i, i + 1) for i in range(count - 1)])]
    slice x7 -> x0, other arithmetic: 28.6 us -> none  [the longest x1 28.1 us: brick_velocity(): cell_sums[6] + time_step * force_x]
    ppermute x18 -> x2, waiting for transfers between devices: 31.7 us -> 5.46 us  [the longest x1 4.01 us: shift_down(): return lax.ppermute(block, axis, [(i + 1, i) for i in range(count - 1)])]
    pallas_call x0 -> x5, Pallas kernels: none -> 23.9 us  [the longest x1 15.3 us: scatter(): pl.pallas_call(functools.partial(scatter_kernel, chunk), grid=(points //...]
    all_gather x1 -> x3, blocking collectives: 6.89 us -> 17.9 us  [the longest x1 6.17 us: neighbours(): stacked = lax.all_gather(block, axis, axis=0)]
    slice x41 -> x0, local copies, waits for them, and re-layouts: 7.63 us -> none  [the longest x1 5.3 us: shards(): outgoing = jnp.concatenate([cell_sums[:6], permeability[None]], axis=0)]
    concatenate x4 -> x0, local copies, waits for them, and re-layouts: 6.99 us -> none  [the longest x1 6.96 us: point_sums(): jnp.concatenate([stress * weight, point_velocity * weight, weight[None]],...]
  transfers between devices with their start and end apart: 18 -> 2, of which waited for: 12 -> 2; matrix products, arithmetic and copies ran while one was open for 11% -> 1% of each run, Pallas kernels for 0% -> 0%
where the time goes in v2:
time: 57.1 us; the launch traced here: 56.8 us
  Pallas kernels  23.9 us (42%)
  blocking collectives  17.9 us (31%)
  starting transfers between devices  6.21 us (11%)
  waiting for transfers between devices  5.46 us (10%)
  local copies, waits for them, and re-layouts  1.89 us (3%)
  between operations  1.37 us (2%)
    pallas_call x1, Pallas kernels, scatter(): pl.pallas_call(functools.partial(scatter_kernel, chunk), grid=(points //...  15.3 us
    all_gather x1, blocking collectives, neighbours(): stacked = lax.all_gather(block, axis, axis=0)  6.17 us
    all_gather x1, blocking collectives, shards(): lax.all_gather(z_pack(where, sums, perm, below, above, packs), 'gz', axis=0)  6.02 us
    all_gather x1, blocking collectives, shards(): lax.all_gather(reduced, 'gz', axis=0)  5.7 us
    ppermute x1, starting transfers between devices, shift_up(): return lax.ppermute(block, axis, [(i, i + 1) for i in range(count - 1)])  4.92 us
    ppermute x1, waiting for transfers between devices, shift_down(): return lax.ppermute(block, axis, [(i + 1, i) for i in range(count - 1)])  4.01 us
    pallas_call x1, Pallas kernels, local_solve(): pl.pallas_call(local_kernel, in_specs=[smem] + [vmem] * 7, out_shape=[jax...  3.17 us
    pallas_call x1, Pallas kernels, y_pack(): pl.pallas_call(y_pack_kernel, out_shape=jax.ShapeDtypeStruct((CELLS, COLS...  2.21 us
  transfers between devices with their start and end apart: 2, of which 2 were waited for; matrix products, arithmetic and copies ran while one was open for 1% of the time, Pallas kernels for 0%

profile of v2, /device:TPU:0, one launch (start us, length us, event | category | flops | bytes accessed | tf_op | source)
XLA Modules:
  0.0 56.8 jit_solution(2240532779931924948)
XLA Ops:
  1.3 15.3 %point_sums.1 = (f32[10,128,128]{2,1,0:T(8,128)}, f32[18,16,128]{2,1,0:T(8,128)}, f32[18,16,128]{2,1,0:T(8,128)}) custom-call(s32[1]{0:T(128)} %bitcast.24.count, f32[6,24576]{1,0:T(8,128)} %trial.1, f32[1,24576]{1,0:T(1,128)} %bitcast.38, f32[1,24576]{1,0:T(1,128)} %bitcast.39, f32[3,24576]{1,0:T(4,128)} %vel.1, f32[1,24576]{1,0:T(1,128)} %bitcast.40, ...), custom_call_target="tpu_custom_call" | custom-call | flops 12079595520 | bytes 1572864 | tf_op jit(solution)/shard_map/point_sums/pallas_call | solution.py:136
  16.6 4.9 %collective-permute-start = (f32[18,16,128]{2,1,0:T(8,128)}, f32[18,16,128]{2,1,0:T(8,128)S(1)}, u32[]{:S(2)}, u32[]{:S(2)}) collective-permute-start(f32[18,16,128]{2,1,0:T(8,128)} %get-tuple-element.11), channel_id=1, source_target_pairs={{0,8},{8,16},{16,24},{1,9},{9,17},{17,25},{2,10},{10,18},{18,26},{... | collective-permute-start | bytes 442376 | tf_op jit(solution)/shard_map/ppermute | solution.py:583
  21.5 1.3 %collective-permute-start.1 = (f32[18,16,128]{2,1,0:T(8,128)}, f32[18,16,128]{2,1,0:T(8,128)S(1)}, u32[]{:S(2)}, u32[]{:S(2)}) collective-permute-start(f32[18,16,128]{2,1,0:T(8,128)} %get-tuple-element.12), channel_id=1, source_target_pairs={{8,0},{16,8},{24,16},{9,1},{17,9},{25,17},{10,2},{18,10},{26,18},{... | collective-permute-start | bytes 442376 | tf_op jit(solution)/shard_map/ppermute | solution.py:588
  22.8 0.6 %stack.71.where = s32[11]{0:T(128)} concatenate(s32[1]{0:T(128)} %bitcast, s32[1]{0:T(128)} %bitcast.1, s32[1]{0:T(128)} %bitcast.2, s32[1]{0:T(128)} %bitcast.3, s32[1]{0:T(128)} %bitcast.4, s32[1]{0:T(128)} %bitcast.5, s32[1]{0:T(128)} %bitcast.6, s32[1]{0:T(128)} %bitcast.7, s32[1]{0:T(128)} %bitcast.8, s32[1]{0:T(128)} %bitcast.9, s32[1]{0:T(128)} %bitcast.10), dimensions={0} | concatenate | bytes 88 | tf_op jit(solution)/shard_map/stack | solution.py:614
  23.4 1.4 %collective-permute-done.below = f32[18,16,128]{2,1,0:T(8,128)S(1)} collective-permute-done((f32[18,16,128]{2,1,0:T(8,128)}, f32[18,16,128]{2,1,0:T(8,128)S(1)}, u32[]{:S(2)}, u32[]{:S(2)}) %collective-permute-start) | collective-permute-done | bytes 147488 | tf_op jit(solution)/shard_map/ppermute | solution.py:583
  24.9 0.0 copy-start.1
  24.9 4.0 %collective-permute-done.1.above = f32[18,16,128]{2,1,0:T(8,128)S(1)} collective-permute-done((f32[18,16,128]{2,1,0:T(8,128)}, f32[18,16,128]{2,1,0:T(8,128)S(1)}, u32[]{:S(2)}, u32[]{:S(2)}) %collective-permute-start.1) | collective-permute-done | bytes 147488 | tf_op jit(solution)/shard_map/ppermute | solution.py:588
  28.9 0.0 copy-start.3
  28.9 0.0 copy-done.1
  28.9 0.7 %copy-done.3 = f32[18,16,128]{2,1,0:T(8,128)} copy-done((f32[18,16,128]{2,1,0:T(8,128)}, f32[18,16,128]{2,1,0:T(8,128)S(1)}, u32[]{:S(2)}) %copy-start.3) | copy-done | bytes 147480
  29.6 2.2 %y_pack.1 = f32[128,128]{1,0:T(8,128)} custom-call(f32[10,128,128]{2,1,0:T(8,128)} %get-tuple-element.10.sums.first.last, f32[128,128]{1,0:T(8,128)} %bitcast.35, f32[128,128]{1,0:T(8,128)} %bitcast.28, f32[18,16,128]{2,1,0:T(8,128)} %copy-done.1, f32[18,16,128]{2,1,0:T(8,128)} %copy-done.3), custom_call_target="tpu_custom_call" | custom-call | tf_op jit(solution)/shard_map/y_pack/pallas_call | solution.py:175
  31.8 6.2 %all-gather = f32[256,128]{1,0:T(8,128)} all-gather(f32[128,128]{1,0:T(8,128)} %y_pack.1), channel_id=2, replica_groups=mesh['gx'=4,'gy'=2,'gz'=4] {'gy'}, dimensions={0}, use_global_device_ids=true | all-gather | bytes 196608 | tf_op jit(solution)/shard_map/all_gather | solution.py:595
  38.0 1.8 %z_pack.1 = f32[112,128]{1,0:T(8,128)} custom-call(s32[11]{0:T(128)} %stack.71.where, f32[10,128,128]{2,1,0:T(8,128)} %get-tuple-element.10.sums.first.last, f32[10,128,128]{2,1,0:T(8,128)} %get-tuple-element.10.sums.first.last, f32[128,128]{1,0:T(8,128)} %bitcast.29, f32[128,128]{1,0:T(8,128)} %bitcast.30, f32[18,16,128]{2,1,0:T(8,128)} %copy-done.1, ...), custom_call_target="tpu_custom_call" | custom-call | tf_op jit(solution)/shard_map/z_pack/pallas_call | solution.py:224
  39.7 6.0 %all-gather.1 = f32[448,128]{1,0:T(8,128)S(1)} all-gather(f32[112,128]{1,0:T(8,128)} %z_pack.1), channel_id=3, replica_groups=mesh['gx'=4,'gy'=2,'gz'=4] {'gz'}, dimensions={0}, use_global_device_ids=true | all-gather | bytes 286720 | tf_op jit(solution)/shard_map/all_gather | solution.py:615
  45.7 0.0 copy-done
  45.7 0.0 copy-done.4
  45.8 0.0 copy-done.6
  45.8 0.0 copy-done.7
  45.8 0.0 copy-done.2
  45.8 0.0 copy-done.5
  45.8 0.6 %copy-done.8 = s32[11]{0:T(128)S(1)} copy-done((s32[11]{0:T(128)S(1)}, s32[11]{0:T(128)}, u32[]{:S(2)}) %copy-start.8) | copy-done | bytes 68
  46.4 3.2 %local_solve.1 = (f32[3,128,128]{2,1,0:T(8,128)S(1)}, f32[3,3,14,8,128]{4,3,2,1,0:T(8,128)S(1)}, f32[112,128]{1,0:T(8,128)S(1)}) custom-call(s32[11]{0:T(128)S(1)} %copy-done.8, f32[10,128,128]{2,1,0:T(8,128)S(1)} %copy-done, f32[128,128]{1,0:T(8,128)S(1)} %bitcast.36, f32[128,128]{1,0:T(8,128)S(1)} %bitcast.31, f32[18,16,128]{2,1,0:T(8,128)S(1)} %copy-done.2, ...), custom_call_target="tpu_custom_call" | custom-call | tf_op jit(solution)/shard_map/local_solve/pallas_call | solution.py:466
  49.5 5.7 %all-gather.2 = f32[448,128]{1,0:T(8,128)S(1)} all-gather(f32[112,128]{1,0:T(8,128)S(1)} %get-tuple-element.15), channel_id=4, replica_groups=mesh['gx'=4,'gy'=2,'gz'=4] {'gz'}, dimensions={0}, use_global_device_ids=true | all-gather | bytes 286720 | tf_op jit(solution)/shard_map/all_gather | solution.py:617
  55.2 1.5 %final.1 = (f32[3,128,128]{2,1,0:T(8,128)}, f32[128,128]{1,0:T(8,128)}) custom-call(s32[11]{0:T(128)S(1)} %copy-done.8, f32[3,128,128]{2,1,0:T(8,128)S(1)} %get-tuple-element.13.vel, f32[3,3,14,8,128]{4,3,2,1,0:T(8,128)S(1)} %get-tuple-element.14.inner, f32[4,112,128]{2,1,0:T(8,128)S(1)} %bitcast.32), custom_call_target="tpu_custom_call" | custom-call | tf_op jit(solution)/shard_map/final/pallas_call | solution.py:569
  (7 shorter events, 0.0 us)
Async XLA Ops:
  16.6 8.3 %collective-permute-start = (f32[18,16,128]{2,1,0:T(8,128)}, f32[18,16,128]{2,1,0:T(8,128)S(1)}, u32[]{:S(2)}, u32[]{:S(2)}) collective-permute-start(f32[18,16,128]{2,1,0:T(8,128)} %get-tuple-element.11), channel_id=1, source_target_pairs={{0,8},{8,16},{16,24},{1,9},{9,17},{17,25},{2,10},{10,18},{18,26},{... | collective-permute-start | bytes 442376 | tf_op jit(solution)/shard_map/ppermute | solution.py:583
  21.5 7.4 %collective-permute-start.1 = (f32[18,16,128]{2,1,0:T(8,128)}, f32[18,16,128]{2,1,0:T(8,128)S(1)}, u32[]{:S(2)}, u32[]{:S(2)}) collective-permute-start(f32[18,16,128]{2,1,0:T(8,128)} %get-tuple-element.12), channel_id=1, source_target_pairs={{8,0},{16,8},{24,16},{9,1},{17,9},{25,17},{10,2},{18,10},{26,18},{... | collective-permute-start | bytes 442376 | tf_op jit(solution)/shard_map/ppermute | solution.py:588
  24.9 4.0 %copy-start.1 = (f32[18,16,128]{2,1,0:T(8,128)}, f32[18,16,128]{2,1,0:T(8,128)S(1)}, u32[]{:S(2)}) copy-start(f32[18,16,128]{2,1,0:T(8,128)S(1)} %collective-permute-done.below) | copy-start | bytes 442372
  28.9 0.7 %copy-start.3 = (f32[18,16,128]{2,1,0:T(8,128)}, f32[18,16,128]{2,1,0:T(8,128)S(1)}, u32[]{:S(2)}) copy-start(f32[18,16,128]{2,1,0:T(8,128)S(1)} %collective-permute-done.1.above) | copy-start | bytes 442372
  37.9 7.8 %copy-start = (f32[10,128,128]{2,1,0:T(8,128)S(1)}, f32[10,128,128]{2,1,0:T(8,128)}, u32[]{:S(2)}) copy-start(f32[10,128,128]{2,1,0:T(8,128)} %get-tuple-element.10.sums.first.last) | copy-start | bytes 1966084
  37.9 7.8 %copy-start.4 = (f32[18,16,128]{2,1,0:T(8,128)S(1)}, f32[18,16,128]{2,1,0:T(8,128)}, u32[]{:S(2)}) copy-start(f32[18,16,128]{2,1,0:T(8,128)} %copy-done.3) | copy-start | bytes 442372
  37.9 7.8 %copy-start.6 = (f32[16,8,128]{2,1,0:T(8,128)S(1)}, f32[16,8,128]{2,1,0:T(8,128)}, u32[]{:S(2)}) copy-start(f32[16,8,128]{2,1,0:T(8,128)} %param.19) | copy-start | bytes 196612
  38.0 7.8 %copy-start.7 = (f32[16,8,128]{2,1,0:T(8,128)S(1)}, f32[16,8,128]{2,1,0:T(8,128)}, u32[]{:S(2)}) copy-start(f32[16,8,128]{2,1,0:T(8,128)} %param.18) | copy-start | bytes 196612
  39.7 6.1 %copy-start.2 = (f32[18,16,128]{2,1,0:T(8,128)S(1)}, f32[18,16,128]{2,1,0:T(8,128)}, u32[]{:S(2)}) copy-start(f32[18,16,128]{2,1,0:T(8,128)} %copy-done.1) | copy-start | bytes 442372
  39.7 6.1 %copy-start.5 = (f32[256,128]{1,0:T(8,128)S(1)}, f32[256,128]{1,0:T(8,128)}, u32[]{:S(2)}) copy-start(f32[256,128]{1,0:T(8,128)} %all-gather) | copy-start | bytes 393220
  45.7 0.6 %copy-start.8 = (s32[11]{0:T(128)S(1)}, s32[11]{0:T(128)}, u32[]{:S(2)}) copy-start(s32[11]{0:T(128)} %stack.71.where) | copy-start | bytes 136

commit v3 on v2

v3 whole, which is shorter than its diff:
```python
import functools

import jax
import jax.numpy as jnp
from jax import lax
from jax.experimental import pallas as pl
from jax.experimental.pallas import tpu as pltpu
from jax.sharding import PartitionSpec as P

bf = jnp.bfloat16
f8 = jnp.float8_e4m3fn
f32 = jnp.float32
i32 = jnp.int32

LEVELS, ROWS, COLS = 16, 8, 128
CELLS = LEVELS * ROWS

ZX, YZ, ZZ, XX, YY, XY, MX, MY, MZ, MASS, POR, PERM = range(12)
FIELDS = 12
STRESS_ORDER = (5, 4, 2, 0, 1, 3)

X_ROWS = (
    (ZX, 0), (ZX, 1), (YZ, 0), (ZZ, 0), (PERM, 0), (POR, 0),
    (XX, 0), (XX, 1), (XX, 2), (XY, 0), (XY, 1), (YY, 0),
    (MX, 0), (MX, 1), (MY, 0), (MZ, 0), (MASS, 0), (MASS, 1),
)
Y_DEPTH = {ZX: 1, YZ: 2, ZZ: 1, XX: 1, YY: 3, XY: 2, MX: 1, MY: 2, MZ: 1, MASS: 2, POR: 1, PERM: 1}
Y_PLACE = {}
_at = 0
for _f in range(FIELDS):
    Y_PLACE[_f] = _at + Y_DEPTH[_f]
    _at += 2 * Y_DEPTH[_f]
HALF = 64
FACE, MAIN, NEAR, FAR, RIGHT, SOURCE, ECHO, VELZ, STRESSZ = range(9)
WEIGHT, SHEARX, SHEARY = range(3)
NARROW, WIDE = 18, 6
MSG_X = 8 * (NARROW + WIDE)
MSG_X_WIDE = MSG_X + 8 * -(-NARROW // 4)
MSG_Y = MSG_X_WIDE + 8 * -(-WIDE // 2)
MSG_ROWS = MSG_Y + 8
LANE_WIDE = 2 * NARROW
LANE_CORNER = LANE_WIDE + 4 * WIDE


def tile_iota(dim):
    return lax.broadcasted_iota(i32, (ROWS, COLS), dim)


def turn(tile, shift, axis):
    shift %= tile.shape[axis]
    return tile if shift == 0 else pltpu.roll(tile, shift, axis)


def row_stress(trial, mean, cons, flag):
    part = lax.broadcasted_iota(i32, trial.shape, 0)
    size = jnp.sqrt(
        jnp.sum(trial * trial * jnp.where(part < 3, 1.5, 3.0), axis=0, keepdims=True)
    )
    yield_size = 1.2 * jnp.sqrt(mean * (cons - mean))
    factor = jnp.where(flag == 1, yield_size / jnp.maximum(size, 1.0), 1.0)
    return trial * factor - jnp.where(part < 3, mean, 0.0)


def scatter_kernel(
    chunk, count, trial, mean, cons, vel, wt, cell, flag, por, perm, out, low, high, acc
):
    step = pl.program_id(0)
    slot = step * chunk + lax.broadcasted_iota(i32, (1, chunk), 1)
    weight = jnp.where(slot < count[0], wt[...], 0.0)
    stress = row_stress(trial[...], mean[...], cons[...], flag[...]) * weight
    momentum = vel[...] * weight
    place = cell[...]
    hi = (place >> 7) & 63
    lo = ((place >> 13) << 7) | (place & 127)

    def spread(row, count, kind):
        return jnp.broadcast_to(row, (count, chunk)).astype(kind)

    one, zero = jnp.array(1, bf), jnp.array(0, bf)
    base = lax.broadcasted_iota(i32, (16, chunk), 0)

    def equal(index, count):
        index = spread(index.astype(f32), 16, bf)
        return [(base + b * 16).astype(f32).astype(bf) == index for b in range(count // 16)]

    hi_mask = equal(hi, 64)
    right = jnp.concatenate([jnp.where(m, one, zero) for m in equal(lo, 256)], axis=0)
    base32 = lax.broadcasted_iota(i32, (32, chunk), 0)
    hi_mask8 = [base32 + 32 * b == jnp.broadcast_to(hi, (32, chunk)) for b in range(2)]
    zero8 = jnp.zeros((32, chunk), f8)
    rows = [stress[i : i + 1] for i in STRESS_ORDER]
    rows += [momentum[i : i + 1] for i in range(3)] + [weight]
    left, left8 = [], []
    for row in rows:
        top = row.astype(bf).astype(f32)
        part = spread(top, 16, bf)
        left += [jnp.where(m, part, zero) for m in hi_mask]
        part = spread((row - top) * 256.0, 32, f8)
        left8 += [jnp.where(m, part, zero8) for m in hi_mask8]
    left = jnp.concatenate(left, axis=0)
    left8 = jnp.concatenate(left8, axis=0)
    dims = (((1,), (1,)), ((), ()))
    prod = lax.dot_general(left, right, dims, preferred_element_type=f32)
    prod8 = lax.dot_general(left8, right.astype(f8), dims, preferred_element_type=f32)
    prod = prod + prod8 * (1 / 256.0)

    @pl.when(step == 0)
    def _():
        acc[...] = prod

    @pl.when(step > 0)
    def _():
        acc[...] += prod

    @pl.when(step == pl.num_programs(0) - 1)
    def _():
        for i in range(10):
            out[i, 0:64, :] = acc[i * 64 : i * 64 + 64, :COLS]
            out[i, 64:128, :] = acc[i * 64 : i * 64 + 64, COLS:]
        for q, (field, depth) in enumerate(X_ROWS):
            for face, row in ((low, depth), (high, ROWS - 1 - depth)):
                rows = pl.ds(row, LEVELS, stride=ROWS)
                if field < 10:
                    face[q] = out[field, rows, :]
                else:
                    face[q] = (por if field == POR else perm)[rows, :]


def scatter(trial, mean, cons, vel, wt, cell, flag, count, por, perm):
    points = mean.shape[0]
    chunk = 8192 if points % 8192 == 0 else points
    row = lambda v: v.reshape(1, points)
    spec = lambda r: pl.BlockSpec((r, chunk), lambda i: (0, i))
    fixed = lambda *shape: pl.BlockSpec(shape, lambda i: (0,) * len(shape))
    faces = (len(X_ROWS), LEVELS, COLS)
    return pl.pallas_call(
        functools.partial(scatter_kernel, chunk),
        grid=(points // chunk,),
        in_specs=[pl.BlockSpec(memory_space=pltpu.SMEM)]
        + [spec(r) for r in (6, 1, 1, 3, 1, 1, 1)]
        + [fixed(CELLS, COLS)] * 2,
        out_specs=[fixed(10, CELLS, COLS), fixed(*faces), fixed(*faces)],
        out_shape=[
            jax.ShapeDtypeStruct((10, CELLS, COLS), f32),
            jax.ShapeDtypeStruct(faces, f32),
            jax.ShapeDtypeStruct(faces, f32),
        ],
        scratch_shapes=[pltpu.VMEM((640, 256), f32)],
        compiler_params=pltpu.CompilerParams(vmem_limit_bytes=60 << 20),
        cost_estimate=pl.CostEstimate(
            flops=2 * 960 * 256 * points, bytes_accessed=64 * points, transcendentals=0
        ),
        name="point_sums",
    )(count.reshape(1), trial, row(mean), row(cons), vel, row(wt), row(cell), row(flag), por, perm)


def y_own_kernel(sums, por, perm, out):
    lane = lax.broadcasted_iota(i32, (CELLS, COLS), 1)
    packed = jnp.zeros((CELLS, COLS), f32)
    for field in range(FIELDS):
        at, depth = Y_PLACE[field], Y_DEPTH[field]
        own = sums[field] if field < 10 else (por if field == POR else perm)[...]
        packed = jnp.where((lane >= at - depth) & (lane < at + depth), turn(own, at, 1), packed)
    out[...] = packed


def y_own(sums, por, perm):
    return pl.pallas_call(
        y_own_kernel,
        out_shape=jax.ShapeDtypeStruct((CELLS, COLS), f32),
        cost_estimate=pl.CostEstimate(flops=4000000, bytes_accessed=900000, transcendentals=0),
        name="y_own",
    )(sums, por, perm)


def y_pack_kernel(own, below, above, out):
    lane = lax.broadcasted_iota(i32, (CELLS, COLS), 1)
    lane16 = lax.broadcasted_iota(i32, (LEVELS, COLS), 1)
    slots = [jnp.zeros((LEVELS, COLS), f32)] * ROWS
    for q, (field, deep) in enumerate(X_ROWS):
        at, depth = Y_PLACE[field] + HALF, Y_DEPTH[field]
        mask = (lane16 >= at - depth) & (lane16 < at + depth)
        for source, slot in ((above, deep), (below, ROWS - 1 - deep)):
            slots[slot] = jnp.where(mask, turn(source[q], at, 1), slots[slot])
    out[...] = jnp.where(lane < HALF, own[...], jnp.concatenate(slots, axis=0))


def y_pack(own, below, above):
    return pl.pallas_call(
        y_pack_kernel,
        out_shape=jax.ShapeDtypeStruct((CELLS, COLS), f32),
        name="y_pack",
    )(own, below, above)


def y_from_above(shape):
    lane = lax.broadcasted_iota(i32, shape, 1) & (HALF - 1)
    mask = lane < 0
    for field in range(FIELDS):
        at = Y_PLACE[field]
        mask |= (lane >= at) & (lane < at + Y_DEPTH[field])
    return mask


Y_LOW, Y_HIGH, X_HAS_LOW, X_HAS_HIGH, Y_HAS_LOW, Y_HAS_HIGH, LAYER = range(7)


def met(where, packs, from_above, rows):
    low = packs[where[Y_LOW], rows, :] * where[Y_HAS_LOW].astype(f32)
    high = packs[where[Y_HIGH], rows, :] * where[Y_HAS_HIGH].astype(f32)
    return jnp.where(from_above, high, low)


def diff_x(own, rim):
    row = tile_iota(0)
    own_up, rim_up = turn(own, -1, 0), turn(rim, -1, 0)
    own_down, rim_down = turn(own, 1, 0), turn(rim, 1, 0)
    top, bottom = row == ROWS - 1, row == 0
    return (
        jnp.where(top, rim_up, own_up) - jnp.where(bottom, rim_down, own_down),
        jnp.where(top, own_up, rim_up) - jnp.where(bottom, own_down, rim_down),
    )


def diff_y(own, rim):
    lane = tile_iota(1)
    own_up, rim_up = turn(own, -1, 1), turn(rim, -1, 1)
    own_down, rim_down = turn(own, 1, 1), turn(rim, 1, 1)
    top, bottom = lane == COLS - 1, lane == 0
    return (
        jnp.where(top, rim_up, own_up) - jnp.where(bottom, rim_down, own_down),
        jnp.where(top, own_up, rim_up) - jnp.where(bottom, own_down, rim_down),
    )


def ext_x(t):
    a0, a1 = diff_x(t[0], t[1])
    b0, b1 = diff_x(t[2], t[3])
    return [a0, a1, b0, b1]


def ext_y(t):
    a0, a2 = diff_y(t[0], t[2])
    b1, b3 = diff_y(t[1], t[3])
    return [a0, b1, a2, b3]


def rim_masks(where):
    row, lane = tile_iota(0), tile_iota(1)
    has = lambda low, high, test: jnp.where(test, where[high], where[low]) == 1
    in_x = has(X_HAS_LOW, X_HAS_HIGH, row < 4)
    in_y = has(Y_HAS_LOW, Y_HAS_HIGH, lane < HALF)
    return in_x, in_y, in_x & in_y


def local_kernel(where, sums, por, perm, below, above, packs, vel, inner, out, rim, corner):
    rim[...] = jnp.zeros_like(rim)
    for q, (field, deep) in enumerate(X_ROWS):
        rim[field, pl.ds(deep, LEVELS, stride=ROWS), :] = above[q]
        rim[field, pl.ds(ROWS - 1 - deep, LEVELS, stride=ROWS), :] = below[q]
    from_above = y_from_above((LEVELS, COLS))
    for slot in range(ROWS):
        rows = pl.ds(slot * LEVELS, LEVELS)
        corner[pl.ds(slot, LEVELS, stride=ROWS), :] = met(where, packs, from_above, rows)
    from_above = y_from_above((ROWS, COLS))
    in_x, in_y, in_xy = rim_masks(where)
    in_rims = (in_x, in_y, in_xy)
    inside = lambda t: t[:1] + [jnp.where(m, v, 0.0) for m, v in zip(in_rims, t[1:])]
    zero = jnp.zeros((ROWS, COLS), f32)

    def field_at(field, level):
        rows = pl.ds(level * ROWS, ROWS)
        at = Y_PLACE[field]
        own = sums[field, rows, :] if field < 10 else (por if field == POR else perm)[rows, :]
        lanes = met(where, packs, from_above, rows)
        return [
            own,
            rim[field, rows, :],
            turn(lanes, -at, 1),
            turn(corner[rows, :], -at - HALF, 1),
        ]

    memo = {}

    def get(field, level):
        if not 0 <= level < LEVELS:
            return [zero] * 4
        if (field, level) not in memo:
            memo[field, level] = field_at(field, level)
        return memo[field, level]

    def star(level):
        weight = inside([0.125 / jnp.maximum(m, 0.5) for m in get(MASS, level)])
        dz = lambda f: [u - d for u, d in zip(get(f, level + 1), get(f, level - 1))]
        forces = (
            (ext_x(get(XX, level)), ext_y(get(XY, level)), dz(ZX)),
            (ext_x(get(XY, level)), ext_y(get(YY, level)), dz(YZ)),
            (ext_x(get(ZX, level)), ext_y(get(YZ, level)), dz(ZZ)),
        )
        found = []
        for field, (fx, fy, fz) in zip((MX, MY, MZ), forces):
            found.append(
                [
                    (8.0 * m + (fx[n] + fy[n] + fz[n])) * weight[n]
                    for n, m in enumerate(get(field, level))
                ]
            )
        return found, weight

    def level_perm(level):
        own, x, y, _ = get(PERM, level)
        return [own] + [jnp.where(t > 0.0, t, 1.0) for t in (x, y)]

    def faces(level):
        pairs = zip(level_perm(level), level_perm(level + 1))
        return [0.5 * a * b / (a + b) for a, b in pairs]

    zero3 = [zero] * 3
    stars, weights = {}, {}
    stars[0], weights[0] = star(0)
    first_star = stars[0][2]
    wide = {0: [weights[0], get(ZX, 0), get(YZ, 0)]}
    stress = {0: get(ZZ, 0)}
    down = zero3
    kept, terms, sources, links = [], {}, {}, {}
    for level in range(LEVELS):
        if level + 1 < LEVELS:
            stars[level + 1], weights[level + 1] = star(level + 1)
        vx, vy, vz = stars[level]
        for n, part in enumerate((vx, vy, vz)):
            vel[n, pl.ds(level * ROWS, ROWS), :] = part[0]
        z_up = stars[level + 1][2] if level + 1 < LEVELS else zero3
        z_down = stars[level - 1][2] if level > 0 else zero3
        if level == LEVELS - 1:
            wide[1] = [weights[level], get(ZX, level), get(YZ, level)]
            stress[1] = get(ZZ, level)
        dx, dy = ext_x(vx), ext_y(vy)
        porosity = get(POR, level)[:3]
        up = faces(level) if level + 1 < LEVELS else zero3
        now = []
        for n in range(3):
            source = -0.0015 * (1.0 - porosity[n])
            right = source * (dx[n] + dy[n] + (z_up[n] - z_down[n]))
            main = 0.002 * porosity[n] + (down[n] + up[n])
            now.append((-down[n], main, -up[n], right, source))
        sources[level], links[level] = [t[4] for t in now], up
        down = up
        if level in (0, LEVELS - 1):
            terms[level] = now
        elif level == 1:
            kept.append([(lo, 1.0 / mid, hi, r) for lo, mid, hi, r, _ in now])
        else:
            rows = []
            for (lo, mid, hi, r, _), (f, inv, u, pr) in zip(now, kept[-1]):
                w = lo * inv
                rows.append((-w * f, 1.0 / (mid - w * u), hi, r - w * pr))
            kept.append(rows)
        for key in [k for k in memo if k[1] < level]:
            del memo[key]
    after = last_inner = None
    for n_row in range(len(kept) - 1, -1, -1):
        rows = []
        for t in range(3):
            f, inv, u, r = kept[n_row][t]
            if after is None:
                rows.append((r * inv, -f * inv, -u * inv))
            else:
                b2, f2, g2 = after[t]
                rows.append(((r - u * b2) * inv, -(f + u * f2) * inv, -u * g2 * inv))
            for m in range(3):
                inner[t, m, n_row] = rows[t][m]
        last_inner = last_inner or rows
        after = rows
    first_inner = after
    top = LEVELS - 1
    narrow = []
    for t in range(3):
        _, mid, hi, r, source = terms[0][t]
        b, f, g = first_inner[t]
        echo = sources[1][t] * weights[0][t] / links[0][t]
        face = level_perm(0)[t]
        mine = [face, mid + hi * f, hi * f, hi * g, r - hi * b, source, echo, first_star[t], stress[0][t]]
        lo, mid, _, r, source = terms[top][t]
        b, f, g = last_inner[t]
        echo = sources[top - 1][t] * weights[top][t] / links[top - 1][t]
        face = level_perm(top)[t]
        mine += [face, mid + lo * g, lo * g, lo * f, r - lo * b, source, echo, stars[top][2][t], stress[1][t]]
        narrow.append(mine)
    row, lane = tile_iota(0), tile_iota(1)
    x_parts = [zero] * -(-NARROW // 4)
    x_wide = [zero] * -(-WIDE // 2)
    y_part = zero

    def between(index, at, count):
        return (index >= at) & (index < at + count)

    for q in range(NARROW):
        own, x, y = (narrow[t][q] for t in range(3))
        out[8 * q : 8 * q + 8, :] = own
        at = 2 * q % 8
        x_parts[q // 4] = jnp.where(between(row, at, 2), turn(x, at + 1, 0), x_parts[q // 4])
        y_part = jnp.where(between(lane, 2 * q, 2), turn(y, 2 * q + 1, 1), y_part)
    for m, (own, x, y, xy) in enumerate(wide[0] + wide[1]):
        at = 8 * (NARROW + m)
        out[at : at + 8, :] = own
        at = 4 * (m % 2)
        x_wide[m // 2] = jnp.where(between(row, at, 4), turn(x, at + 2, 0), x_wide[m // 2])
        at = LANE_WIDE + 4 * m
        y_part = jnp.where(between(lane, at, 4), turn(y, at + 2, 1), y_part)
        at = LANE_CORNER + 2 * m
        y_part = jnp.where(between(lane, at, 2), turn(xy, at + 1, 1), y_part)
    for n, part in enumerate(x_parts):
        out[MSG_X + 8 * n : MSG_X + 8 * n + 8, :] = part
    for n, part in enumerate(x_wide):
        out[MSG_X_WIDE + 8 * n : MSG_X_WIDE + 8 * n + 8, :] = part
    out[MSG_Y : MSG_Y + 8, :] = y_part


def local_solve(where, sums, por, perm, below, above, packs):
    smem = pl.BlockSpec(memory_space=pltpu.SMEM)
    vmem = pl.BlockSpec(memory_space=pltpu.VMEM)
    return pl.pallas_call(
        local_kernel,
        in_specs=[smem] + [vmem] * 6,
        out_shape=[
            jax.ShapeDtypeStruct((3, CELLS, COLS), f32),
            jax.ShapeDtypeStruct((3, 3, LEVELS - 2, ROWS, COLS), f32),
            jax.ShapeDtypeStruct((MSG_ROWS, COLS), f32),
        ],
        scratch_shapes=[pltpu.VMEM((FIELDS, CELLS, COLS), f32), pltpu.VMEM((CELLS, COLS), f32)],
        compiler_params=pltpu.CompilerParams(vmem_limit_bytes=32 << 20),
        name="local_solve",
    )(where, sums, por, perm, below, above, packs)


def final_kernel(layers, where, vel, inner, told, out, pressure):
    me = where[LAYER]
    zero = jnp.zeros((ROWS, COLS), f32)

    def narrow(k, side, what):
        q = 9 * side + what
        at = MSG_X + 8 * (q // 4)
        return [
            told[k, 8 * q : 8 * q + 8, :],
            turn(told[k, at : at + 8, :], -(2 * q % 8 + 1), 0),
            turn(told[k, MSG_Y : MSG_Y + 8, :], -(2 * q + 1), 1),
        ]

    def wide(k, side, what):
        m = 3 * side + what
        own = 8 * (NARROW + m)
        at = MSG_X_WIDE + 8 * (m // 2)
        lanes = told[k, MSG_Y : MSG_Y + 8, :]
        return [
            told[k, own : own + 8, :],
            turn(told[k, at : at + 8, :], -(4 * (m % 2) + 2), 0),
            turn(lanes, -(LANE_WIDE + 4 * m + 2), 1),
            turn(lanes, -(LANE_CORNER + 2 * m + 1), 1),
        ]

    def times(*factors):
        product = factors[0]
        for factor in factors[1:]:
            product = [a * b for a, b in zip(product, factor)]
        return product

    def plus(*terms):
        total = terms[0]
        for term in terms[1:]:
            total = [a + b for a, b in zip(total, term)]
        return total

    def minus(a, b):
        return [x - y for x, y in zip(a, b)]

    def half_face(a, b):
        return [0.5 * x * y / (x + y) for x, y in zip(a, b)]

    rows, gains, echoes = [], [], []
    for k in range(layers):
        gain, echo = [], []
        sides = []
        for side, other in ((0, k - 1), (1, k + 1)):
            right = narrow(k, side, RIGHT)
            main = narrow(k, side, MAIN)
            if 0 <= other < layers:
                weight = wide(k, side, WEIGHT)
                sign = -1.0 if side == 0 else 1.0
                weight = [sign * w for w in weight]
                stress = narrow(other, 1 - side, STRESSZ)
                vx = times(weight, wide(other, 1 - side, SHEARX))
                vy = times(weight, wide(other, 1 - side, SHEARY))
                vz = times(weight, stress)
                change = times(wide(other, 1 - side, WEIGHT), narrow(k, side, STRESSZ))
                beyond = minus(narrow(other, 1 - side, VELZ), [sign * c for c in change])
                spread = plus(ext_x(vx)[:3], ext_y(vy)[:3], [sign * v for v in beyond])
                right = plus(right, times(narrow(k, side, SOURCE), spread))
                link = half_face(narrow(k, side, FACE), narrow(other, 1 - side, FACE))
                main = plus(main, link)
                echo.append(times(narrow(k, side, ECHO), stress))
                gain.append((vx[0], vy[0], vz[0]))
            else:
                link = [zero] * 3
                if side == 1:
                    main = plus(main, [0.25 * v for v in narrow(k, side, FACE)])
                echo.append([zero] * 3)
                gain.append((zero, zero, zero))
            sides.append((link, main, right))
        for side, (link, main, right) in enumerate(sides):
            near, far = narrow(k, side, NEAR), narrow(k, side, FAR)
            right = minus(right, plus(times(near, echo[side]), times(far, echo[1 - side])))
            inv = [1.0 / m for m in main]
            link = [-v * i for v, i in zip(link, inv)]
            far, right = times(far, inv), times(right, inv)
            rows.append((link, far, right) if side == 0 else (far, link, right))
        gains.append(gain)
        echoes.append(echo)
    done = []
    for n, (lo, hi, r) in enumerate(rows):
        if n == 0:
            done.append((hi, r))
            continue
        hs, rs = done[-1]
        inv = [1.0 / (1.0 - l * h) for l, h in zip(lo, hs)]
        done.append((times(hi, inv), times(minus(r, times(lo, rs)), inv)))
    ends = [None] * len(rows)
    ends[-1] = done[-1][1]
    for n in range(len(rows) - 2, -1, -1):
        hs, rs = done[n]
        ends[n] = minus(rs, times(hs, ends[n + 1]))

    def mine(values):
        chosen = values[0]
        for k in range(1, layers):
            chosen = [jnp.where(me == k, v, c) for v, c in zip(values[k], chosen)]
        return chosen

    first, last = mine(ends[0::2]), mine(ends[1::2])
    under = mine([[zero]] + [e[:1] for e in ends[1:-1:2]])[0]
    over = mine([e[:1] for e in ends[2::2]] + [[zero]])[0]
    first_seen = plus(first, mine([e[0] for e in echoes]))
    last_seen = plus(last, mine([e[1] for e in echoes]))
    gain = {0: mine([g[0] for g in gains]), LEVELS - 1: mine([g[1] for g in gains])}
    in_x, in_y, _ = rim_masks(where)

    def press(level):
        if level < 0:
            return [under]
        if level >= LEVELS:
            return [over]
        if level == 0:
            parts = first
        elif level == LEVELS - 1:
            parts = last
        else:
            parts = [
                inner[t, 0, level - 1]
                + inner[t, 1, level - 1] * first_seen[t]
                + inner[t, 2, level - 1] * last_seen[t]
                for t in range(3)
            ]
        return [parts[0], jnp.where(in_x, parts[1], 0.0), jnp.where(in_y, parts[2], 0.0)]

    before, now = press(-1), press(0)
    for level in range(LEVELS):
        after = press(level + 1)
        rows_at = pl.ds(level * ROWS, ROWS)
        pressure[rows_at, :] = now[0]
        grads = (
            diff_x(now[0], now[1])[0],
            diff_y(now[0], now[2])[0],
            after[0] - before[0],
        )
        for n in range(3):
            value = vel[n, rows_at, :] - 0.125 * grads[n]
            out[n, rows_at, :] = value + gain[level][n] if level in gain else value
        before, now = now, after


def final(where, vel, inner, told):
    smem = pl.BlockSpec(memory_space=pltpu.SMEM)
    vmem = pl.BlockSpec(memory_space=pltpu.VMEM)
    return pl.pallas_call(
        functools.partial(final_kernel, told.shape[0]),
        in_specs=[smem] + [vmem] * 3,
        out_shape=[
            jax.ShapeDtypeStruct((3, CELLS, COLS), f32),
            jax.ShapeDtypeStruct((CELLS, COLS), f32),
        ],
        compiler_params=pltpu.CompilerParams(vmem_limit_bytes=32 << 20),
        name="final",
    )(where, vel, inner, told)


def shift_up(block, axis):
    count = lax.axis_size(axis)
    return lax.ppermute(block, axis, [(i, i + 1) for i in range(count - 1)])


def shift_down(block, axis):
    count = lax.axis_size(axis)
    return lax.ppermute(block, axis, [(i + 1, i) for i in range(count - 1)])


def neighbours(block, axis):
    count, me = lax.axis_size(axis), lax.axis_index(axis)
    if count > 4:
        return jnp.stack([shift_up(block, axis), shift_down(block, axis)]), 0, 1
    stacked = lax.all_gather(block, axis, axis=0)
    return stacked, jnp.maximum(me - 1, 0), jnp.minimum(me + 1, count - 1)


def shards(trial, mean, cons, vel, wt, cell, flag, count, por, perm):
    por = por.reshape(CELLS, COLS)
    perm = perm.reshape(CELLS, COLS)
    sums, low, high = scatter(trial, mean, cons, vel, wt, cell, flag, count, por, perm)
    above = shift_down(low, "gx")
    below = shift_up(high, "gx")

    def ends(axis):
        me = lax.axis_index(axis)
        return [(me > 0).astype(i32), (me < lax.axis_size(axis) - 1).astype(i32)]

    has = ends("gx") + ends("gy")
    own = y_own(sums, por, perm)
    packs, y_low, y_high = neighbours(y_pack(own, below, above), "gy")
    where = jnp.stack(
        [jnp.asarray(v, i32) for v in [y_low, y_high] + has + [lax.axis_index("gz")]]
    )
    star, inner, told = local_solve(where, sums, por, perm, below, above, packs)
    velocity, pressure = final(where, star, inner, lax.all_gather(told, "gz", axis=0))
    return (
        velocity.reshape(3, LEVELS, ROWS, COLS),
        pressure.reshape(LEVELS, ROWS, COLS),
    )


def solution(mesh):
    points = ("gx", "gy", "gz")
    cells = P("gz", "gx", "gy")
    placed = (
        P(None, points), P(points), P(points), P(None, points), P(points), P(points), P(points),
        P(*points), cells, cells,
    )
    return jax.shard_map(
        shards,
        mesh=mesh,
        in_specs=placed,
        out_specs=(P(None, *cells), cells),
        check_vma=False,
    )
```

time: 57.1 us -> 49.9 us (0.87)
  blocking collectives: 17.9 us -> 12.5 us
  waiting for transfers between devices: 5.46 us -> 3.9 us
    all_gather x2 -> x1, blocking collectives: 11.7 us -> 7.26 us  [shards(): lax.all_gather(told, 'gz', axis=0)]
    ppermute x1, waiting for transfers between devices: 1.44 us -> 0.01 us  [shift_up(): return lax.ppermute(block, axis, [(i, i + 1) for i in range(count - 1)])]
    all_gather x1, blocking collectives: 6.17 us -> 5.27 us  [neighbours(): stacked = lax.all_gather(block, axis, axis=0)]
    unnamed x18 -> x14, local copies, waits for them, and re-layouts: 1.26 us -> 1.59 us
  transfers between devices with their start and end apart: 2 -> 2, of which waited for: 2 -> 1; matrix products, arithmetic and copies ran while one was open for 1% -> 0% of each run, Pallas kernels for 0% -> 4%
where the time goes in v3:
time: 49.9 us; the launch traced here: 49.7 us
  Pallas kernels  24 us (48%)
  blocking collectives  12.5 us (25%)
  starting transfers between devices  6.21 us (12%)
  waiting for transfers between devices  3.9 us (8%)
  local copies, waits for them, and re-layouts  1.67 us (3%)
  between operations  1.35 us (3%)
    pallas_call x1, Pallas kernels, scatter(): pl.pallas_call(functools.partial(scatter_kernel, chunk), grid=(points //...  15.3 us
    all_gather x1, blocking collectives, shards(): lax.all_gather(told, 'gz', axis=0)  7.26 us
    all_gather x1, blocking collectives, neighbours(): stacked = lax.all_gather(block, axis, axis=0)  5.27 us
    ppermute x1, starting transfers between devices, shift_up(): return lax.ppermute(block, axis, [(i, i + 1) for i in range(count - 1)])  4.92 us
    ppermute x1, waiting for transfers between devices, shift_down(): return lax.ppermute(block, axis, [(i + 1, i) for i in range(count - 1)])  3.9 us
    pallas_call x1, Pallas kernels, local_solve(): pl.pallas_call(local_kernel, in_specs=[smem] + [vmem] * 6, out_shape=[jax...  3.13 us
    pallas_call x1, Pallas kernels, y_own(): pl.pallas_call(y_own_kernel, out_shape=jax.ShapeDtypeStruct((CELLS, COLS)...  2.09 us
    pallas_call x1, Pallas kernels, y_pack(): pl.pallas_call(y_pack_kernel, out_shape=jax.ShapeDtypeStruct((CELLS, COLS...  1.79 us
  transfers between devices with their start and end apart: 2, of which 1 were waited for; matrix products, arithmetic and copies ran while one was open for 0% of the time, Pallas kernels for 4%

profile of v3, /device:TPU:0, one launch (start us, length us, event | category | flops | bytes accessed | tf_op | source)
XLA Modules:
  0.0 49.7 jit_solution(16338254128078528376)
XLA Ops:
  1.3 15.3 %point_sums.1 = (f32[10,128,128]{2,1,0:T(8,128)}, f32[18,16,128]{2,1,0:T(8,128)}, f32[18,16,128]{2,1,0:T(8,128)}) custom-call(s32[1]{0:T(128)} %bitcast.19.count, f32[6,24576]{1,0:T(8,128)} %trial.1, f32[1,24576]{1,0:T(1,128)} %bitcast.29, f32[1,24576]{1,0:T(1,128)} %bitcast.30, f32[3,24576]{1,0:T(4,128)} %vel.1, f32[1,24576]{1,0:T(1,128)} %bitcast.31, ...), custom_call_target="tpu_custom_call" | custom-call | flops 12079595520 | bytes 1572864 | tf_op jit(solution)/shard_map/point_sums/pallas_call | solution.py:136
  16.5 4.9 %collective-permute-start = (f32[18,16,128]{2,1,0:T(8,128)}, f32[18,16,128]{2,1,0:T(8,128)S(1)}, u32[]{:S(2)}, u32[]{:S(2)}) collective-permute-start(f32[18,16,128]{2,1,0:T(8,128)} %get-tuple-element.11), channel_id=1, source_target_pairs={{0,8},{8,16},{16,24},{1,9},{9,17},{17,25},{2,10},{10,18},{18,26},{... | collective-permute-start | bytes 442376 | tf_op jit(solution)/shard_map/ppermute | solution.py:597
  21.5 1.3 %collective-permute-start.1 = (f32[18,16,128]{2,1,0:T(8,128)}, f32[18,16,128]{2,1,0:T(8,128)S(1)}, u32[]{:S(2)}, u32[]{:S(2)}) collective-permute-start(f32[18,16,128]{2,1,0:T(8,128)} %get-tuple-element.12), channel_id=1, source_target_pairs={{8,0},{16,8},{24,16},{9,1},{17,9},{25,17},{10,2},{18,10},{26,18},{... | collective-permute-start | bytes 442376 | tf_op jit(solution)/shard_map/ppermute | solution.py:602
  22.8 0.1 stack.47.where
  22.9 0.0 copy-start
  22.9 0.0 copy-start.6
  22.9 2.1 %y_own.1.own = f32[128,128]{1,0:T(8,128)} custom-call(f32[10,128,128]{2,1,0:T(8,128)} %get-tuple-element.10.sums, f32[128,128]{1,0:T(8,128)} %bitcast.23, f32[128,128]{1,0:T(8,128)} %bitcast.26), custom_call_target="tpu_custom_call" | custom-call | flops 4000000 | bytes 900000 | tf_op jit(solution)/shard_map/y_own/pallas_call | solution.py:168
  25.0 0.0 collective-permute-done.below
  25.0 0.0 copy-start.1
  25.0 3.9 %collective-permute-done.1.above = f32[18,16,128]{2,1,0:T(8,128)S(1)} collective-permute-done((f32[18,16,128]{2,1,0:T(8,128)}, f32[18,16,128]{2,1,0:T(8,128)S(1)}, u32[]{:S(2)}, u32[]{:S(2)}) %collective-permute-start.1) | collective-permute-done | bytes 147488 | tf_op jit(solution)/shard_map/ppermute | solution.py:602
  28.9 0.0 copy-done.1
  28.9 0.0 copy-start.3
  28.9 0.7 %copy-done.3 = f32[18,16,128]{2,1,0:T(8,128)} copy-done((f32[18,16,128]{2,1,0:T(8,128)}, f32[18,16,128]{2,1,0:T(8,128)S(1)}, u32[]{:S(2)}) %copy-start.3) | copy-done | bytes 147480
  29.6 1.8 %y_pack.1 = f32[128,128]{1,0:T(8,128)} custom-call(f32[128,128]{1,0:T(8,128)} %y_own.1.own, f32[18,16,128]{2,1,0:T(8,128)} %copy-done.1, f32[18,16,128]{2,1,0:T(8,128)} %copy-done.3), custom_call_target="tpu_custom_call" | custom-call | tf_op jit(solution)/shard_map/y_pack/pallas_call | solution.py:189
  31.3 5.3 %all-gather = f32[256,128]{1,0:T(8,128)S(1)} all-gather(f32[128,128]{1,0:T(8,128)} %y_pack.1), channel_id=2, replica_groups=mesh['gx'=4,'gy'=2,'gz'=4] {'gy'}, dimensions={0}, use_global_device_ids=true | all-gather | bytes 196608 | tf_op jit(solution)/shard_map/all_gather | solution.py:609
  36.6 0.0 copy-done
  36.6 0.0 copy-done.5
  36.6 0.0 copy-done.6
  36.6 0.0 copy-done.2
  36.6 0.0 copy-start.4
  36.7 0.9 %copy-done.4 = f32[18,16,128]{2,1,0:T(8,128)S(1)} copy-done((f32[18,16,128]{2,1,0:T(8,128)S(1)}, f32[18,16,128]{2,1,0:T(8,128)}, u32[]{:S(2)}) %copy-start.4) | copy-done | bytes 147480
  37.6 3.1 %local_solve.1 = (f32[3,128,128]{2,1,0:T(8,128)S(1)}, f32[3,3,14,8,128]{4,3,2,1,0:T(8,128)S(1)}, f32[264,128]{1,0:T(8,128)S(1)}) custom-call(s32[7]{0:T(128)S(1)} %stack.47.where, f32[10,128,128]{2,1,0:T(8,128)S(1)} %copy-done, f32[128,128]{1,0:T(8,128)S(1)} %bitcast.24, f32[128,128]{1,0:T(8,128)S(1)} %bitcast.27, f32[18,16,128]{2,1,0:T(8,128)S(1)} %copy-done.2, ...), custom_call_target="tpu_custom_call" | custom-call | tf_op jit(solution)/shard_map/local_solve/pallas_call | solution.py:422
  40.7 7.3 %all-gather.1 = f32[1056,128]{1,0:T(8,128)S(1)} all-gather(f32[264,128]{1,0:T(8,128)S(1)} %get-tuple-element.15), channel_id=3, replica_groups=mesh['gx'=4,'gy'=2,'gz'=4] {'gz'}, dimensions={0}, use_global_device_ids=true | all-gather | bytes 675840 | tf_op jit(solution)/shard_map/all_gather | solution.py:631
  48.0 1.7 %final.1 = (f32[3,128,128]{2,1,0:T(8,128)}, f32[128,128]{1,0:T(8,128)}) custom-call(s32[7]{0:T(128)S(1)} %stack.47.where, f32[3,128,128]{2,1,0:T(8,128)S(1)} %get-tuple-element.13.vel, f32[3,3,14,8,128]{4,3,2,1,0:T(8,128)S(1)} %get-tuple-element.14.inner, f32[4,264,128]{2,1,0:T(8,128)S(1)} %bitcast.20), custom_call_target="tpu_custom_call" | custom-call | tf_op jit(solution)/shard_map/final/pallas_call | solution.py:583
  (2 shorter events, 0.0 us)
Async XLA Ops:
  16.5 8.4 %collective-permute-start = (f32[18,16,128]{2,1,0:T(8,128)}, f32[18,16,128]{2,1,0:T(8,128)S(1)}, u32[]{:S(2)}, u32[]{:S(2)}) collective-permute-start(f32[18,16,128]{2,1,0:T(8,128)} %get-tuple-element.11), channel_id=1, source_target_pairs={{0,8},{8,16},{16,24},{1,9},{9,17},{17,25},{2,10},{10,18},{18,26},{... | collective-permute-start | bytes 442376 | tf_op jit(solution)/shard_map/ppermute | solution.py:597
  21.5 7.4 %collective-permute-start.1 = (f32[18,16,128]{2,1,0:T(8,128)}, f32[18,16,128]{2,1,0:T(8,128)S(1)}, u32[]{:S(2)}, u32[]{:S(2)}) collective-permute-start(f32[18,16,128]{2,1,0:T(8,128)} %get-tuple-element.12), channel_id=1, source_target_pairs={{8,0},{16,8},{24,16},{9,1},{17,9},{25,17},{10,2},{18,10},{26,18},{... | collective-permute-start | bytes 442376 | tf_op jit(solution)/shard_map/ppermute | solution.py:602
  22.9 13.7 %copy-start = (f32[10,128,128]{2,1,0:T(8,128)S(1)}, f32[10,128,128]{2,1,0:T(8,128)}, u32[]{:S(2)}) copy-start(f32[10,128,128]{2,1,0:T(8,128)} %get-tuple-element.10.sums) | copy-start | bytes 1966084
  22.9 13.7 %copy-start.5 = (f32[16,8,128]{2,1,0:T(8,128)S(1)}, f32[16,8,128]{2,1,0:T(8,128)}, u32[]{:S(2)}) copy-start(f32[16,8,128]{2,1,0:T(8,128)} %param.18) | copy-start | bytes 196612
  22.9 13.7 %copy-start.6 = (f32[16,8,128]{2,1,0:T(8,128)S(1)}, f32[16,8,128]{2,1,0:T(8,128)}, u32[]{:S(2)}) copy-start(f32[16,8,128]{2,1,0:T(8,128)} %param.19) | copy-start | bytes 196612
  25.0 3.9 %copy-start.1 = (f32[18,16,128]{2,1,0:T(8,128)}, f32[18,16,128]{2,1,0:T(8,128)S(1)}, u32[]{:S(2)}) copy-start(f32[18,16,128]{2,1,0:T(8,128)S(1)} %collective-permute-done.below) | copy-start | bytes 442372
  28.9 0.7 %copy-start.3 = (f32[18,16,128]{2,1,0:T(8,128)}, f32[18,16,128]{2,1,0:T(8,128)S(1)}, u32[]{:S(2)}) copy-start(f32[18,16,128]{2,1,0:T(8,128)S(1)} %collective-permute-done.1.above) | copy-start | bytes 442372
  31.3 5.3 %copy-start.2 = (f32[18,16,128]{2,1,0:T(8,128)S(1)}, f32[18,16,128]{2,1,0:T(8,128)}, u32[]{:S(2)}) copy-start(f32[18,16,128]{2,1,0:T(8,128)} %copy-done.1) | copy-start | bytes 442372
  36.6 0.9 %copy-start.4 = (f32[18,16,128]{2,1,0:T(8,128)S(1)}, f32[18,16,128]{2,1,0:T(8,128)}, u32[]{:S(2)}) copy-start(f32[18,16,128]{2,1,0:T(8,128)} %copy-done.3) | copy-start | bytes 442372

commit v4 on v3

--- a/solution.py
+++ b/solution.py
@@ -24,6 +24,8 @@
     (XX, 0), (XX, 1), (XX, 2), (XY, 0), (XY, 1), (YY, 0),
     (MX, 0), (MX, 1), (MY, 0), (MZ, 0), (MASS, 0), (MASS, 1),
 )
+X_DEEP = 3
+X_SENT = len(X_ROWS) + X_DEEP
 Y_DEPTH = {ZX: 1, YZ: 2, ZZ: 1, XX: 1, YY: 3, XY: 2, MX: 1, MY: 2, MZ: 1, MASS: 2, POR: 1, PERM: 1}
 Y_PLACE = {}
 _at = 0
@@ -61,15 +63,16 @@
     return trial * factor - jnp.where(part < 3, mean, 0.0)
 
 
-def scatter_kernel(
-    chunk, count, trial, mean, cons, vel, wt, cell, flag, por, perm, out, low, high, acc
-):
-    step = pl.program_id(0)
-    slot = step * chunk + lax.broadcasted_iota(i32, (1, chunk), 1)
-    weight = jnp.where(slot < count[0], wt[...], 0.0)
-    stress = row_stress(trial[...], mean[...], cons[...], flag[...]) * weight
-    momentum = vel[...] * weight
-    place = cell[...]
+def point_rows(trial, mean, cons, vel, wt, flag, live):
+    weight = jnp.where(live, wt, 0.0)
+    stress = row_stress(trial, mean, cons, flag) * weight
+    momentum = vel * weight
+    rows = [stress[i : i + 1] for i in STRESS_ORDER]
+    return rows + [momentum[i : i + 1] for i in range(3)] + [weight]
+
+
+def cell_products(rows, place):
+    chunk = place.shape[1]
     hi = (place >> 7) & 63
     lo = ((place >> 13) << 7) | (place & 127)
 
@@ -88,8 +91,6 @@
     base32 = lax.broadcasted_iota(i32, (32, chunk), 0)
     hi_mask8 = [base32 + 32 * b == jnp.broadcast_to(hi, (32, chunk)) for b in range(2)]
     zero8 = jnp.zeros((32, chunk), f8)
-    rows = [stress[i : i + 1] for i in STRESS_ORDER]
-    rows += [momentum[i : i + 1] for i in range(3)] + [weight]
     left, left8 = [], []
     for row in rows:
         top = row.astype(bf).astype(f32)
@@ -102,56 +103,96 @@
     dims = (((1,), (1,)), ((), ()))
     prod = lax.dot_general(left, right, dims, preferred_element_type=f32)
     prod8 = lax.dot_general(left8, right.astype(f8), dims, preferred_element_type=f32)
-    prod = prod + prod8 * (1 / 256.0)
-
-    @pl.when(step == 0)
-    def _():
-        acc[...] = prod
-
-    @pl.when(step > 0)
-    def _():
-        acc[...] += prod
-
-    @pl.when(step == pl.num_programs(0) - 1)
-    def _():
-        for i in range(10):
-            out[i, 0:64, :] = acc[i * 64 : i * 64 + 64, :COLS]
-            out[i, 64:128, :] = acc[i * 64 : i * 64 + 64, COLS:]
-        for q, (field, depth) in enumerate(X_ROWS):
-            for face, row in ((low, depth), (high, ROWS - 1 - depth)):
-                rows = pl.ds(row, LEVELS, stride=ROWS)
-                if field < 10:
-                    face[q] = out[field, rows, :]
-                else:
-                    face[q] = (por if field == POR else perm)[rows, :]
+    return prod + prod8 * (1 / 256.0)
+
+
+def scatter_kernel(chunk, *refs):
+    sources, (out, low, high), scratch = refs[:10], refs[10:13], refs[13:]
+    trial, mean, cons, vel, wt, cell, flag, count, por, perm = scratch[:10]
+    acc, sems = scratch[10:]
+    chunks = cell.shape[1] // chunk
+
+    def copy(n, c):
+        if n < 7:
+            at = pl.ds(pl.multiple_of(c * chunk, chunk), chunk)
+            return pltpu.make_async_copy(sources[n].at[:, at], scratch[n].at[:, at], sems.at[n, c])
+        return pltpu.make_async_copy(sources[n], scratch[n], sems.at[n, 0])
+
+    copy(7, 0).start()
+    for c in range(chunks):
+        for n in range(7):
+            copy(n, c).start()
+    copy(8, 0).start()
+    copy(9, 0).start()
+    copy(7, 0).wait()
+
+    def step(c, carry):
+        for n in range(7):
+            copy(n, c).wait()
+        at = pl.ds(pl.multiple_of(c * chunk, chunk), chunk)
+        slot = c * chunk + lax.broadcasted_iota(i32, (1, chunk), 1)
+        live = slot < count[0]
+        rows = point_rows(
+            trial[:, at], mean[:, at], cons[:, at], vel[:, at], wt[:, at], flag[:, at], live
+        )
+        prod = cell_products(rows, cell[:, at])
+
+        @pl.when(c == 0)
+        def _():
+            acc[...] = prod
+
+        @pl.when(c > 0)
+        def _():
+            acc[...] += prod
+
+        return carry
+
+    lax.fori_loop(0, chunks, step, 0)
+    copy(8, 0).wait()
+    copy(9, 0).wait()
+    for i in range(10):
+        out[i, 0:64, :] = acc[i * 64 : i * 64 + 64, :COLS]
+        out[i, 64:128, :] = acc[i * 64 : i * 64 + 64, COLS:]
+    lane = lax.broadcasted_iota(i32, (LEVELS, COLS), 1)
+    packed = [[jnp.zeros((LEVELS, COLS), f32)] * X_DEEP for _ in range(2)]
+    for q, (field, deep) in enumerate(X_ROWS):
+        at, depth = Y_PLACE[field] + HALF, Y_DEPTH[field]
+        mask = (lane >= at - depth) & (lane < at + depth)
+        for side, row in ((0, deep), (1, ROWS - 1 - deep)):
+            rows = pl.ds(row, LEVELS, stride=ROWS)
+            if field < 10:
+                values = out[field, rows, :]
+            else:
+                values = (por if field == POR else perm)[rows, :]
+            (low, high)[side][q] = values
+            packed[side][deep] = jnp.where(mask, turn(values, at, 1), packed[side][deep])
+    for deep in range(X_DEEP):
+        low[len(X_ROWS) + deep] = packed[0][deep]
+        high[len(X_ROWS) + X_DEEP - 1 - deep] = packed[1][deep]
 
 
 def scatter(trial, mean, cons, vel, wt, cell, flag, count, por, perm):
     points = mean.shape[0]
-    chunk = 8192 if points % 8192 == 0 else points
+    chunk = points // 2 if points % 256 == 0 else points
     row = lambda v: v.reshape(1, points)
-    spec = lambda r: pl.BlockSpec((r, chunk), lambda i: (0, i))
-    fixed = lambda *shape: pl.BlockSpec(shape, lambda i: (0,) * len(shape))
-    faces = (len(X_ROWS), LEVELS, COLS)
+    args = (trial, row(mean), row(cons), vel, row(wt), row(cell), row(flag), count, por, perm)
+    faces = (X_SENT, LEVELS, COLS)
     return pl.pallas_call(
         functools.partial(scatter_kernel, chunk),
-        grid=(points // chunk,),
-        in_specs=[pl.BlockSpec(memory_space=pltpu.SMEM)]
-        + [spec(r) for r in (6, 1, 1, 3, 1, 1, 1)]
-        + [fixed(CELLS, COLS)] * 2,
-        out_specs=[fixed(10, CELLS, COLS), fixed(*faces), fixed(*faces)],
+        in_specs=[pl.BlockSpec(memory_space=pltpu.HBM)] * len(args),
         out_shape=[
             jax.ShapeDtypeStruct((10, CELLS, COLS), f32),
             jax.ShapeDtypeStruct(faces, f32),
             jax.ShapeDtypeStruct(faces, f32),
         ],
-        scratch_shapes=[pltpu.VMEM((640, 256), f32)],
-        compiler_params=pltpu.CompilerParams(vmem_limit_bytes=60 << 20),
+        scratch_shapes=[pltpu.VMEM(v.shape, v.dtype) for v in args]
+        + [pltpu.VMEM((640, 256), f32), pltpu.SemaphoreType.DMA((len(args), points // chunk))],
+        compiler_params=pltpu.CompilerParams(vmem_limit_bytes=56 << 20),
         cost_estimate=pl.CostEstimate(
             flops=2 * 960 * 256 * points, bytes_accessed=64 * points, transcendentals=0
         ),
         name="point_sums",
-    )(count.reshape(1), trial, row(mean), row(cons), vel, row(wt), row(cell), row(flag), por, perm)
+    )(*args)
 
 
 def y_own_kernel(sums, por, perm, out):
@@ -169,28 +210,16 @@
         y_own_kernel,
         out_shape=jax.ShapeDtypeStruct((CELLS, COLS), f32),
         cost_estimate=pl.CostEstimate(flops=4000000, bytes_accessed=900000, transcendentals=0),
+        compiler_params=pltpu.CompilerParams(vmem_limit_bytes=8 << 20),
         name="y_own",
     )(sums, por, perm)
 
 
-def y_pack_kernel(own, below, above, out):
-    lane = lax.broadcasted_iota(i32, (CELLS, COLS), 1)
-    lane16 = lax.broadcasted_iota(i32, (LEVELS, COLS), 1)
-    slots = [jnp.zeros((LEVELS, COLS), f32)] * ROWS
-    for q, (field, deep) in enumerate(X_ROWS):
-        at, depth = Y_PLACE[field] + HALF, Y_DEPTH[field]
-        mask = (lane16 >= at - depth) & (lane16 < at + depth)
-        for source, slot in ((above, deep), (below, ROWS - 1 - deep)):
-            slots[slot] = jnp.where(mask, turn(source[q], at, 1), slots[slot])
-    out[...] = jnp.where(lane < HALF, own[...], jnp.concatenate(slots, axis=0))
-
-
-def y_pack(own, below, above):
-    return pl.pallas_call(
-        y_pack_kernel,
-        out_shape=jax.ShapeDtypeStruct((CELLS, COLS), f32),
-        name="y_pack",
-    )(own, below, above)
+def with_rims(own, below, above):
+    rows = X_DEEP * LEVELS
+    first = above[len(X_ROWS) :].reshape(rows, COLS)
+    last = below[len(X_ROWS) :].reshape(rows, COLS)
+    return own + jnp.concatenate([first, jnp.zeros((CELLS - 2 * rows, COLS), f32), last])
 
 
 def y_from_above(shape):
@@ -428,7 +457,7 @@
             jax.ShapeDtypeStruct((MSG_ROWS, COLS), f32),
         ],
         scratch_shapes=[pltpu.VMEM((FIELDS, CELLS, COLS), f32), pltpu.VMEM((CELLS, COLS), f32)],
-        compiler_params=pltpu.CompilerParams(vmem_limit_bytes=32 << 20),
+        compiler_params=pltpu.CompilerParams(vmem_limit_bytes=16 << 20),
         name="local_solve",
     )(where, sums, por, perm, below, above, packs)
 
@@ -587,7 +616,7 @@
             jax.ShapeDtypeStruct((3, CELLS, COLS), f32),
             jax.ShapeDtypeStruct((CELLS, COLS), f32),
         ],
-        compiler_params=pltpu.CompilerParams(vmem_limit_bytes=32 << 20),
+        compiler_params=pltpu.CompilerParams(vmem_limit_bytes=16 << 20),
         name="final",
     )(where, vel, inner, told)
 
@@ -623,7 +652,7 @@
 
     has = ends("gx") + ends("gy")
     own = y_own(sums, por, perm)
-    packs, y_low, y_high = neighbours(y_pack(own, below, above), "gy")
+    packs, y_low, y_high = neighbours(with_rims(own, below, above), "gy")
     where = jnp.stack(
         [jnp.asarray(v, i32) for v in [y_low, y_high] + has + [lax.axis_index("gz")]]
     )

time: 49.9 us -> 46.9 us (0.940)
  Pallas kernels: 24 us -> 20.2 us
  waiting for transfers between devices: 3.9 us -> 5.08 us
    pallas_call x2 -> x1, Pallas kernels: 17.1 us -> 15.1 us  [scatter(): pl.pallas_call(functools.partial(scatter_kernel, chunk), in_specs=[pl.Blo...]
    pallas_call x1, Pallas kernels: 2.09 us -> 0.26 us  [y_own(): pl.pallas_call(y_own_kernel, out_shape=jax.ShapeDtypeStruct((CELLS, COLS)...]
    ppermute x1, waiting for transfers between devices: 0.01 us -> 1.07 us  [shift_up(): return lax.ppermute(block, axis, [(i, i + 1) for i in range(count - 1)])]
    unnamed x14 -> x8, local copies, waits for them, and re-layouts: 1.59 us -> 1.1 us
  transfers between devices with their start and end apart: 2 -> 2, of which waited for: 1 -> 2; matrix products, arithmetic and copies ran while one was open for 0% -> 0% of each run, Pallas kernels for 4% -> 1%
where the time goes in v4:
time: 46.9 us; the launch traced here: 46.6 us
  Pallas kernels  20.2 us (43%)
  blocking collectives  12.2 us (26%)
  starting transfers between devices  6.36 us (14%)
  waiting for transfers between devices  5.08 us (11%)
  between operations  1.38 us (3%)
  local copies, waits for them, and re-layouts  1.26 us (3%)
    pallas_call x1, Pallas kernels, scatter(): pl.pallas_call(functools.partial(scatter_kernel, chunk), in_specs=[pl.Blo...  15.1 us
    all_gather x1, blocking collectives, shards(): lax.all_gather(told, 'gz', axis=0)  7.26 us
    ppermute x1, starting transfers between devices, shift_up(): return lax.ppermute(block, axis, [(i, i + 1) for i in range(count - 1)])  5.07 us
    all_gather x1, blocking collectives, neighbours(): stacked = lax.all_gather(block, axis, axis=0)  4.94 us
    ppermute x1, waiting for transfers between devices, shift_down(): return lax.ppermute(block, axis, [(i + 1, i) for i in range(count - 1)])  4.01 us
    pallas_call x1, Pallas kernels, local_solve(): pl.pallas_call(local_kernel, in_specs=[smem] + [vmem] * 6, out_shape=[jax...  3.13 us
    pallas_call x1, Pallas kernels, final(): pl.pallas_call(functools.partial(final_kernel, told.shape[0]), in_specs=[...  1.72 us
    ppermute x1, starting transfers between devices, shift_down(): return lax.ppermute(block, axis, [(i + 1, i) for i in range(count - 1)])  1.29 us
  transfers between devices with their start and end apart: 2, of which 2 were waited for; matrix products, arithmetic and copies ran while one was open for 0% of the time, Pallas kernels for 1%

profile of v4, /device:TPU:0, one launch (start us, length us, event | category | flops | bytes accessed | tf_op | source)
XLA Modules:
  0.0 46.6 jit_solution(3737377278777476888)
XLA Ops:
  1.3 0.0 copy-start.3
  1.3 15.1 %point_sums.1 = (f32[10,128,128]{2,1,0:T(8,128)}, f32[21,16,128]{2,1,0:T(8,128)}, f32[21,16,128]{2,1,0:T(8,128)}) custom-call(f32[6,24576]{1,0:T(8,128)} %refs_0_.1, f32[1,24576]{1,0:T(1,128)} %bitcast.31, f32[1,24576]{1,0:T(1,128)} %bitcast.32, f32[3,24576]{1,0:T(4,128)} %refs_3_.1, f32[1,24576]{1,0:T(1,128)} %bitcast.33, s32[1,24576]{1,0:T(1,128)} %bitcast.34, ...), custom_call_target="tpu_custom_call" | custom-call | flops 12079595520 | bytes 1572864 | tf_op jit(solution)/shard_map/point_sums/pallas_call | solution.py:180
  16.4 0.0 copy-start.2
  16.4 5.1 %collective-permute-start = (f32[21,16,128]{2,1,0:T(8,128)}, f32[21,16,128]{2,1,0:T(8,128)S(1)}, u32[]{:S(2)}, u32[]{:S(2)}) collective-permute-start(f32[21,16,128]{2,1,0:T(8,128)} %get-tuple-element.11), channel_id=1, source_target_pairs={{0,8},{8,16},{16,24},{1,9},{9,17},{17,25},{2,10},{10,18},{18,26},{... | collective-permute-start | bytes 516104 | tf_op jit(solution)/shard_map/ppermute | solution.py:626
  21.5 1.3 %collective-permute-start.1 = (f32[21,16,128]{2,1,0:T(8,128)}, f32[21,16,128]{2,1,0:T(8,128)S(1)}, u32[]{:S(2)}, u32[]{:S(2)}) collective-permute-start(f32[21,16,128]{2,1,0:T(8,128)} %get-tuple-element.12), channel_id=1, source_target_pairs={{8,0},{16,8},{24,16},{9,1},{17,9},{25,17},{10,2},{18,10},{26,18},{... | collective-permute-start | bytes 516104 | tf_op jit(solution)/shard_map/ppermute | solution.py:631
  22.8 0.1 pad.1.clone
  22.9 0.1 stack.47.where
  23.0 0.0 copy-done.3
  23.0 0.0 copy-done.2
  23.0 0.0 copy-start
  23.0 1.1 %copy-done = f32[10,128,128]{2,1,0:T(8,128)S(1)} copy-done((f32[10,128,128]{2,1,0:T(8,128)S(1)}, f32[10,128,128]{2,1,0:T(8,128)}, u32[]{:S(2)}) %copy-start) | copy-done | bytes 655384
  24.1 0.0 copy-start.1
  24.1 0.3 y_own.1
  24.3 1.1 %collective-permute-done.below = f32[21,16,128]{2,1,0:T(8,128)S(1)} collective-permute-done((f32[21,16,128]{2,1,0:T(8,128)}, f32[21,16,128]{2,1,0:T(8,128)S(1)}, u32[]{:S(2)}, u32[]{:S(2)}) %collective-permute-start) | collective-permute-done | bytes 172064 | tf_op jit(solution)/shard_map/ppermute | solution.py:626
  25.4 4.0 %collective-permute-done.1.above = f32[21,16,128]{2,1,0:T(8,128)S(1)} collective-permute-done((f32[21,16,128]{2,1,0:T(8,128)}, f32[21,16,128]{2,1,0:T(8,128)S(1)}, u32[]{:S(2)}, u32[]{:S(2)}) %collective-permute-start.1) | collective-permute-done | bytes 172064 | tf_op jit(solution)/shard_map/ppermute | solution.py:631
  29.4 0.1 maximum_add_fusion
  29.5 4.9 %all-gather = f32[256,128]{1,0:T(8,128)S(1)} all-gather(f32[128,128]{1,0:T(8,128)S(1)} %maximum_add_fusion), channel_id=2, replica_groups=mesh['gx'=4,'gy'=2,'gz'=4] {'gy'}, dimensions={0}, use_global_device_ids=true | all-gather | bytes 196608 | tf_op jit(solution)/shard_map/all_gather | solution.py:638
  34.5 0.0 copy-done.1
  34.5 3.1 %local_solve.1 = (f32[3,128,128]{2,1,0:T(8,128)S(1)}, f32[3,3,14,8,128]{4,3,2,1,0:T(8,128)S(1)}, f32[264,128]{1,0:T(8,128)S(1)}) custom-call(s32[7]{0:T(128)S(1)} %stack.47.where, f32[10,128,128]{2,1,0:T(8,128)S(1)} %copy-done.1, f32[128,128]{1,0:T(8,128)S(1)} %bitcast.24, f32[128,128]{1,0:T(8,128)S(1)} %bitcast.27, ...), custom_call_target="tpu_custom_call" | custom-call | tf_op jit(solution)/shard_map/local_solve/pallas_call | solution.py:451
  37.6 7.3 %all-gather.1 = f32[1056,128]{1,0:T(8,128)S(1)} all-gather(f32[264,128]{1,0:T(8,128)S(1)} %get-tuple-element.15), channel_id=3, replica_groups=mesh['gx'=4,'gy'=2,'gz'=4] {'gz'}, dimensions={0}, use_global_device_ids=true | all-gather | bytes 675840 | tf_op jit(solution)/shard_map/all_gather | solution.py:660
  44.9 1.7 %final.1 = (f32[3,128,128]{2,1,0:T(8,128)}, f32[128,128]{1,0:T(8,128)}) custom-call(s32[7]{0:T(128)S(1)} %stack.47.where, f32[3,128,128]{2,1,0:T(8,128)S(1)} %get-tuple-element.13.vel, f32[3,3,14,8,128]{4,3,2,1,0:T(8,128)S(1)} %get-tuple-element.14.inner, f32[4,264,128]{2,1,0:T(8,128)S(1)} %bitcast.20), custom_call_target="tpu_custom_call" | custom-call | tf_op jit(solution)/shard_map/final/pallas_call | solution.py:612
  (3 shorter events, 0.0 us)
Async XLA Ops:
  1.3 21.7 %copy-start.3 = (f32[16,8,128]{2,1,0:T(8,128)S(1)}, f32[16,8,128]{2,1,0:T(8,128)}, u32[]{:S(2)}) copy-start(f32[16,8,128]{2,1,0:T(8,128)} %param.19) | copy-start | bytes 196612
  16.4 6.6 %copy-start.2 = (f32[16,8,128]{2,1,0:T(8,128)S(1)}, f32[16,8,128]{2,1,0:T(8,128)}, u32[]{:S(2)}) copy-start(f32[16,8,128]{2,1,0:T(8,128)} %param.18) | copy-start | bytes 196612
  16.4 9.0 %collective-permute-start = (f32[21,16,128]{2,1,0:T(8,128)}, f32[21,16,128]{2,1,0:T(8,128)S(1)}, u32[]{:S(2)}, u32[]{:S(2)}) collective-permute-start(f32[21,16,128]{2,1,0:T(8,128)} %get-tuple-element.11), channel_id=1, source_target_pairs={{0,8},{8,16},{16,24},{1,9},{9,17},{17,25},{2,10},{10,18},{18,26},{... | collective-permute-start | bytes 516104 | tf_op jit(solution)/shard_map/ppermute | solution.py:626
  21.5 7.9 %collective-permute-start.1 = (f32[21,16,128]{2,1,0:T(8,128)}, f32[21,16,128]{2,1,0:T(8,128)S(1)}, u32[]{:S(2)}, u32[]{:S(2)}) collective-permute-start(f32[21,16,128]{2,1,0:T(8,128)} %get-tuple-element.12), channel_id=1, source_target_pairs={{8,0},{16,8},{24,16},{9,1},{17,9},{25,17},{10,2},{18,10},{26,18},{... | collective-permute-start | bytes 516104 | tf_op jit(solution)/shard_map/ppermute | solution.py:631
  23.0 1.1 %copy-start = (f32[10,128,128]{2,1,0:T(8,128)S(1)}, f32[10,128,128]{2,1,0:T(8,128)}, u32[]{:S(2)}) copy-start(f32[10,128,128]{2,1,0:T(8,128)} %get-tuple-element.10.sums) | copy-start | bytes 1966084
  24.1 10.4 %copy-start.1 = (f32[10,128,128]{2,1,0:T(8,128)S(1)}, f32[10,128,128]{2,1,0:T(8,128)}, u32[]{:S(2)}) copy-start(f32[10,128,128]{2,1,0:T(8,128)} %get-tuple-element.10.sums) | copy-start | bytes 1966084

commit v5 on v4

--- a/solution.py
+++ b/solution.py
@@ -71,71 +71,53 @@
     return rows + [momentum[i : i + 1] for i in range(3)] + [weight]
 
 
-def cell_products(rows, place):
+def cell_products(rows, place, groups):
     chunk = place.shape[1]
-    hi = (place >> 7) & 63
-    lo = ((place >> 13) << 7) | (place & 127)
-
-    def spread(row, count, kind):
-        return jnp.broadcast_to(row, (count, chunk)).astype(kind)
+    row = (place >> 7) & (ROWS - 1)
+    deep = jnp.where(row < ROWS // 2, row, ROWS - 1 - row)
+    hi = deep * 16 + (row >> 2) * 8 + ((place >> 10) & 7)
+    lo = ((place >> 13) << 7) | (place & (COLS - 1))
+
+    def spread(row):
+        return jnp.broadcast_to(row, (16, chunk)).astype(bf)
 
     one, zero = jnp.array(1, bf), jnp.array(0, bf)
     base = lax.broadcasted_iota(i32, (16, chunk), 0)
 
     def equal(index, count):
-        index = spread(index.astype(f32), 16, bf)
+        index = spread(index.astype(f32))
         return [(base + b * 16).astype(f32).astype(bf) == index for b in range(count // 16)]
 
-    hi_mask = equal(hi, 64)
+    mask = equal(hi, 64)
     right = jnp.concatenate([jnp.where(m, one, zero) for m in equal(lo, 256)], axis=0)
-    base32 = lax.broadcasted_iota(i32, (32, chunk), 0)
-    hi_mask8 = [base32 + 32 * b == jnp.broadcast_to(hi, (32, chunk)) for b in range(2)]
-    zero8 = jnp.zeros((32, chunk), f8)
-    left, left8 = [], []
-    for row in rows:
-        top = row.astype(bf).astype(f32)
-        part = spread(top, 16, bf)
-        left += [jnp.where(m, part, zero) for m in hi_mask]
-        part = spread((row - top) * 256.0, 32, f8)
-        left8 += [jnp.where(m, part, zero8) for m in hi_mask8]
-    left = jnp.concatenate(left, axis=0)
-    left8 = jnp.concatenate(left8, axis=0)
+    tops = [row.astype(bf).astype(f32) for row in rows]
+    parts = [spread(top) for top in tops]
+    rests = [spread((row - top) * 256.0) for row, top in zip(rows, tops)]
+    left = jnp.concatenate([jnp.where(mask[d], parts[f], zero) for f, d in groups], axis=0)
+    left8 = jnp.concatenate([jnp.where(mask[d], rests[f], zero) for f, d in groups], axis=0)
     dims = (((1,), (1,)), ((), ()))
     prod = lax.dot_general(left, right, dims, preferred_element_type=f32)
-    prod8 = lax.dot_general(left8, right.astype(f8), dims, preferred_element_type=f32)
+    prod8 = lax.dot_general(
+        left8.astype(f8), right.astype(f8), dims, preferred_element_type=f32
+    )
     return prod + prod8 * (1 / 256.0)
 
 
-def scatter_kernel(chunk, *refs):
-    sources, (out, low, high), scratch = refs[:10], refs[10:13], refs[13:]
-    trial, mean, cons, vel, wt, cell, flag, count, por, perm = scratch[:10]
-    acc, sems = scratch[10:]
-    chunks = cell.shape[1] // chunk
-
-    def copy(n, c):
-        if n < 7:
-            at = pl.ds(pl.multiple_of(c * chunk, chunk), chunk)
-            return pltpu.make_async_copy(sources[n].at[:, at], scratch[n].at[:, at], sems.at[n, c])
-        return pltpu.make_async_copy(sources[n], scratch[n], sems.at[n, 0])
-
-    copy(7, 0).start()
-    for c in range(chunks):
-        for n in range(7):
-            copy(n, c).start()
-    copy(8, 0).start()
-    copy(9, 0).start()
-    copy(7, 0).wait()
+POINT_ARGS = 8
+
+
+def group_sums(chunk, groups, args, acc, arrived=lambda c: None):
+    trial, mean, cons, vel, wt, cell, flag, count = args[:POINT_ARGS]
 
     def step(c, carry):
-        for n in range(7):
-            copy(n, c).wait()
+        arrived(c)
         at = pl.ds(pl.multiple_of(c * chunk, chunk), chunk)
         slot = c * chunk + lax.broadcasted_iota(i32, (1, chunk), 1)
         live = slot < count[0]
         rows = point_rows(
             trial[:, at], mean[:, at], cons[:, at], vel[:, at], wt[:, at], flag[:, at], live
         )
-        prod = cell_products(rows, cell[:, at])
+        prod = cell_products(rows, cell[:, at], groups)
 
         @pl.when(c == 0)
         def _():
@@ -147,72 +129,126 @@
 
         return carry
 
-    lax.fori_loop(0, chunks, step, 0)
-    copy(8, 0).wait()
-    copy(9, 0).wait()
-    for i in range(10):
-        out[i, 0:64, :] = acc[i * 64 : i * 64 + 64, :COLS]
-        out[i, 64:128, :] = acc[i * 64 : i * 64 + 64, COLS:]
+    lax.fori_loop(0, cell.shape[1] // chunk, step, 0)
+
+
+def copied_sums(chunk, groups, sources, scratch, acc, sems):
+    chunks = sources[1].shape[1] // chunk
+    points = range(POINT_ARGS - 1)
+
+    def copy(n, c):
+        if n in points:
+            at = pl.ds(pl.multiple_of(c * chunk, chunk), chunk)
+            return pltpu.make_async_copy(sources[n].at[:, at], scratch[n].at[:, at], sems.at[n, c])
+        return pltpu.make_async_copy(sources[n], scratch[n], sems.at[n, 0])
+
+    others = range(POINT_ARGS, len(sources))
+    copy(7, 0).start()
+    for c in range(chunks):
+        for n in points:
+            copy(n, c).start()
+    for n in others:
+        copy(n, 0).start()
+    copy(7, 0).wait()
+
+    def arrived(c):
+        for n in points:
+            copy(n, c).wait()
+
+    group_sums(chunk, groups, scratch, acc, arrived)
+    for n in others:
+        copy(n, 0).wait()
+
+
+NEAR_GROUPS = tuple(x for x in X_ROWS if x[0] < 10)
+FAR_GROUPS = tuple(
+    (f, d) for f in range(10) for d in range(ROWS // 2) if (f, d) not in NEAR_GROUPS
+)
+HALVES = ((0, 0), (1, COLS))
+
+
+def near_kernel(chunk, *refs):
+    sources, (acc, low, high), scratch, sems = refs[:10], refs[10:13], refs[13:23], refs[23]
+    copied_sums(chunk, NEAR_GROUPS, sources, scratch, acc, sems)
+    por, perm = scratch[POINT_ARGS:]
     lane = lax.broadcasted_iota(i32, (LEVELS, COLS), 1)
     packed = [[jnp.zeros((LEVELS, COLS), f32)] * X_DEEP for _ in range(2)]
     for q, (field, deep) in enumerate(X_ROWS):
         at, depth = Y_PLACE[field] + HALF, Y_DEPTH[field]
         mask = (lane >= at - depth) & (lane < at + depth)
         for side, row in ((0, deep), (1, ROWS - 1 - deep)):
-            rows = pl.ds(row, LEVELS, stride=ROWS)
+            face = (low, high)[side]
             if field < 10:
-                values = out[field, rows, :]
+                first = NEAR_GROUPS.index((field, deep)) * 16 + side * 8
+                for half, col in HALVES:
+                    face[q, 8 * half : 8 * half + 8, :] = acc[first : first + 8, col : col + COLS]
             else:
-                values = (por if field == POR else perm)[rows, :]
-            (low, high)[side][q] = values
-            packed[side][deep] = jnp.where(mask, turn(values, at, 1), packed[side][deep])
+                face[q] = (por if field == POR else perm)[pl.ds(row, LEVELS, stride=ROWS), :]
+            packed[side][deep] = jnp.where(mask, turn(face[q], at, 1), packed[side][deep])
     for deep in range(X_DEEP):
         low[len(X_ROWS) + deep] = packed[0][deep]
         high[len(X_ROWS) + X_DEEP - 1 - deep] = packed[1][deep]
 
 
-def scatter(trial, mean, cons, vel, wt, cell, flag, count, por, perm):
-    points = mean.shape[0]
-    chunk = points // 2 if points % 256 == 0 else points
-    row = lambda v: v.reshape(1, points)
-    args = (trial, row(mean), row(cons), vel, row(wt), row(cell), row(flag), count, por, perm)
-    faces = (X_SENT, LEVELS, COLS)
-    return pl.pallas_call(
-        functools.partial(scatter_kernel, chunk),
-        in_specs=[pl.BlockSpec(memory_space=pltpu.HBM)] * len(args),
-        out_shape=[
-            jax.ShapeDtypeStruct((10, CELLS, COLS), f32),
-            jax.ShapeDtypeStruct(faces, f32),
-            jax.ShapeDtypeStruct(faces, f32),
-        ],
-        scratch_shapes=[pltpu.VMEM(v.shape, v.dtype) for v in args]
-        + [pltpu.VMEM((640, 256), f32), pltpu.SemaphoreType.DMA((len(args), points // chunk))],
-        compiler_params=pltpu.CompilerParams(vmem_limit_bytes=56 << 20),
-        cost_estimate=pl.CostEstimate(
-            flops=2 * 960 * 256 * points, bytes_accessed=64 * points, transcendentals=0
-        ),
-        name="point_sums",
-    )(*args)
-
-
-def y_own_kernel(sums, por, perm, out):
+def far_kernel(chunk, *refs):
+    args, out, own, acc = refs[:11], *refs[11:]
+    group_sums(chunk, FAR_GROUPS, args, acc)
+    por, perm, near = args[POINT_ARGS:]
+    for groups, values in ((NEAR_GROUPS, near), (FAR_GROUPS, acc)):
+        for n, (field, deep) in enumerate(groups):
+            for side, row in ((0, deep), (1, ROWS - 1 - deep)):
+                first = n * 16 + side * 8
+                for half, col in HALVES:
+                    rows = pl.ds(half * (CELLS // 2) + row, LEVELS // 2, stride=ROWS)
+                    out[field, rows, :] = values[first : first + 8, col : col + COLS]
     lane = lax.broadcasted_iota(i32, (CELLS, COLS), 1)
     packed = jnp.zeros((CELLS, COLS), f32)
     for field in range(FIELDS):
         at, depth = Y_PLACE[field], Y_DEPTH[field]
-        own = sums[field] if field < 10 else (por if field == POR else perm)[...]
-        packed = jnp.where((lane >= at - depth) & (lane < at + depth), turn(own, at, 1), packed)
-    out[...] = packed
-
-
-def y_own(sums, por, perm):
+        values = out[field] if field < 10 else (por if field == POR else perm)[...]
+        mask = (lane >= at - depth) & (lane < at + depth)
+        packed = jnp.where(mask, turn(values, at, 1), packed)
+    own[...] = packed
+
+
+def group_call(kernel, groups, args, outs, copied, scratch, grant, name):
+    points = args[1].shape[1]
+    chunk = points // 2 if points % 256 == 0 else points
+    if copied:
+        scratch = [pltpu.VMEM(v.shape, v.dtype) for v in args] + scratch
+        scratch = scratch + [pltpu.SemaphoreType.DMA((len(args), points // chunk))]
+    space = pltpu.HBM if copied else pltpu.VMEM
     return pl.pallas_call(
-        y_own_kernel,
-        out_shape=jax.ShapeDtypeStruct((CELLS, COLS), f32),
-        cost_estimate=pl.CostEstimate(flops=4000000, bytes_accessed=900000, transcendentals=0),
-        compiler_params=pltpu.CompilerParams(vmem_limit_bytes=8 << 20),
-        name="y_own",
-    )(sums, por, perm)
+        functools.partial(kernel, chunk),
+        in_specs=[pl.BlockSpec(memory_space=space)] * len(args),
+        out_shape=[jax.ShapeDtypeStruct(shape, f32) for shape in outs],
+        scratch_shapes=scratch,
+        compiler_params=pltpu.CompilerParams(vmem_limit_bytes=grant << 20),
+        cost_estimate=pl.CostEstimate(
+            flops=2 * 24 * len(groups) * 256 * points, bytes_accessed=64 * points, transcendentals=0
+        ),
+        name=name,
+    )(*args)
+
+
+def point_args(trial, mean, cons, vel, wt, cell, flag, count):
+    row = lambda v: v.reshape(1, -1)
+    return (trial, row(mean), row(cons), vel, row(wt), row(cell), row(flag), count)
+
+
+def near_sums(points, por, perm):
+    acc = (16 * len(NEAR_GROUPS), 2 * COLS)
+    faces = (X_SENT, LEVELS, COLS)
+    outs = [acc, faces, faces]
+    args = (*points, por, perm)
+    return group_call(near_kernel, NEAR_GROUPS, args, outs, True, [], 56, "near_sums")
+
+
+def far_sums(points, por, perm, near):
+    acc = pltpu.VMEM((16 * len(FAR_GROUPS), 2 * COLS), f32)
+    outs = [(10, CELLS, COLS), (CELLS, COLS)]
+    args = (*points, por, perm, near)
+    return group_call(far_kernel, FAR_GROUPS, args, outs, False, [acc], 44, "far_sums")
 
 
 def with_rims(own, below, above):
@@ -642,7 +678,8 @@
 def shards(trial, mean, cons, vel, wt, cell, flag, count, por, perm):
     por = por.reshape(CELLS, COLS)
     perm = perm.reshape(CELLS, COLS)
-    sums, low, high = scatter(trial, mean, cons, vel, wt, cell, flag, count, por, perm)
+    points = point_args(trial, mean, cons, vel, wt, cell, flag, count)
+    near, low, high = near_sums(points, por, perm)
     above = shift_down(low, "gx")
     below = shift_up(high, "gx")
 
@@ -651,7 +688,7 @@
         return [(me > 0).astype(i32), (me < lax.axis_size(axis) - 1).astype(i32)]
 
     has = ends("gx") + ends("gy")
-    own = y_own(sums, por, perm)
+    sums, own = far_sums(points, por, perm, near)
     packs, y_low, y_high = neighbours(with_rims(own, below, above), "gy")
     where = jnp.stack(
         [jnp.asarray(v, i32) for v in [y_low, y_high] + has + [lax.axis_index("gz")]]

time: 46.9 us -> 43.6 us (0.930)
  waiting for transfers between devices: 5.08 us -> 0.01 us
  Pallas kernels: 20.2 us -> 22.1 us
    ppermute x1, waiting for transfers between devices: 4.01 us -> 0.01 us  [shift_down(): return lax.ppermute(block, axis, [(i + 1, i) for i in range(count - 1)])]
    pallas_call x2, Pallas kernels: 15.4 us -> 17.2 us  [group_call(): pl.pallas_call(functools.partial(kernel, chunk), in_specs=[pl.BlockSpec(m...]
    ppermute x1, waiting for transfers between devices: 1.07 us -> 0.01 us  [shift_up(): return lax.ppermute(block, axis, [(i, i + 1) for i in range(count - 1)])]
    unnamed x8 -> x20, local copies, waits for them, and re-layouts: 1.1 us -> 0.98 us
  transfers between devices with their start and end apart: 2 -> 2, of which waited for: 2 -> 0; matrix products, arithmetic and copies ran while one was open for 0% -> 0% of each run, Pallas kernels for 1% -> 19%
where the time goes in v5:
time: 43.6 us; the launch traced here: 43.3 us
  Pallas kernels  22.1 us (51%)
  blocking collectives  12.2 us (28%)
  starting transfers between devices  6.23 us (14%)
  between operations  1.52 us (3%)
  local copies, waits for them, and re-layouts  1.15 us (3%)
    pallas_call x2, Pallas kernels, group_call(): pl.pallas_call(functools.partial(kernel, chunk), in_specs=[pl.BlockSpec(m...  17.2 us
    all_gather x1, blocking collectives, shards(): lax.all_gather(told, 'gz', axis=0)  7.26 us
    all_gather x1, blocking collectives, neighbours(): stacked = lax.all_gather(block, axis, axis=0)  4.94 us
    ppermute x1, starting transfers between devices, shift_up(): return lax.ppermute(block, axis, [(i, i + 1) for i in range(count - 1)])  4.94 us
    pallas_call x1, Pallas kernels, local_solve(): pl.pallas_call(local_kernel, in_specs=[smem] + [vmem] * 6, out_shape=[jax...  3.13 us
    pallas_call x1, Pallas kernels, final(): pl.pallas_call(functools.partial(final_kernel, told.shape[0]), in_specs=[...  1.72 us
    ppermute x1, starting transfers between devices, shift_down(): return lax.ppermute(block, axis, [(i + 1, i) for i in range(count - 1)])  1.29 us
    unnamed x20, local copies, waits for them, and re-layouts  0.98 us
  transfers between devices with their start and end apart: 2, of which 0 were waited for; matrix products, arithmetic and copies ran while one was open for 0% of the time, Pallas kernels for 19%

profile of v5, /device:TPU:0, one launch (start us, length us, event | category | flops | bytes accessed | tf_op | source)
XLA Modules:
  0.0 43.3 jit_solution(9915472426485895807)
XLA Ops:
  1.3 0.0 copy-start
  1.3 0.0 copy-start.1
  1.3 0.0 copy-start.2
  1.3 0.0 copy-start.3
  1.3 0.0 copy-start.4
  1.3 0.0 copy-start.5
  1.3 0.0 copy-start.6
  1.3 0.0 copy-start.7
  1.4 0.0 copy-start.8
  1.4 8.8 %near_sums.1 = (f32[256,256]{1,0:T(8,128)}, f32[21,16,128]{2,1,0:T(8,128)}, f32[21,16,128]{2,1,0:T(8,128)}) custom-call(f32[6,24576]{1,0:T(8,128)} %refs_0_.3, f32[1,24576]{1,0:T(1,128)} %bitcast.28, f32[1,24576]{1,0:T(1,128)} %bitcast.30, f32[3,24576]{1,0:T(4,128)} %refs_3_.3, f32[1,24576]{1,0:T(1,128)} %bitcast.32, s32[1,24576]{1,0:T(1,128)} %bitcast.34, ...), custom_call_target="tpu_custom_call" | custom-call | flops 4831838208 | bytes 1572864 | tf_op jit(solution)/shard_map/near_sums/pallas_call | solution.py:221
  10.2 4.9 %collective-permute-start = (f32[21,16,128]{2,1,0:T(8,128)}, f32[21,16,128]{2,1,0:T(8,128)S(1)}, u32[]{:S(2)}, u32[]{:S(2)}) collective-permute-start(f32[21,16,128]{2,1,0:T(8,128)} %get-tuple-element.14), channel_id=1, source_target_pairs={{0,8},{8,16},{16,24},{1,9},{9,17},{17,25},{2,10},{10,18},{18,26},{... | collective-permute-start | bytes 516104 | tf_op jit(solution)/shard_map/ppermute | solution.py:662
  15.1 1.3 %collective-permute-start.1 = (f32[21,16,128]{2,1,0:T(8,128)}, f32[21,16,128]{2,1,0:T(8,128)S(1)}, u32[]{:S(2)}, u32[]{:S(2)}) collective-permute-start(f32[21,16,128]{2,1,0:T(8,128)} %get-tuple-element.15), channel_id=1, source_target_pairs={{8,0},{16,8},{24,16},{9,1},{17,9},{25,17},{10,2},{18,10},{26,18},{... | collective-permute-start | bytes 516104 | tf_op jit(solution)/shard_map/ppermute | solution.py:667
  16.4 0.0 copy-done
  16.5 0.9 %copy-done.9 = f32[256,256]{1,0:T(8,128)S(1)} copy-done((f32[256,256]{1,0:T(8,128)S(1)}, f32[256,256]{1,0:T(8,128)}, u32[]{:S(2)}) %copy-start.9) | copy-done | bytes 262168
  17.5 8.4 %far_sums.1 = (f32[10,128,128]{2,1,0:T(8,128)S(1)}, f32[128,128]{1,0:T(8,128)S(1)}) custom-call(f32[6,24576]{1,0:T(8,128)S(1)} %copy-done.2, f32[1,24576]{1,0:T(1,128)S(1)} %bitcast.29, f32[1,24576]{1,0:T(1,128)S(1)} %bitcast.31, f32[3,24576]{1,0:T(4,128)S(1)} %copy-done.3, f32[1,24576]{1,0:T(1,128)S(1)} %bitcast.33, s32[1,24576]{1,0:T(1,128)S(1)} %bitcast.35, ...), custom_call_target="tpu_custom_call" | custom-call | flops 7247757312 | bytes 1572864 | tf_op jit(solution)/shard_map/far_sums/pallas_call | solution.py:221
  25.9 0.1 pad.1.clone
  26.0 0.1 stack.47.where
  26.1 0.0 collective-permute-done.below
  26.1 0.0 collective-permute-done.1.above
  26.1 0.1 maximum_add_fusion
  26.2 4.9 %all-gather = f32[256,128]{1,0:T(8,128)S(1)} all-gather(f32[128,128]{1,0:T(8,128)S(1)} %maximum_add_fusion), channel_id=2, replica_groups=mesh['gx'=4,'gy'=2,'gz'=4] {'gy'}, dimensions={0}, use_global_device_ids=true | all-gather | bytes 196608 | tf_op jit(solution)/shard_map/all_gather | solution.py:674
  31.1 3.1 %local_solve.1 = (f32[3,128,128]{2,1,0:T(8,128)S(1)}, f32[3,3,14,8,128]{4,3,2,1,0:T(8,128)S(1)}, f32[264,128]{1,0:T(8,128)S(1)}) custom-call(s32[7]{0:T(128)S(1)} %stack.47.where, f32[10,128,128]{2,1,0:T(8,128)S(1)} %get-tuple-element.13.sums, f32[128,128]{1,0:T(8,128)S(1)} %bitcast.24, f32[128,128]{1,0:T(8,128)S(1)} %bitcast.27, ...), custom_call_target="tpu_custom_call" | custom-call | tf_op jit(solution)/shard_map/local_solve/pallas_call | solution.py:487
  34.3 7.3 %all-gather.1 = f32[1056,128]{1,0:T(8,128)S(1)} all-gather(f32[264,128]{1,0:T(8,128)S(1)} %get-tuple-element.19), channel_id=3, replica_groups=mesh['gx'=4,'gy'=2,'gz'=4] {'gz'}, dimensions={0}, use_global_device_ids=true | all-gather | bytes 675840 | tf_op jit(solution)/shard_map/all_gather | solution.py:697
  41.5 1.7 %final.1 = (f32[3,128,128]{2,1,0:T(8,128)}, f32[128,128]{1,0:T(8,128)}) custom-call(s32[7]{0:T(128)S(1)} %stack.47.where, f32[3,128,128]{2,1,0:T(8,128)S(1)} %get-tuple-element.17.vel, f32[3,3,14,8,128]{4,3,2,1,0:T(8,128)S(1)} %get-tuple-element.18.inner, f32[4,264,128]{2,1,0:T(8,128)S(1)} %bitcast.20), custom_call_target="tpu_custom_call" | custom-call | tf_op jit(solution)/shard_map/final/pallas_call | solution.py:648
  (12 shorter events, 0.0 us)
Async XLA Ops:
  1.3 15.1 %copy-start = (f32[16,8,128]{2,1,0:T(8,128)S(1)}, f32[16,8,128]{2,1,0:T(8,128)}, u32[]{:S(2)}) copy-start(f32[16,8,128]{2,1,0:T(8,128)} %param.18) | copy-start | bytes 196612
  1.3 15.1 %copy-start.1 = (f32[16,8,128]{2,1,0:T(8,128)S(1)}, f32[16,8,128]{2,1,0:T(8,128)}, u32[]{:S(2)}) copy-start(f32[16,8,128]{2,1,0:T(8,128)} %param.19) | copy-start | bytes 196612
  1.3 15.1 %copy-start.2 = (f32[6,24576]{1,0:T(8,128)S(1)}, f32[6,24576]{1,0:T(8,128)}, u32[]{:S(2)}) copy-start(f32[6,24576]{1,0:T(8,128)} %refs_0_.3) | copy-start | bytes 1769476
  1.3 15.1 %copy-start.3 = (f32[3,24576]{1,0:T(4,128)S(1)}, f32[3,24576]{1,0:T(4,128)}, u32[]{:S(2)}) copy-start(f32[3,24576]{1,0:T(4,128)} %refs_3_.3) | copy-start | bytes 884740
  1.3 15.1 %copy-start.4 = (f32[24576]{0:T(1024)S(1)}, f32[24576]{0:T(1024)}, u32[]{:S(2)}) copy-start(f32[24576]{0:T(1024)} %param.11) | copy-start | bytes 294916
  1.3 15.1 %copy-start.5 = (f32[24576]{0:T(1024)S(1)}, f32[24576]{0:T(1024)}, u32[]{:S(2)}) copy-start(f32[24576]{0:T(1024)} %param.12) | copy-start | bytes 294916
  1.3 15.1 %copy-start.6 = (f32[24576]{0:T(1024)S(1)}, f32[24576]{0:T(1024)}, u32[]{:S(2)}) copy-start(f32[24576]{0:T(1024)} %param.14) | copy-start | bytes 294916
  1.3 15.1 %copy-start.7 = (s32[24576]{0:T(1024)S(1)}, s32[24576]{0:T(1024)}, u32[]{:S(2)}) copy-start(s32[24576]{0:T(1024)} %param.15) | copy-start | bytes 294916
  1.4 15.1 %copy-start.8 = (s32[24576]{0:T(1024)S(1)}, s32[24576]{0:T(1024)}, u32[]{:S(2)}) copy-start(s32[24576]{0:T(1024)} %param.16) | copy-start | bytes 294916
  10.2 15.9 %collective-permute-start = (f32[21,16,128]{2,1,0:T(8,128)}, f32[21,16,128]{2,1,0:T(8,128)S(1)}, u32[]{:S(2)}, u32[]{:S(2)}) collective-permute-start(f32[21,16,128]{2,1,0:T(8,128)} %get-tuple-element.14), channel_id=1, source_target_pairs={{0,8},{8,16},{16,24},{1,9},{9,17},{17,25},{2,10},{10,18},{18,26},{... | collective-permute-start | bytes 516104 | tf_op jit(solution)/shard_map/ppermute | solution.py:662
  15.1 11.0 %collective-permute-start.1 = (f32[21,16,128]{2,1,0:T(8,128)}, f32[21,16,128]{2,1,0:T(8,128)S(1)}, u32[]{:S(2)}, u32[]{:S(2)}) collective-permute-start(f32[21,16,128]{2,1,0:T(8,128)} %get-tuple-element.15), channel_id=1, source_target_pairs={{8,0},{16,8},{24,16},{9,1},{17,9},{25,17},{10,2},{18,10},{26,18},{... | collective-permute-start | bytes 516104 | tf_op jit(solution)/shard_map/ppermute | solution.py:667
  16.5 1.0 %copy-start.9 = (f32[256,256]{1,0:T(8,128)S(1)}, f32[256,256]{1,0:T(8,128)}, u32[]{:S(2)}) copy-start(f32[256,256]{1,0:T(8,128)} %get-tuple-element.12.refs_10_) | copy-start | bytes 786436

commit v6 on v5

--- a/solution.py
+++ b/solution.py
@@ -191,10 +191,12 @@
 
 
 def far_kernel(chunk, *refs):
-    args, out, own, acc = refs[:11], *refs[11:]
+    args, acc = refs[:POINT_ARGS], refs[POINT_ARGS]
     group_sums(chunk, FAR_GROUPS, args, acc)
-    por, perm, near = args[POINT_ARGS:]
-    for groups, values in ((NEAR_GROUPS, near), (FAR_GROUPS, acc)):
+
+
+def assemble_kernel(near, far, por, perm, out, own):
+    for groups, values in ((NEAR_GROUPS, near), (FAR_GROUPS, far)):
         for n, (field, deep) in enumerate(groups):
             for side, row in ((0, deep), (1, ROWS - 1 - deep)):
                 first = n * 16 + side * 8
@@ -209,6 +211,19 @@
         mask = (lane >= at - depth) & (lane < at + depth)
         packed = jnp.where(mask, turn(values, at, 1), packed)
     own[...] = packed
+
+
+def assemble(near, far, por, perm):
+    return pl.pallas_call(
+        assemble_kernel,
+        out_shape=[
+            jax.ShapeDtypeStruct((10, CELLS, COLS), f32),
+            jax.ShapeDtypeStruct((CELLS, COLS), f32),
+        ],
+        compiler_params=pltpu.CompilerParams(vmem_limit_bytes=8 << 20),
+        cost_estimate=pl.CostEstimate(flops=4000000, bytes_accessed=1500000, transcendentals=0),
+        name="assemble",
+    )(near, far, por, perm)
 
 
 def group_call(kernel, groups, args, outs, copied, scratch, grant, name):
@@ -244,11 +259,9 @@
     return group_call(near_kernel, NEAR_GROUPS, args, outs, True, [], 56, "near_sums")
 
 
-def far_sums(points, por, perm, near):
-    acc = pltpu.VMEM((16 * len(FAR_GROUPS), 2 * COLS), f32)
-    outs = [(10, CELLS, COLS), (CELLS, COLS)]
-    args = (*points, por, perm, near)
-    return group_call(far_kernel, FAR_GROUPS, args, outs, False, [acc], 44, "far_sums")
+def far_sums(points):
+    outs = [(16 * len(FAR_GROUPS), 2 * COLS)]
+    return group_call(far_kernel, FAR_GROUPS, points, outs, False, [], 44, "far_sums")[0]
 
 
 def with_rims(own, below, above):
@@ -337,7 +350,9 @@
         rows = pl.ds(level * ROWS, ROWS)
         at = Y_PLACE[field]
         own = sums[field, rows, :] if field < 10 else (por if field == POR else perm)[rows, :]
-        lanes = met(where, packs, from_above, rows)
+        if level not in merged:
+            merged[level] = met(where, packs, from_above, rows)
+        lanes = merged[level]
         return [
             own,
             rim[field, rows, :],
@@ -345,7 +360,7 @@
             turn(corner[rows, :], -at - HALF, 1),
         ]
 
-    memo = {}
+    memo, merged = {}, {}
 
     def get(field, level):
         if not 0 <= level < LEVELS:
@@ -688,7 +703,7 @@
         return [(me > 0).astype(i32), (me < lax.axis_size(axis) - 1).astype(i32)]
 
     has = ends("gx") + ends("gy")
-    sums, own = far_sums(points, por, perm, near)
+    sums, own = assemble(near, far_sums(points), por, perm)
     packs, y_low, y_high = neighbours(with_rims(own, below, above), "gy")
     where = jnp.stack(
         [jnp.asarray(v, i32) for v in [y_low, y_high] + has + [lax.axis_index("gz")]]

time: 43.6 us -> 42.8 us (0.982)
  local copies, waits for them, and re-layouts: 1.15 us -> 0.22 us
    unnamed x20, local copies, waits for them, and re-layouts: 0.98 us -> 0.05 us
  transfers between devices with their start and end apart: 2 -> 2, of which waited for: 0 -> 0; matrix products, arithmetic and copies ran while one was open for 0% -> 0% of each run, Pallas kernels for 19% -> 20%
where the time goes in v6:
time: 42.8 us; the launch traced here: 42.5 us
  Pallas kernels  22.1 us (52%)
  blocking collectives  12.2 us (29%)
  starting transfers between devices  6.36 us (15%)
  between operations  1.54 us (4%)
    pallas_call x2, Pallas kernels, group_call(): pl.pallas_call(functools.partial(kernel, chunk), in_specs=[pl.BlockSpec(m...  16.9 us
    all_gather x1, blocking collectives, shards(): lax.all_gather(told, 'gz', axis=0)  7.26 us
    all_gather x1, blocking collectives, neighbours(): stacked = lax.all_gather(block, axis, axis=0)  4.94 us
    ppermute x1, starting transfers between devices, shift_up(): return lax.ppermute(block, axis, [(i, i + 1) for i in range(count - 1)])  4.94 us
    pallas_call x1, Pallas kernels, local_solve(): pl.pallas_call(local_kernel, in_specs=[smem] + [vmem] * 6, out_shape=[jax...  3.14 us
    pallas_call x1, Pallas kernels, final(): pl.pallas_call(functools.partial(final_kernel, told.shape[0]), in_specs=[...  1.72 us
    ppermute x1, starting transfers between devices, shift_down(): return lax.ppermute(block, axis, [(i + 1, i) for i in range(count - 1)])  1.42 us
  transfers between devices with their start and end apart: 2, of which 0 were waited for; matrix products, arithmetic and copies ran while one was open for 0% of the time, Pallas kernels for 20%

profile of v6, /device:TPU:0, one launch (start us, length us, event | category | flops | bytes accessed | tf_op | source)
XLA Modules:
  0.0 42.5 jit_solution(14482238483683476840)
XLA Ops:
  1.3 0.0 copy-start.3
  1.3 0.0 copy-start.4
  1.3 0.0 copy-start.5
  1.3 0.0 copy-start.6
  1.3 0.0 copy-start.7
  1.3 0.0 copy-start.8
  1.3 8.8 %near_sums.1 = (f32[256,256]{1,0:T(8,128)}, f32[21,16,128]{2,1,0:T(8,128)}, f32[21,16,128]{2,1,0:T(8,128)}) custom-call(f32[6,24576]{1,0:T(8,128)} %refs_0_.3, f32[1,24576]{1,0:T(1,128)} %bitcast.28, f32[1,24576]{1,0:T(1,128)} %bitcast.30, f32[3,24576]{1,0:T(4,128)} %refs_3_.3, f32[1,24576]{1,0:T(1,128)} %bitcast.32, s32[1,24576]{1,0:T(1,128)} %bitcast.34, ...), custom_call_target="tpu_custom_call" | custom-call | flops 4831838208 | bytes 1572864 | tf_op jit(solution)/shard_map/near_sums/pallas_call | solution.py:236
  10.1 4.9 %collective-permute-start = (f32[21,16,128]{2,1,0:T(8,128)}, f32[21,16,128]{2,1,0:T(8,128)S(1)}, u32[]{:S(2)}, u32[]{:S(2)}) collective-permute-start(f32[21,16,128]{2,1,0:T(8,128)} %get-tuple-element.14), channel_id=1, source_target_pairs={{0,8},{8,16},{16,24},{1,9},{9,17},{17,25},{2,10},{10,18},{18,26},{... | collective-permute-start | bytes 516104 | tf_op jit(solution)/shard_map/ppermute | solution.py:677
  15.1 0.0 copy-start
  15.1 1.4 %collective-permute-start.1 = (f32[21,16,128]{2,1,0:T(8,128)}, f32[21,16,128]{2,1,0:T(8,128)S(1)}, u32[]{:S(2)}, u32[]{:S(2)}) collective-permute-start(f32[21,16,128]{2,1,0:T(8,128)} %get-tuple-element.15), channel_id=1, source_target_pairs={{8,0},{16,8},{24,16},{9,1},{17,9},{25,17},{10,2},{18,10},{26,18},{... | collective-permute-start | bytes 516104 | tf_op jit(solution)/shard_map/ppermute | solution.py:682
  16.6 0.0 copy-start.1
  16.6 0.0 copy-start.2
  16.6 8.1 %far_sums.1.far = f32[384,256]{1,0:T(8,128)S(1)} custom-call(f32[6,24576]{1,0:T(8,128)S(1)} %copy-done.3, f32[1,24576]{1,0:T(1,128)S(1)} %bitcast.29, f32[1,24576]{1,0:T(1,128)S(1)} %bitcast.31, f32[3,24576]{1,0:T(4,128)S(1)} %copy-done.4, f32[1,24576]{1,0:T(1,128)S(1)} %bitcast.33, s32[1,24576]{1,0:T(1,128)S(1)} %bitcast.35, s32[1,24576]{1,0:T(1,128)S(1)} %bitcast.37, ...), custom_call_target="tpu_custom_call" | custom-call | flops 7247757312 | bytes 1572864 | tf_op jit(solution)/shard_map/far_sums/pallas_call | solution.py:236
  24.8 0.1 pad.1.clone
  24.9 0.1 stack.47.where
  25.0 0.0 copy-done.1
  25.0 0.3 assemble.1
  25.3 0.0 collective-permute-done.below
  25.3 0.0 collective-permute-done.1.above
  25.3 0.1 maximum_add_fusion
  25.4 4.9 %all-gather = f32[256,128]{1,0:T(8,128)S(1)} all-gather(f32[128,128]{1,0:T(8,128)S(1)} %maximum_add_fusion), channel_id=2, replica_groups=mesh['gx'=4,'gy'=2,'gz'=4] {'gy'}, dimensions={0}, use_global_device_ids=true | all-gather | bytes 196608 | tf_op jit(solution)/shard_map/all_gather | solution.py:689
  30.4 3.1 %local_solve.1 = (f32[3,128,128]{2,1,0:T(8,128)S(1)}, f32[3,3,14,8,128]{4,3,2,1,0:T(8,128)S(1)}, f32[264,128]{1,0:T(8,128)S(1)}) custom-call(s32[7]{0:T(128)S(1)} %stack.47.where, f32[10,128,128]{2,1,0:T(8,128)S(1)} %get-tuple-element.13.sums, f32[128,128]{1,0:T(8,128)S(1)} %bitcast.24, f32[128,128]{1,0:T(8,128)S(1)} %bitcast.27, ...), custom_call_target="tpu_custom_call" | custom-call | tf_op jit(solution)/shard_map/local_solve/pallas_call | solution.py:502
  33.5 7.3 %all-gather.1 = f32[1056,128]{1,0:T(8,128)S(1)} all-gather(f32[264,128]{1,0:T(8,128)S(1)} %get-tuple-element.19), channel_id=3, replica_groups=mesh['gx'=4,'gy'=2,'gz'=4] {'gz'}, dimensions={0}, use_global_device_ids=true | all-gather | bytes 675840 | tf_op jit(solution)/shard_map/all_gather | solution.py:712
  40.8 1.7 %final.1 = (f32[3,128,128]{2,1,0:T(8,128)}, f32[128,128]{1,0:T(8,128)}) custom-call(s32[7]{0:T(128)S(1)} %stack.47.where, f32[3,128,128]{2,1,0:T(8,128)S(1)} %get-tuple-element.17.vel, f32[3,3,14,8,128]{4,3,2,1,0:T(8,128)S(1)} %get-tuple-element.18.inner, f32[4,264,128]{2,1,0:T(8,128)S(1)} %bitcast.20), custom_call_target="tpu_custom_call" | custom-call | tf_op jit(solution)/shard_map/final/pallas_call | solution.py:663
  (13 shorter events, 0.0 us)
Async XLA Ops:
  1.3 15.2 %copy-start.3 = (f32[6,24576]{1,0:T(8,128)S(1)}, f32[6,24576]{1,0:T(8,128)}, u32[]{:S(2)}) copy-start(f32[6,24576]{1,0:T(8,128)} %refs_0_.3) | copy-start | bytes 1769476
  1.3 15.2 %copy-start.4 = (f32[3,24576]{1,0:T(4,128)S(1)}, f32[3,24576]{1,0:T(4,128)}, u32[]{:S(2)}) copy-start(f32[3,24576]{1,0:T(4,128)} %refs_3_.3) | copy-start | bytes 884740
  1.3 15.2 %copy-start.5 = (f32[24576]{0:T(1024)S(1)}, f32[24576]{0:T(1024)}, u32[]{:S(2)}) copy-start(f32[24576]{0:T(1024)} %param.11) | copy-start | bytes 294916
  1.3 15.2 %copy-start.6 = (f32[24576]{0:T(1024)S(1)}, f32[24576]{0:T(1024)}, u32[]{:S(2)}) copy-start(f32[24576]{0:T(1024)} %param.12) | copy-start | bytes 294916
  1.3 15.2 %copy-start.7 = (f32[24576]{0:T(1024)S(1)}, f32[24576]{0:T(1024)}, u32[]{:S(2)}) copy-start(f32[24576]{0:T(1024)} %param.14) | copy-start | bytes 294916
  1.3 15.2 %copy-start.8 = (s32[24576]{0:T(1024)S(1)}, s32[24576]{0:T(1024)}, u32[]{:S(2)}) copy-start(s32[24576]{0:T(1024)} %param.15) | copy-start | bytes 294916
  1.3 15.2 %copy-start.9 = (s32[24576]{0:T(1024)S(1)}, s32[24576]{0:T(1024)}, u32[]{:S(2)}) copy-start(s32[24576]{0:T(1024)} %param.16) | copy-start | bytes 294916
  10.1 15.1 %collective-permute-start = (f32[21,16,128]{2,1,0:T(8,128)}, f32[21,16,128]{2,1,0:T(8,128)S(1)}, u32[]{:S(2)}, u32[]{:S(2)}) collective-permute-start(f32[21,16,128]{2,1,0:T(8,128)} %get-tuple-element.14), channel_id=1, source_target_pairs={{0,8},{8,16},{16,24},{1,9},{9,17},{17,25},{2,10},{10,18},{18,26},{... | collective-permute-start | bytes 516104 | tf_op jit(solution)/shard_map/ppermute | solution.py:677
  15.1 9.9 %copy-start = (f32[256,256]{1,0:T(8,128)S(1)}, f32[256,256]{1,0:T(8,128)}, u32[]{:S(2)}) copy-start(f32[256,256]{1,0:T(8,128)} %get-tuple-element.12.near) | copy-start | bytes 786436
  15.1 10.2 %collective-permute-start.1 = (f32[21,16,128]{2,1,0:T(8,128)}, f32[21,16,128]{2,1,0:T(8,128)S(1)}, u32[]{:S(2)}, u32[]{:S(2)}) collective-permute-start(f32[21,16,128]{2,1,0:T(8,128)} %get-tuple-element.15), channel_id=1, source_target_pairs={{8,0},{16,8},{24,16},{9,1},{17,9},{25,17},{10,2},{18,10},{26,18},{... | collective-permute-start | bytes 516104 | tf_op jit(solution)/shard_map/ppermute | solution.py:682
  16.6 8.4 %copy-start.1 = (f32[16,8,128]{2,1,0:T(8,128)S(1)}, f32[16,8,128]{2,1,0:T(8,128)}, u32[]{:S(2)}) copy-start(f32[16,8,128]{2,1,0:T(8,128)} %param.18) | copy-start | bytes 196612
  16.6 8.4 %copy-start.2 = (f32[16,8,128]{2,1,0:T(8,128)S(1)}, f32[16,8,128]{2,1,0:T(8,128)}, u32[]{:S(2)}) copy-start(f32[16,8,128]{2,1,0:T(8,128)} %param.19) | copy-start | bytes 196612

commit v7 on v6

--- a/solution.py
+++ b/solution.py
@@ -684,6 +684,8 @@
 
 def neighbours(block, axis):
     count, me = lax.axis_size(axis), lax.axis_index(axis)
+    if count == 2:
+        return lax.ppermute(block, axis, [(0, 1), (1, 0)])[None], 0, 0
     if count > 4:
         return jnp.stack([shift_up(block, axis), shift_down(block, axis)]), 0, 1
     stacked = lax.all_gather(block, axis, axis=0)

time: 42.8 us -> 42.1 us (0.984)
  blocking collectives: 12.2 us -> 7.26 us
  waiting for transfers between devices: 0.01 us -> 2.66 us
  starting transfers between devices: 6.36 us -> 7.94 us
    all_gather x1 -> x0, blocking collectives: 4.94 us -> none  [neighbours(): stacked = lax.all_gather(block, axis, axis=0)]
    ppermute x0 -> x1, waiting for transfers between devices: none -> 2.66 us  [neighbours(): return (lax.ppermute(block, axis, [(0, 1), (1, 0)])[None], 0, 0)]
    ppermute x0 -> x1, starting transfers between devices: none -> 1.58 us  [neighbours(): return (lax.ppermute(block, axis, [(0, 1), (1, 0)])[None], 0, 0)]
  transfers between devices with their start and end apart: 2 -> 3, of which waited for: 0 -> 1; matrix products, arithmetic and copies ran while one was open for 0% -> 0% of each run, Pallas kernels for 20% -> 20%
where the time goes in v7:
time: 42.1 us; the launch traced here: 41.8 us
  Pallas kernels  22.1 us (52%)
  starting transfers between devices  7.94 us (19%)
  blocking collectives  7.26 us (17%)
  waiting for transfers between devices  2.66 us (6%)
  between operations  1.51 us (4%)
    pallas_call x2, Pallas kernels, group_call(): pl.pallas_call(functools.partial(kernel, chunk), in_specs=[pl.BlockSpec(m...  16.9 us
    all_gather x1, blocking collectives, shards(): lax.all_gather(told, 'gz', axis=0)  7.26 us
    ppermute x1, starting transfers between devices, shift_up(): return lax.ppermute(block, axis, [(i, i + 1) for i in range(count - 1)])  4.94 us
    pallas_call x1, Pallas kernels, local_solve(): pl.pallas_call(local_kernel, in_specs=[smem] + [vmem] * 6, out_shape=[jax...  3.14 us
    ppermute x1, waiting for transfers between devices, neighbours(): return (lax.ppermute(block, axis, [(0, 1), (1, 0)])[None], 0, 0)  2.66 us
    pallas_call x1, Pallas kernels, final(): pl.pallas_call(functools.partial(final_kernel, told.shape[0]), in_specs=[...  1.72 us
    ppermute x1, starting transfers between devices, neighbours(): return (lax.ppermute(block, axis, [(0, 1), (1, 0)])[None], 0, 0)  1.58 us
    ppermute x1, starting transfers between devices, shift_down(): return lax.ppermute(block, axis, [(i + 1, i) for i in range(count - 1)])  1.42 us
  transfers between devices with their start and end apart: 3, of which 1 were waited for; matrix products, arithmetic and copies ran while one was open for 0% of the time, Pallas kernels for 20%

profile of v7, /device:TPU:0, one launch (start us, length us, event | category | flops | bytes accessed | tf_op | source)
XLA Modules:
  0.0 41.8 jit_solution(9003719565993056164)
XLA Ops:
  1.3 0.0 copy-start.3
  1.3 0.0 copy-start.4
  1.3 0.0 copy-start.5
  1.3 0.0 copy-start.6
  1.3 0.0 copy-start.7
  1.3 0.0 copy-start.8
  1.3 8.8 %near_sums.1 = (f32[256,256]{1,0:T(8,128)}, f32[21,16,128]{2,1,0:T(8,128)}, f32[21,16,128]{2,1,0:T(8,128)}) custom-call(f32[6,24576]{1,0:T(8,128)} %refs_0_.3, f32[1,24576]{1,0:T(1,128)} %bitcast.26, f32[1,24576]{1,0:T(1,128)} %bitcast.28, f32[3,24576]{1,0:T(4,128)} %refs_3_.3, f32[1,24576]{1,0:T(1,128)} %bitcast.30, s32[1,24576]{1,0:T(1,128)} %bitcast.32, ...), custom_call_target="tpu_custom_call" | custom-call | flops 4831838208 | bytes 1572864 | tf_op jit(solution)/shard_map/near_sums/pallas_call | solution.py:236
  10.1 4.9 %collective-permute-start = (f32[21,16,128]{2,1,0:T(8,128)}, f32[21,16,128]{2,1,0:T(8,128)S(1)}, u32[]{:S(2)}, u32[]{:S(2)}) collective-permute-start(f32[21,16,128]{2,1,0:T(8,128)} %get-tuple-element.14), channel_id=1, source_target_pairs={{0,8},{8,16},{16,24},{1,9},{9,17},{17,25},{2,10},{10,18},{18,26},{... | collective-permute-start | bytes 516104 | tf_op jit(solution)/shard_map/ppermute | solution.py:677
  15.1 0.0 copy-start.1
  15.1 0.0 copy-start.2
  15.1 1.4 %collective-permute-start.1 = (f32[21,16,128]{2,1,0:T(8,128)}, f32[21,16,128]{2,1,0:T(8,128)S(1)}, u32[]{:S(2)}, u32[]{:S(2)}) collective-permute-start(f32[21,16,128]{2,1,0:T(8,128)} %get-tuple-element.15), channel_id=1, source_target_pairs={{8,0},{16,8},{24,16},{9,1},{17,9},{25,17},{10,2},{18,10},{26,18},{... | collective-permute-start | bytes 516104 | tf_op jit(solution)/shard_map/ppermute | solution.py:682
  16.6 8.1 %far_sums.1.far = f32[384,256]{1,0:T(8,128)S(1)} custom-call(f32[6,24576]{1,0:T(8,128)S(1)} %copy-done.3, f32[1,24576]{1,0:T(1,128)S(1)} %bitcast.27, f32[1,24576]{1,0:T(1,128)S(1)} %bitcast.29, f32[3,24576]{1,0:T(4,128)S(1)} %copy-done.4, f32[1,24576]{1,0:T(1,128)S(1)} %bitcast.31, s32[1,24576]{1,0:T(1,128)S(1)} %bitcast.33, s32[1,24576]{1,0:T(1,128)S(1)} %bitcast.35, ...), custom_call_target="tpu_custom_call" | custom-call | flops 7247757312 | bytes 1572864 | tf_op jit(solution)/shard_map/far_sums/pallas_call | solution.py:236
  24.8 0.1 pad.1.clone
  24.9 0.0 copy-done
  24.9 0.3 assemble.1
  25.2 0.0 collective-permute-done.below
  25.2 0.0 collective-permute-done.1.above
  25.2 0.1 maximum_add_fusion
  25.3 1.6 %collective-permute-start.2 = (f32[128,128]{1,0:T(8,128)S(1)}, f32[128,128]{1,0:T(8,128)S(1)}, u32[]{:S(2)}, u32[]{:S(2)}) collective-permute-start(f32[128,128]{1,0:T(8,128)S(1)} %maximum_add_fusion), channel_id=1, source_target_pairs={{0,4},{4,0},{1,5},{5,1},{2,6},{6,2},{3,7},{7,3},{8,12},{12,8},{9,1... | collective-permute-start | bytes 196616 | tf_op jit(solution)/shard_map/ppermute | solution.py:688
  26.9 0.1 stack.39.where
  27.0 2.7 %collective-permute-done.2 = f32[128,128]{1,0:T(8,128)S(1)} collective-permute-done((f32[128,128]{1,0:T(8,128)S(1)}, f32[128,128]{1,0:T(8,128)S(1)}, u32[]{:S(2)}, u32[]{:S(2)}) %collective-permute-start.2) | collective-permute-done | bytes 65568 | tf_op jit(solution)/shard_map/ppermute | solution.py:688
  29.6 3.1 %local_solve.1 = (f32[3,128,128]{2,1,0:T(8,128)S(1)}, f32[3,3,14,8,128]{4,3,2,1,0:T(8,128)S(1)}, f32[264,128]{1,0:T(8,128)S(1)}) custom-call(s32[7]{0:T(128)S(1)} %stack.39.where, f32[10,128,128]{2,1,0:T(8,128)S(1)} %get-tuple-element.13.sums, f32[128,128]{1,0:T(8,128)S(1)} %bitcast.21, f32[128,128]{1,0:T(8,128)S(1)} %bitcast.24, ...), custom_call_target="tpu_custom_call" | custom-call | tf_op jit(solution)/shard_map/local_solve/pallas_call | solution.py:502
  32.8 7.3 %all-gather = f32[1056,128]{1,0:T(8,128)S(1)} all-gather(f32[264,128]{1,0:T(8,128)S(1)} %get-tuple-element.19), channel_id=2, replica_groups=mesh['gx'=4,'gy'=2,'gz'=4] {'gz'}, dimensions={0}, use_global_device_ids=true | all-gather | bytes 675840 | tf_op jit(solution)/shard_map/all_gather | solution.py:714
  40.0 1.7 %final.1 = (f32[3,128,128]{2,1,0:T(8,128)}, f32[128,128]{1,0:T(8,128)}) custom-call(s32[7]{0:T(128)S(1)} %stack.39.where, f32[3,128,128]{2,1,0:T(8,128)S(1)} %get-tuple-element.17.vel, f32[3,3,14,8,128]{4,3,2,1,0:T(8,128)S(1)} %get-tuple-element.18.inner, f32[4,264,128]{2,1,0:T(8,128)S(1)} %bitcast.18), custom_call_target="tpu_custom_call" | custom-call | tf_op jit(solution)/shard_map/final/pallas_call | solution.py:663
  (15 shorter events, 0.0 us)
Async XLA Ops:
  1.3 15.3 %copy-start.3 = (f32[6,24576]{1,0:T(8,128)S(1)}, f32[6,24576]{1,0:T(8,128)}, u32[]{:S(2)}) copy-start(f32[6,24576]{1,0:T(8,128)} %refs_0_.3) | copy-start | bytes 1769476
  1.3 15.3 %copy-start.4 = (f32[3,24576]{1,0:T(4,128)S(1)}, f32[3,24576]{1,0:T(4,128)}, u32[]{:S(2)}) copy-start(f32[3,24576]{1,0:T(4,128)} %refs_3_.3) | copy-start | bytes 884740
  1.3 15.3 %copy-start.5 = (f32[24576]{0:T(1024)S(1)}, f32[24576]{0:T(1024)}, u32[]{:S(2)}) copy-start(f32[24576]{0:T(1024)} %param.11) | copy-start | bytes 294916
  1.3 15.3 %copy-start.6 = (f32[24576]{0:T(1024)S(1)}, f32[24576]{0:T(1024)}, u32[]{:S(2)}) copy-start(f32[24576]{0:T(1024)} %param.12) | copy-start | bytes 294916
  1.3 15.3 %copy-start.7 = (f32[24576]{0:T(1024)S(1)}, f32[24576]{0:T(1024)}, u32[]{:S(2)}) copy-start(f32[24576]{0:T(1024)} %param.14) | copy-start | bytes 294916
  1.3 15.3 %copy-start.8 = (s32[24576]{0:T(1024)S(1)}, s32[24576]{0:T(1024)}, u32[]{:S(2)}) copy-start(s32[24576]{0:T(1024)} %param.15) | copy-start | bytes 294916
  1.3 15.3 %copy-start.9 = (s32[24576]{0:T(1024)S(1)}, s32[24576]{0:T(1024)}, u32[]{:S(2)}) copy-start(s32[24576]{0:T(1024)} %param.16) | copy-start | bytes 294916
  10.1 15.0 %collective-permute-start = (f32[21,16,128]{2,1,0:T(8,128)}, f32[21,16,128]{2,1,0:T(8,128)S(1)}, u32[]{:S(2)}, u32[]{:S(2)}) collective-permute-start(f32[21,16,128]{2,1,0:T(8,128)} %get-tuple-element.14), channel_id=1, source_target_pairs={{0,8},{8,16},{16,24},{1,9},{9,17},{17,25},{2,10},{10,18},{18,26},{... | collective-permute-start | bytes 516104 | tf_op jit(solution)/shard_map/ppermute | solution.py:677
  15.1 9.8 %copy-start = (f32[256,256]{1,0:T(8,128)S(1)}, f32[256,256]{1,0:T(8,128)}, u32[]{:S(2)}) copy-start(f32[256,256]{1,0:T(8,128)} %get-tuple-element.12.near) | copy-start | bytes 786436
  15.1 9.8 %copy-start.1 = (f32[16,8,128]{2,1,0:T(8,128)S(1)}, f32[16,8,128]{2,1,0:T(8,128)}, u32[]{:S(2)}) copy-start(f32[16,8,128]{2,1,0:T(8,128)} %param.18) | copy-start | bytes 196612
  15.1 9.8 %copy-start.2 = (f32[16,8,128]{2,1,0:T(8,128)S(1)}, f32[16,8,128]{2,1,0:T(8,128)}, u32[]{:S(2)}) copy-start(f32[16,8,128]{2,1,0:T(8,128)} %param.19) | copy-start | bytes 196612
  15.1 10.1 %collective-permute-start.1 = (f32[21,16,128]{2,1,0:T(8,128)}, f32[21,16,128]{2,1,0:T(8,128)S(1)}, u32[]{:S(2)}, u32[]{:S(2)}) collective-permute-start(f32[21,16,128]{2,1,0:T(8,128)} %get-tuple-element.15), channel_id=1, source_target_pairs={{8,0},{16,8},{24,16},{9,1},{17,9},{25,17},{10,2},{18,10},{26,18},{... | collective-permute-start | bytes 516104 | tf_op jit(solution)/shard_map/ppermute | solution.py:682
  25.3 4.3 %collective-permute-start.2 = (f32[128,128]{1,0:T(8,128)S(1)}, f32[128,128]{1,0:T(8,128)S(1)}, u32[]{:S(2)}, u32[]{:S(2)}) collective-permute-start(f32[128,128]{1,0:T(8,128)S(1)} %maximum_add_fusion), channel_id=1, source_target_pairs={{0,4},{4,0},{1,5},{5,1},{2,6},{6,2},{3,7},{7,3},{8,12},{12,8},{9,1... | collective-permute-start | bytes 196616 | tf_op jit(solution)/shard_map/ppermute | solution.py:688

commit v8 on v7

--- a/solution.py
+++ b/solution.py
@@ -331,11 +331,58 @@
     return in_x, in_y, in_x & in_y
 
 
-def local_kernel(where, sums, por, perm, below, above, packs, vel, inner, out, rim, corner):
+def partial_kernel(where, sums, por, perm, below, above, rim, parts, edges):
     rim[...] = jnp.zeros_like(rim)
     for q, (field, deep) in enumerate(X_ROWS):
         rim[field, pl.ds(deep, LEVELS, stride=ROWS), :] = above[q]
         rim[field, pl.ds(ROWS - 1 - deep, LEVELS, stride=ROWS), :] = below[q]
+    in_x = rim_masks(where)[0]
+    lane = tile_iota(1)
+    zero = jnp.zeros((ROWS, COLS), f32)
+
+    def get(field, level):
+        if not 0 <= level < LEVELS:
+            return [zero] * 2
+        rows = pl.ds(level * ROWS, ROWS)
+        return [sums[field, rows, :], rim[field, rows, :]]
+
+    for level in range(LEVELS):
+        rows = pl.ds(level * ROWS, ROWS)
+        mass = get(MASS, level)
+        parts[3, 0, rows, :] = 0.125 / jnp.maximum(mass[0], 0.5)
+        parts[3, 1, rows, :] = jnp.where(in_x, 0.125 / jnp.maximum(mass[1], 0.5), 0.0)
+        for n, (field, fx, fy, fz) in enumerate(
+            ((MX, XX, XY, ZX), (MY, XY, YY, YZ), (MZ, ZX, YZ, ZZ))
+        ):
+            in_rows = diff_x(*get(fx, level))
+            higher, lower, momentum = get(fz, level + 1), get(fz, level - 1), get(field, level)
+            for t, tile in enumerate(get(fy, level)):
+                up, down = turn(tile, -1, 1), turn(tile, 1, 1)
+                edges[n, t, rows, :] = jnp.where(lane == COLS - 1, up, down)
+                in_lanes = jnp.where(lane == COLS - 1, 0.0, up) - jnp.where(lane == 0, 0.0, down)
+                parts[n, t, rows, :] = (
+                    8.0 * momentum[t] + in_rows[t] + in_lanes + (higher[t] - lower[t])
+                )
+
+
+def partial_sums(where, sums, por, perm, below, above):
+    smem = pl.BlockSpec(memory_space=pltpu.SMEM)
+    vmem = pl.BlockSpec(memory_space=pltpu.VMEM)
+    return pl.pallas_call(
+        partial_kernel,
+        in_specs=[smem] + [vmem] * 5,
+        out_shape=[
+            jax.ShapeDtypeStruct((FIELDS, CELLS, COLS), f32),
+            jax.ShapeDtypeStruct((4, 2, CELLS, COLS), f32),
+            jax.ShapeDtypeStruct((3, 2, CELLS, COLS), f32),
+        ],
+        compiler_params=pltpu.CompilerParams(vmem_limit_bytes=16 << 20),
+        cost_estimate=pl.CostEstimate(flops=8000000, bytes_accessed=3000000, transcendentals=0),
+        name="partial_sums",
+    )(where, sums, por, perm, below, above)
+
+
+def local_kernel(where, sums, por, perm, rim, parts, edges, packs, vel, inner, out, corner):
     from_above = y_from_above((LEVELS, COLS))
     for slot in range(ROWS):
         rows = pl.ds(slot * LEVELS, LEVELS)
@@ -343,7 +390,6 @@
     from_above = y_from_above((ROWS, COLS))
     in_x, in_y, in_xy = rim_masks(where)
     in_rims = (in_x, in_y, in_xy)
-    inside = lambda t: t[:1] + [jnp.where(m, v, 0.0) for m, v in zip(in_rims, t[1:])]
     zero = jnp.zeros((ROWS, COLS), f32)
 
     def field_at(field, level):
@@ -369,22 +415,32 @@
             memo[field, level] = field_at(field, level)
         return memo[field, level]
 
+    lanes = tile_iota(1)
+    first_lane, last_lane = lanes == 0, lanes == COLS - 1
+
     def star(level):
-        weight = inside([0.125 / jnp.maximum(m, 0.5) for m in get(MASS, level)])
-        dz = lambda f: [u - d for u, d in zip(get(f, level + 1), get(f, level - 1))]
-        forces = (
-            (ext_x(get(XX, level)), ext_y(get(XY, level)), dz(ZX)),
-            (ext_x(get(XY, level)), ext_y(get(YY, level)), dz(YZ)),
-            (ext_x(get(ZX, level)), ext_y(get(YZ, level)), dz(ZZ)),
-        )
+        rows = pl.ds(level * ROWS, ROWS)
+        weight = [0.125 / jnp.maximum(m, 0.5) for m in get(MASS, level)[2:]]
+        weight = [jnp.where(m, w, 0.0) for m, w in zip(in_rims[1:], weight)]
+        weight = [parts[3, 0, rows, :], parts[3, 1, rows, :]] + weight
         found = []
-        for field, (fx, fy, fz) in zip((MX, MY, MZ), forces):
-            found.append(
-                [
-                    (8.0 * m + (fx[n] + fy[n] + fz[n])) * weight[n]
-                    for n, m in enumerate(get(field, level))
-                ]
-            )
+        for n, (field, fx, fy, fz) in enumerate(
+            ((MX, XX, XY, ZX), (MY, XY, YY, YZ), (MZ, ZX, YZ, ZZ))
+        ):
+            in_rows = diff_x(*get(fx, level)[2:])
+            higher, lower = get(fz, level + 1)[2:], get(fz, level - 1)[2:]
+            momentum = get(field, level)[2:]
+            own, outer = [], []
+            for t, packed in enumerate((merged[level], corner[rows, :])):
+                at = Y_PLACE[fy] + HALF * t
+                up, down = turn(packed, -at - 1, 1), turn(packed, 1 - at, 1)
+                beside = edges[n, t, rows, :]
+                reach = jnp.where(last_lane, up, 0.0) - jnp.where(first_lane, down, 0.0)
+                own.append((parts[n, t, rows, :] + reach) * weight[t])
+                in_lanes = jnp.where(last_lane, beside, up) - jnp.where(first_lane, beside, down)
+                total = 8.0 * momentum[t] + in_rows[t] + in_lanes + (higher[t] - lower[t])
+                outer.append(total * weight[2 + t])
+            found.append(own + outer)
         return found, weight
 
     def level_perm(level):
@@ -496,21 +552,21 @@
     out[MSG_Y : MSG_Y + 8, :] = y_part
 
 
-def local_solve(where, sums, por, perm, below, above, packs):
+def local_solve(where, sums, por, perm, rim, parts, edges, packs):
     smem = pl.BlockSpec(memory_space=pltpu.SMEM)
     vmem = pl.BlockSpec(memory_space=pltpu.VMEM)
     return pl.pallas_call(
         local_kernel,
-        in_specs=[smem] + [vmem] * 6,
+        in_specs=[smem] + [vmem] * 7,
         out_shape=[
             jax.ShapeDtypeStruct((3, CELLS, COLS), f32),
             jax.ShapeDtypeStruct((3, 3, LEVELS - 2, ROWS, COLS), f32),
             jax.ShapeDtypeStruct((MSG_ROWS, COLS), f32),
         ],
-        scratch_shapes=[pltpu.VMEM((FIELDS, CELLS, COLS), f32), pltpu.VMEM((CELLS, COLS), f32)],
+        scratch_shapes=[pltpu.VMEM((CELLS, COLS), f32)],
         compiler_params=pltpu.CompilerParams(vmem_limit_bytes=16 << 20),
         name="local_solve",
-    )(where, sums, por, perm, below, above, packs)
+    )(where, sums, por, perm, rim, parts, edges, packs)
 
 
 def final_kernel(layers, where, vel, inner, told, out, pressure):
@@ -710,7 +766,8 @@
     where = jnp.stack(
         [jnp.asarray(v, i32) for v in [y_low, y_high] + has + [lax.axis_index("gz")]]
     )
-    star, inner, told = local_solve(where, sums, por, perm, below, above, packs)
+    rim, parts, edges = partial_sums(where, sums, por, perm, below, above)
+    star, inner, told = local_solve(where, sums, por, perm, rim, parts, edges, packs)
     velocity, pressure = final(where, star, inner, lax.all_gather(told, "gz", axis=0))
     return (
         velocity.reshape(3, LEVELS, ROWS, COLS),

time: 42.1 us -> 40.5 us (0.962)
  waiting for transfers between devices: 2.66 us -> 1.78 us
  Pallas kernels: 22.1 us -> 21.3 us
    ppermute x1, waiting for transfers between devices: 2.66 us -> 1.77 us  [neighbours(): return (lax.ppermute(block, axis, [(0, 1), (1, 0)])[None], 0, 0)]
    pallas_call x1 -> x2, Pallas kernels: 3.14 us -> 2.39 us  [the longest x1 1.51 us: local_solve(): pl.pallas_call(local_kernel, in_specs=[smem] + [vmem] * 7, out_shape=[jax...]
  transfers between devices with their start and end apart: 3 -> 3, of which waited for: 1 -> 1; matrix products, arithmetic and copies ran while one was open for 0% -> 0% of each run, Pallas kernels for 20% -> 23%
where the time goes in v8:
time: 40.5 us; the launch traced here: 40.1 us
  Pallas kernels  21.3 us (53%)
  starting transfers between devices  7.95 us (20%)
  blocking collectives  7.26 us (18%)
  waiting for transfers between devices  1.78 us (4%)
  between operations  1.52 us (4%)
    pallas_call x2, Pallas kernels, group_call(): pl.pallas_call(functools.partial(kernel, chunk), in_specs=[pl.BlockSpec(m...  16.9 us
    all_gather x1, blocking collectives, shards(): lax.all_gather(told, 'gz', axis=0)  7.26 us
    ppermute x1, starting transfers between devices, shift_up(): return lax.ppermute(block, axis, [(i, i + 1) for i in range(count - 1)])  4.94 us
    ppermute x1, waiting for transfers between devices, neighbours(): return (lax.ppermute(block, axis, [(0, 1), (1, 0)])[None], 0, 0)  1.77 us
    pallas_call x1, Pallas kernels, final(): pl.pallas_call(functools.partial(final_kernel, told.shape[0]), in_specs=[...  1.72 us
    ppermute x1, starting transfers between devices, neighbours(): return (lax.ppermute(block, axis, [(0, 1), (1, 0)])[None], 0, 0)  1.59 us
    pallas_call x1, Pallas kernels, local_solve(): pl.pallas_call(local_kernel, in_specs=[smem] + [vmem] * 7, out_shape=[jax...  1.51 us
    ppermute x1, starting transfers between devices, shift_down(): return lax.ppermute(block, axis, [(i + 1, i) for i in range(count - 1)])  1.42 us
  transfers between devices with their start and end apart: 3, of which 1 were waited for; matrix products, arithmetic and copies ran while one was open for 0% of the time, Pallas kernels for 23%

profile of v8, /device:TPU:0, one launch (start us, length us, event | category | flops | bytes accessed | tf_op | source)
XLA Modules:
  0.0 40.1 jit_solution(4327522866698539049)
XLA Ops:
  1.3 0.0 copy-start.3
  1.3 0.0 copy-start.4
  1.3 0.0 copy-start.5
  1.3 8.8 %near_sums.1 = (f32[256,256]{1,0:T(8,128)}, f32[21,16,128]{2,1,0:T(8,128)}, f32[21,16,128]{2,1,0:T(8,128)}) custom-call(f32[6,24576]{1,0:T(8,128)} %refs_0_.3, f32[1,24576]{1,0:T(1,128)} %bitcast.28, f32[1,24576]{1,0:T(1,128)} %bitcast.30, f32[3,24576]{1,0:T(4,128)} %refs_3_.3, f32[1,24576]{1,0:T(1,128)} %bitcast.32, s32[1,24576]{1,0:T(1,128)} %bitcast.34, ...), custom_call_target="tpu_custom_call" | custom-call | flops 4831838208 | bytes 1572864 | tf_op jit(solution)/shard_map/near_sums/pallas_call | solution.py:236
  10.1 4.9 %collective-permute-start = (f32[21,16,128]{2,1,0:T(8,128)}, f32[21,16,128]{2,1,0:T(8,128)S(1)}, u32[]{:S(2)}, u32[]{:S(2)}) collective-permute-start(f32[21,16,128]{2,1,0:T(8,128)} %get-tuple-element.17), channel_id=1, source_target_pairs={{0,8},{8,16},{16,24},{1,9},{9,17},{17,25},{2,10},{10,18},{18,26},{... | collective-permute-start | bytes 516104 | tf_op jit(solution)/shard_map/ppermute | solution.py:733
  15.1 0.0 copy-start
  15.1 0.0 copy-start.1
  15.1 0.0 copy-start.2
  15.1 1.4 %collective-permute-start.1 = (f32[21,16,128]{2,1,0:T(8,128)}, f32[21,16,128]{2,1,0:T(8,128)S(1)}, u32[]{:S(2)}, u32[]{:S(2)}) collective-permute-start(f32[21,16,128]{2,1,0:T(8,128)} %get-tuple-element.18), channel_id=1, source_target_pairs={{8,0},{16,8},{24,16},{9,1},{17,9},{25,17},{10,2},{18,10},{26,18},{... | collective-permute-start | bytes 516104 | tf_op jit(solution)/shard_map/ppermute | solution.py:738
  16.6 8.1 %far_sums.1.far = f32[384,256]{1,0:T(8,128)S(1)} custom-call(f32[6,24576]{1,0:T(8,128)S(1)} %copy-done.3, f32[1,24576]{1,0:T(1,128)S(1)} %bitcast.29, f32[1,24576]{1,0:T(1,128)S(1)} %bitcast.31, f32[3,24576]{1,0:T(4,128)S(1)} %copy-done.4, f32[1,24576]{1,0:T(1,128)S(1)} %bitcast.33, s32[1,24576]{1,0:T(1,128)S(1)} %bitcast.35, s32[1,24576]{1,0:T(1,128)S(1)} %bitcast.37, ...), custom_call_target="tpu_custom_call" | custom-call | flops 7247757312 | bytes 1572864 | tf_op jit(solution)/shard_map/far_sums/pallas_call | solution.py:236
  24.8 0.1 pad.1.clone
  24.8 0.0 copy-done
  24.8 0.0 copy-done.2
  24.9 0.3 assemble.1
  25.2 0.0 collective-permute-done.below
  25.2 0.0 collective-permute-done.1.above
  25.2 0.1 maximum_add_fusion
  25.3 1.6 %collective-permute-start.2 = (f32[128,128]{1,0:T(8,128)S(1)}, f32[128,128]{1,0:T(8,128)S(1)}, u32[]{:S(2)}, u32[]{:S(2)}) collective-permute-start(f32[128,128]{1,0:T(8,128)S(1)} %maximum_add_fusion), channel_id=1, source_target_pairs={{0,4},{4,0},{1,5},{5,1},{2,6},{6,2},{3,7},{7,3},{8,12},{12,8},{9,1... | collective-permute-start | bytes 196616 | tf_op jit(solution)/shard_map/ppermute | solution.py:744
  26.9 0.1 stack.39.where
  27.0 0.9 %partial_sums.1 = (f32[12,128,128]{2,1,0:T(8,128)S(1)}, f32[4,2,128,128]{3,2,1,0:T(8,128)S(1)}, f32[3,2,128,128]{3,2,1,0:T(8,128)S(1)}) custom-call(s32[7]{0:T(128)S(1)} %stack.39.where, f32[10,128,128]{2,1,0:T(8,128)S(1)} %get-tuple-element.16.sums, f32[128,128]{1,0:T(8,128)S(1)} %bitcast.21, f32[128,128]{1,0:T(8,128)S(1)} %bitcast.25, ...), custom_call_target="tpu_custom_call" | custom-call | flops 8000000 | bytes 3000000 | tf_op jit(solution)/shard_map/partial_sums/pallas_call | solution.py:371
  27.9 1.8 %collective-permute-done.2 = f32[128,128]{1,0:T(8,128)S(1)} collective-permute-done((f32[128,128]{1,0:T(8,128)S(1)}, f32[128,128]{1,0:T(8,128)S(1)}, u32[]{:S(2)}, u32[]{:S(2)}) %collective-permute-start.2) | collective-permute-done | bytes 65568 | tf_op jit(solution)/shard_map/ppermute | solution.py:744
  29.6 1.5 %local_solve.1 = (f32[3,128,128]{2,1,0:T(8,128)S(1)}, f32[3,3,14,8,128]{4,3,2,1,0:T(8,128)S(1)}, f32[264,128]{1,0:T(8,128)S(1)}) custom-call(s32[7]{0:T(128)S(1)} %stack.39.where, f32[10,128,128]{2,1,0:T(8,128)S(1)} %get-tuple-element.16.sums, f32[128,128]{1,0:T(8,128)S(1)} %bitcast.22, f32[128,128]{1,0:T(8,128)S(1)} %bitcast.26, ...), custom_call_target="tpu_custom_call" | custom-call | tf_op jit(solution)/shard_map/local_solve/pallas_call | solution.py:558
  31.1 7.3 %all-gather = f32[1056,128]{1,0:T(8,128)S(1)} all-gather(f32[264,128]{1,0:T(8,128)S(1)} %get-tuple-element.25), channel_id=2, replica_groups=mesh['gx'=4,'gy'=2,'gz'=4] {'gz'}, dimensions={0}, use_global_device_ids=true | all-gather | bytes 675840 | tf_op jit(solution)/shard_map/all_gather | solution.py:771
  38.4 1.7 %final.1 = (f32[3,128,128]{2,1,0:T(8,128)}, f32[128,128]{1,0:T(8,128)}) custom-call(s32[7]{0:T(128)S(1)} %stack.39.where, f32[3,128,128]{2,1,0:T(8,128)S(1)} %get-tuple-element.23.vel, f32[3,3,14,8,128]{4,3,2,1,0:T(8,128)S(1)} %get-tuple-element.24.inner, f32[4,264,128]{2,1,0:T(8,128)S(1)} %bitcast.18), custom_call_target="tpu_custom_call" | custom-call | tf_op jit(solution)/shard_map/final/pallas_call | solution.py:719
  (16 shorter events, 0.0 us)
Async XLA Ops:
  1.3 15.3 %copy-start.3 = (f32[6,24576]{1,0:T(8,128)S(1)}, f32[6,24576]{1,0:T(8,128)}, u32[]{:S(2)}) copy-start(f32[6,24576]{1,0:T(8,128)} %refs_0_.3) | copy-start | bytes 1769476
  1.3 15.3 %copy-start.4 = (f32[3,24576]{1,0:T(4,128)S(1)}, f32[3,24576]{1,0:T(4,128)}, u32[]{:S(2)}) copy-start(f32[3,24576]{1,0:T(4,128)} %refs_3_.3) | copy-start | bytes 884740
  1.3 15.3 %copy-start.5 = (f32[24576]{0:T(1024)S(1)}, f32[24576]{0:T(1024)}, u32[]{:S(2)}) copy-start(f32[24576]{0:T(1024)} %param.11) | copy-start | bytes 294916
  1.3 15.3 %copy-start.6 = (f32[24576]{0:T(1024)S(1)}, f32[24576]{0:T(1024)}, u32[]{:S(2)}) copy-start(f32[24576]{0:T(1024)} %param.12) | copy-start | bytes 294916
  1.3 15.3 %copy-start.7 = (f32[24576]{0:T(1024)S(1)}, f32[24576]{0:T(1024)}, u32[]{:S(2)}) copy-start(f32[24576]{0:T(1024)} %param.14) | copy-start | bytes 294916
  1.3 15.3 %copy-start.8 = (s32[24576]{0:T(1024)S(1)}, s32[24576]{0:T(1024)}, u32[]{:S(2)}) copy-start(s32[24576]{0:T(1024)} %param.15) | copy-start | bytes 294916
  1.3 15.3 %copy-start.9 = (s32[24576]{0:T(1024)S(1)}, s32[24576]{0:T(1024)}, u32[]{:S(2)}) copy-start(s32[24576]{0:T(1024)} %param.16) | copy-start | bytes 294916
  10.1 15.0 %collective-permute-start = (f32[21,16,128]{2,1,0:T(8,128)}, f32[21,16,128]{2,1,0:T(8,128)S(1)}, u32[]{:S(2)}, u32[]{:S(2)}) collective-permute-start(f32[21,16,128]{2,1,0:T(8,128)} %get-tuple-element.17), channel_id=1, source_target_pairs={{0,8},{8,16},{16,24},{1,9},{9,17},{17,25},{2,10},{10,18},{18,26},{... | collective-permute-start | bytes 516104 | tf_op jit(solution)/shard_map/ppermute | solution.py:733
  15.1 9.8 %copy-start = (f32[16,8,128]{2,1,0:T(8,128)S(1)}, f32[16,8,128]{2,1,0:T(8,128)}, u32[]{:S(2)}) copy-start(f32[16,8,128]{2,1,0:T(8,128)} %param.18) | copy-start | bytes 196612
  15.1 9.8 %copy-start.1 = (f32[16,8,128]{2,1,0:T(8,128)S(1)}, f32[16,8,128]{2,1,0:T(8,128)}, u32[]{:S(2)}) copy-start(f32[16,8,128]{2,1,0:T(8,128)} %param.19) | copy-start | bytes 196612
  15.1 9.8 %copy-start.2 = (f32[256,256]{1,0:T(8,128)S(1)}, f32[256,256]{1,0:T(8,128)}, u32[]{:S(2)}) copy-start(f32[256,256]{1,0:T(8,128)} %get-tuple-element.15.near) | copy-start | bytes 786436
  15.1 10.1 %collective-permute-start.1 = (f32[21,16,128]{2,1,0:T(8,128)}, f32[21,16,128]{2,1,0:T(8,128)S(1)}, u32[]{:S(2)}, u32[]{:S(2)}) collective-permute-start(f32[21,16,128]{2,1,0:T(8,128)} %get-tuple-element.18), channel_id=1, source_target_pairs={{8,0},{16,8},{24,16},{9,1},{17,9},{25,17},{10,2},{18,10},{26,18},{... | collective-permute-start | bytes 516104 | tf_op jit(solution)/shard_map/ppermute | solution.py:738
  25.3 4.3 %collective-permute-start.2 = (f32[128,128]{1,0:T(8,128)S(1)}, f32[128,128]{1,0:T(8,128)S(1)}, u32[]{:S(2)}, u32[]{:S(2)}) collective-permute-start(f32[128,128]{1,0:T(8,128)S(1)} %maximum_add_fusion), channel_id=1, source_target_pairs={{0,4},{4,0},{1,5},{5,1},{2,6},{6,2},{3,7},{7,3},{8,12},{12,8},{9,1... | collective-permute-start | bytes 196616 | tf_op jit(solution)/shard_map/ppermute | solution.py:744

commit v9 on v8

--- a/solution.py
+++ b/solution.py
@@ -33,9 +33,9 @@
     Y_PLACE[_f] = _at + Y_DEPTH[_f]
     _at += 2 * Y_DEPTH[_f]
 HALF = 64
-FACE, MAIN, NEAR, FAR, RIGHT, SOURCE, ECHO, VELZ, STRESSZ = range(9)
+FACE, MAIN, NEAR, RIGHT, SOURCE, ECHO, VELZ, STRESSZ, FAR = range(9)
 WEIGHT, SHEARX, SHEARY = range(3)
-NARROW, WIDE = 18, 6
+NARROW, WIDE = 17, 6
 MSG_X = 8 * (NARROW + WIDE)
 MSG_X_WIDE = MSG_X + 8 * -(-NARROW // 4)
 MSG_Y = MSG_X_WIDE + 8 * -(-WIDE // 2)
@@ -515,12 +515,12 @@
         b, f, g = first_inner[t]
         echo = sources[1][t] * weights[0][t] / links[0][t]
         face = level_perm(0)[t]
-        mine = [face, mid + hi * f, hi * f, hi * g, r - hi * b, source, echo, first_star[t], stress[0][t]]
+        mine = [face, mid + hi * f, hi * f, r - hi * b, source, echo, first_star[t], stress[0][t], hi * g]
         lo, mid, _, r, source = terms[top][t]
         b, f, g = last_inner[t]
         echo = sources[top - 1][t] * weights[top][t] / links[top - 1][t]
         face = level_perm(top)[t]
-        mine += [face, mid + lo * g, lo * g, lo * f, r - lo * b, source, echo, stars[top][2][t], stress[1][t]]
+        mine += [face, mid + lo * g, lo * g, r - lo * b, source, echo, stars[top][2][t], stress[1][t]]
         narrow.append(mine)
     row, lane = tile_iota(0), tile_iota(1)
     x_parts = [zero] * -(-NARROW // 4)
@@ -643,7 +643,7 @@
                 gain.append((zero, zero, zero))
             sides.append((link, main, right))
         for side, (link, main, right) in enumerate(sides):
-            near, far = narrow(k, side, NEAR), narrow(k, side, FAR)
+            near, far = narrow(k, side, NEAR), narrow(k, 0, FAR)
             right = minus(right, plus(times(near, echo[side]), times(far, echo[1 - side])))
             inv = [1.0 / m for m in main]
             link = [-v * i for v, i in zip(link, inv)]

time: 40.5 us -> 40.4 us (level)
  no operation moved by 1% of the time
where the time goes in v9:
time: 40.4 us; the launch traced here: 40 us
  Pallas kernels  21.3 us (53%)
  starting transfers between devices  7.95 us (20%)
  blocking collectives  7.17 us (18%)
  waiting for transfers between devices  1.77 us (4%)
  between operations  1.52 us (4%)
    pallas_call x2, Pallas kernels, group_call(): pl.pallas_call(functools.partial(kernel, chunk), in_specs=[pl.BlockSpec(m...  16.9 us
    all_gather x1, blocking collectives, shards(): lax.all_gather(told, 'gz', axis=0)  7.17 us
    ppermute x1, starting transfers between devices, shift_up(): return lax.ppermute(block, axis, [(i, i + 1) for i in range(count - 1)])  4.94 us
    ppermute x1, waiting for transfers between devices, neighbours(): return (lax.ppermute(block, axis, [(0, 1), (1, 0)])[None], 0, 0)  1.76 us
    pallas_call x1, Pallas kernels, final(): pl.pallas_call(functools.partial(final_kernel, told.shape[0]), in_specs=[...  1.7 us
    ppermute x1, starting transfers between devices, neighbours(): return (lax.ppermute(block, axis, [(0, 1), (1, 0)])[None], 0, 0)  1.59 us
    pallas_call x1, Pallas kernels, local_solve(): pl.pallas_call(local_kernel, in_specs=[smem] + [vmem] * 7, out_shape=[jax...  1.52 us
    ppermute x1, starting transfers between devices, shift_down(): return lax.ppermute(block, axis, [(i + 1, i) for i in range(count - 1)])  1.42 us
  transfers between devices with their start and end apart: 3, of which 1 were waited for; matrix products, arithmetic and copies ran while one was open for 0% of the time, Pallas kernels for 23%

profile of v9, /device:TPU:0, one launch (start us, length us, event | category | flops | bytes accessed | tf_op | source)
XLA Modules:
  0.0 40.0 jit_solution(17742648237229289399)
XLA Ops:
  1.3 0.0 copy-start.3
  1.3 0.0 copy-start.4
  1.3 0.0 copy-start.5
  1.3 0.0 copy-start.6
  1.3 0.0 copy-start.7
  1.3 0.0 copy-start.8
  1.3 8.8 %near_sums.1 = (f32[256,256]{1,0:T(8,128)}, f32[21,16,128]{2,1,0:T(8,128)}, f32[21,16,128]{2,1,0:T(8,128)}) custom-call(f32[6,24576]{1,0:T(8,128)} %refs_0_.3, f32[1,24576]{1,0:T(1,128)} %bitcast.28, f32[1,24576]{1,0:T(1,128)} %bitcast.30, f32[3,24576]{1,0:T(4,128)} %refs_3_.3, f32[1,24576]{1,0:T(1,128)} %bitcast.32, s32[1,24576]{1,0:T(1,128)} %bitcast.34, ...), custom_call_target="tpu_custom_call" | custom-call | flops 4831838208 | bytes 1572864 | tf_op jit(solution)/shard_map/near_sums/pallas_call | solution.py:236
  10.1 4.9 %collective-permute-start = (f32[21,16,128]{2,1,0:T(8,128)}, f32[21,16,128]{2,1,0:T(8,128)S(1)}, u32[]{:S(2)}, u32[]{:S(2)}) collective-permute-start(f32[21,16,128]{2,1,0:T(8,128)} %get-tuple-element.17), channel_id=1, source_target_pairs={{0,8},{8,16},{16,24},{1,9},{9,17},{17,25},{2,10},{10,18},{18,26},{... | collective-permute-start | bytes 516104 | tf_op jit(solution)/shard_map/ppermute | solution.py:733
  15.1 0.0 copy-start
  15.1 0.0 copy-start.1
  15.1 1.4 %collective-permute-start.1 = (f32[21,16,128]{2,1,0:T(8,128)}, f32[21,16,128]{2,1,0:T(8,128)S(1)}, u32[]{:S(2)}, u32[]{:S(2)}) collective-permute-start(f32[21,16,128]{2,1,0:T(8,128)} %get-tuple-element.18), channel_id=1, source_target_pairs={{8,0},{16,8},{24,16},{9,1},{17,9},{25,17},{10,2},{18,10},{26,18},{... | collective-permute-start | bytes 516104 | tf_op jit(solution)/shard_map/ppermute | solution.py:738
  16.6 8.1 %far_sums.1.far = f32[384,256]{1,0:T(8,128)S(1)} custom-call(f32[6,24576]{1,0:T(8,128)S(1)} %copy-done.3, f32[1,24576]{1,0:T(1,128)S(1)} %bitcast.29, f32[1,24576]{1,0:T(1,128)S(1)} %bitcast.31, f32[3,24576]{1,0:T(4,128)S(1)} %copy-done.4, f32[1,24576]{1,0:T(1,128)S(1)} %bitcast.33, s32[1,24576]{1,0:T(1,128)S(1)} %bitcast.35, s32[1,24576]{1,0:T(1,128)S(1)} %bitcast.37, ...), custom_call_target="tpu_custom_call" | custom-call | flops 7247757312 | bytes 1572864 | tf_op jit(solution)/shard_map/far_sums/pallas_call | solution.py:236
  24.8 0.1 pad.1.clone
  24.9 0.3 assemble.1
  25.2 0.0 collective-permute-done.below
  25.2 0.0 collective-permute-done.1.above
  25.2 0.1 maximum_add_fusion
  25.3 1.6 %collective-permute-start.2 = (f32[128,128]{1,0:T(8,128)S(1)}, f32[128,128]{1,0:T(8,128)S(1)}, u32[]{:S(2)}, u32[]{:S(2)}) collective-permute-start(f32[128,128]{1,0:T(8,128)S(1)} %maximum_add_fusion), channel_id=1, source_target_pairs={{0,4},{4,0},{1,5},{5,1},{2,6},{6,2},{3,7},{7,3},{8,12},{12,8},{9,1... | collective-permute-start | bytes 196616 | tf_op jit(solution)/shard_map/ppermute | solution.py:744
  26.9 0.1 stack.39.where
  27.0 0.9 %partial_sums.1 = (f32[12,128,128]{2,1,0:T(8,128)S(1)}, f32[4,2,128,128]{3,2,1,0:T(8,128)S(1)}, f32[3,2,128,128]{3,2,1,0:T(8,128)S(1)}) custom-call(s32[7]{0:T(128)S(1)} %stack.39.where, f32[10,128,128]{2,1,0:T(8,128)S(1)} %get-tuple-element.16.sums, f32[128,128]{1,0:T(8,128)S(1)} %bitcast.21, f32[128,128]{1,0:T(8,128)S(1)} %bitcast.25, ...), custom_call_target="tpu_custom_call" | custom-call | flops 8000000 | bytes 3000000 | tf_op jit(solution)/shard_map/partial_sums/pallas_call | solution.py:371
  27.9 1.8 %collective-permute-done.2 = f32[128,128]{1,0:T(8,128)S(1)} collective-permute-done((f32[128,128]{1,0:T(8,128)S(1)}, f32[128,128]{1,0:T(8,128)S(1)}, u32[]{:S(2)}, u32[]{:S(2)}) %collective-permute-start.2) | collective-permute-done | bytes 65568 | tf_op jit(solution)/shard_map/ppermute | solution.py:744
  29.6 1.5 %local_solve.1 = (f32[3,128,128]{2,1,0:T(8,128)S(1)}, f32[3,3,14,8,128]{4,3,2,1,0:T(8,128)S(1)}, f32[256,128]{1,0:T(8,128)S(1)}) custom-call(s32[7]{0:T(128)S(1)} %stack.39.where, f32[10,128,128]{2,1,0:T(8,128)S(1)} %get-tuple-element.16.sums, f32[128,128]{1,0:T(8,128)S(1)} %bitcast.22, f32[128,128]{1,0:T(8,128)S(1)} %bitcast.26, ...), custom_call_target="tpu_custom_call" | custom-call | tf_op jit(solution)/shard_map/local_solve/pallas_call | solution.py:558
  31.2 7.2 %all-gather = f32[1024,128]{1,0:T(8,128)S(1)} all-gather(f32[256,128]{1,0:T(8,128)S(1)} %get-tuple-element.25), channel_id=2, replica_groups=mesh['gx'=4,'gy'=2,'gz'=4] {'gz'}, dimensions={0}, use_global_device_ids=true | all-gather | bytes 655360 | tf_op jit(solution)/shard_map/all_gather | solution.py:771
  38.3 1.7 %final.1 = (f32[3,128,128]{2,1,0:T(8,128)}, f32[128,128]{1,0:T(8,128)}) custom-call(s32[7]{0:T(128)S(1)} %stack.39.where, f32[3,128,128]{2,1,0:T(8,128)S(1)} %get-tuple-element.23.vel, f32[3,3,14,8,128]{4,3,2,1,0:T(8,128)S(1)} %get-tuple-element.24.inner, f32[4,256,128]{2,1,0:T(8,128)S(1)} %bitcast.18), custom_call_target="tpu_custom_call" | custom-call | tf_op jit(solution)/shard_map/final/pallas_call | solution.py:719
  (16 shorter events, 0.0 us)
Async XLA Ops:
  1.3 15.3 %copy-start.3 = (f32[6,24576]{1,0:T(8,128)S(1)}, f32[6,24576]{1,0:T(8,128)}, u32[]{:S(2)}) copy-start(f32[6,24576]{1,0:T(8,128)} %refs_0_.3) | copy-start | bytes 1769476
  1.3 15.3 %copy-start.4 = (f32[3,24576]{1,0:T(4,128)S(1)}, f32[3,24576]{1,0:T(4,128)}, u32[]{:S(2)}) copy-start(f32[3,24576]{1,0:T(4,128)} %refs_3_.3) | copy-start | bytes 884740
  1.3 15.3 %copy-start.5 = (f32[24576]{0:T(1024)S(1)}, f32[24576]{0:T(1024)}, u32[]{:S(2)}) copy-start(f32[24576]{0:T(1024)} %param.11) | copy-start | bytes 294916
  1.3 15.3 %copy-start.6 = (f32[24576]{0:T(1024)S(1)}, f32[24576]{0:T(1024)}, u32[]{:S(2)}) copy-start(f32[24576]{0:T(1024)} %param.12) | copy-start | bytes 294916
  1.3 15.3 %copy-start.7 = (f32[24576]{0:T(1024)S(1)}, f32[24576]{0:T(1024)}, u32[]{:S(2)}) copy-start(f32[24576]{0:T(1024)} %param.14) | copy-start | bytes 294916
  1.3 15.3 %copy-start.8 = (s32[24576]{0:T(1024)S(1)}, s32[24576]{0:T(1024)}, u32[]{:S(2)}) copy-start(s32[24576]{0:T(1024)} %param.15) | copy-start | bytes 294916
  1.3 15.3 %copy-start.9 = (s32[24576]{0:T(1024)S(1)}, s32[24576]{0:T(1024)}, u32[]{:S(2)}) copy-start(s32[24576]{0:T(1024)} %param.16) | copy-start | bytes 294916
  10.1 15.0 %collective-permute-start = (f32[21,16,128]{2,1,0:T(8,128)}, f32[21,16,128]{2,1,0:T(8,128)S(1)}, u32[]{:S(2)}, u32[]{:S(2)}) collective-permute-start(f32[21,16,128]{2,1,0:T(8,128)} %get-tuple-element.17), channel_id=1, source_target_pairs={{0,8},{8,16},{16,24},{1,9},{9,17},{17,25},{2,10},{10,18},{18,26},{... | collective-permute-start | bytes 516104 | tf_op jit(solution)/shard_map/ppermute | solution.py:733
  15.1 9.8 %copy-start = (f32[16,8,128]{2,1,0:T(8,128)S(1)}, f32[16,8,128]{2,1,0:T(8,128)}, u32[]{:S(2)}) copy-start(f32[16,8,128]{2,1,0:T(8,128)} %param.18) | copy-start | bytes 196612
  15.1 9.8 %copy-start.1 = (f32[16,8,128]{2,1,0:T(8,128)S(1)}, f32[16,8,128]{2,1,0:T(8,128)}, u32[]{:S(2)}) copy-start(f32[16,8,128]{2,1,0:T(8,128)} %param.19) | copy-start | bytes 196612
  15.1 9.8 %copy-start.2 = (f32[256,256]{1,0:T(8,128)S(1)}, f32[256,256]{1,0:T(8,128)}, u32[]{:S(2)}) copy-start(f32[256,256]{1,0:T(8,128)} %get-tuple-element.15.near) | copy-start | bytes 786436
  15.1 10.1 %collective-permute-start.1 = (f32[21,16,128]{2,1,0:T(8,128)}, f32[21,16,128]{2,1,0:T(8,128)S(1)}, u32[]{:S(2)}, u32[]{:S(2)}) collective-permute-start(f32[21,16,128]{2,1,0:T(8,128)} %get-tuple-element.18), channel_id=1, source_target_pairs={{8,0},{16,8},{24,16},{9,1},{17,9},{25,17},{10,2},{18,10},{26,18},{... | collective-permute-start | bytes 516104 | tf_op jit(solution)/shard_map/ppermute | solution.py:738
  25.3 4.3 %collective-permute-start.2 = (f32[128,128]{1,0:T(8,128)S(1)}, f32[128,128]{1,0:T(8,128)S(1)}, u32[]{:S(2)}, u32[]{:S(2)}) collective-permute-start(f32[128,128]{1,0:T(8,128)S(1)} %maximum_add_fusion), channel_id=1, source_target_pairs={{0,4},{4,0},{1,5},{5,1},{2,6},{6,2},{3,7},{7,3},{8,12},{12,8},{9,1... | collective-permute-start | bytes 196616 | tf_op jit(solution)/shard_map/ppermute | solution.py:744
